TPU v7x, 256 devices: a whole 4x4x8 slice. The times are simulated.
256 devices in a mesh: ctx: 32 (over z, x_lo, core), head: 8 (over y, x_hi).
Axes of the slice: x: 4 (x_hi: 2, x_lo: 2; x = x_hi * 2 + x_lo), y: 4, z: 8, core: 2. Of those that a mesh axis runs over, the one named last changes fastest.
Arguments:
- queries: bfloat16 [3, 64, 128, 192], P(None, 'ctx', 'head'), may hold values from -50 to 50, as said below
- cache: bfloat16 [32768, 576], P('ctx'), may hold values from -6 to 6
- w_uk: bfloat16 [128, 128, 512], P('head', 'ctx'), may hold values from -0.5 to 0.5
- w_uv: bfloat16 [128, 512, 128], P('head', 'ctx'), may hold values from -1 to 1
- selected: int32 [3, 64, 16], replicated, may hold values from 0 to 255, as said below
- lengths: int32 [64], replicated, may hold values from 2048 to 32766, as said below
Outputs:
- attended: bfloat16 [3, 64, 128, 128], P(None, 'ctx', 'head')
Inputs may be any that keep to these rules, and one draw needn't show every extreme that they name: `queries`: in the shown draw of normal law; in the hidden draw some rows' rotary entries are large. `selected`: for each step and row, 16 distinct block numbers, block 0 among them, and each block b starts before the row's length (b * 128 < lengths[r]). `lengths`: both ends of the range are taken by some row in every draw.
All inputs are finite; a program needn't handle non-finite values.
Results may differ from a plain program's by a relative error of at most 0.0064.
Values may be sent and summed in bfloat16 or wider, within the bound.
No kernel may reach another device: no remote copies, remote signals or barrier semaphores. Data moves between devices by JAX's collectives and lax.ppermute only.
A program may use at most 64 MiB of HBM per device.

v0:
```python
import jax
import jax.numpy as jnp
from jax import lax
from jax.sharding import PartitionSpec as P

DN = 128
R = 64
C = 512
BLK = 128
STEPS = 3


NEG_FILL = -1e30


def shard_terms(query_rows, cache, chosen_rows, length_rows, first_pos, step_index):
    scale_factor = (DN + R) ** (-0.5)
    shard_len = cache.shape[0]
    scores = (
        jnp.einsum("bhe,se->bhs", query_rows, cache, preferred_element_type=jnp.float32)
        * scale_factor
    )
    positions = first_pos + jnp.arange(shard_len, dtype=jnp.int32)
    local_blocks = first_pos // BLK + jnp.arange(shard_len // BLK, dtype=jnp.int32)
    chosen_block = jnp.any(chosen_rows[:, :, None] == local_blocks[None, None, :], axis=1)
    chosen_token = jnp.broadcast_to(chosen_block[:, :, None], chosen_block.shape + (BLK,)).reshape(
        chosen_block.shape[0], shard_len
    )
    visible = (chosen_token & (positions[None, :] < length_rows[:, None] + step_index))[:, None, :]
    shard_max = jnp.max(jnp.where(visible, scores, NEG_FILL), axis=-1)
    weights = jnp.where(visible, jnp.exp(scores - shard_max[..., None]), 0.0).astype(jnp.bfloat16)
    shard_total = jnp.sum(weights, axis=-1, dtype=jnp.float32)
    shard_latent = jnp.einsum(
        "bhs,sc->bhc", weights, cache[:, :C], preferred_element_type=jnp.float32
    )
    return (shard_max, shard_total, shard_latent)


def collect_terms(query_block, cache, chosen_step, lengths, first_pos, step_index):
    gathered = lax.all_gather(query_block, "ctx", axis=0, tiled=True)
    all_rows = gathered.shape[0]
    head_count = gathered.shape[1]
    block_rows = 32

    def block_terms(block_index):
        row_start = block_index * block_rows
        rows_here = lax.dynamic_slice_in_dim(gathered, row_start, block_rows, 0)
        chosen_here = lax.dynamic_slice_in_dim(chosen_step, row_start, block_rows, 0)
        length_here = lax.dynamic_slice_in_dim(lengths, row_start, block_rows, 0)
        return shard_terms(rows_here, cache, chosen_here, length_here, first_pos, step_index)

    shard_max, shard_total, shard_latent = lax.map(
        block_terms, jnp.arange(all_rows // block_rows, dtype=jnp.int32)
    )
    shard_max = shard_max.reshape(all_rows, head_count)
    shard_total = shard_total.reshape(all_rows, head_count)
    shard_latent = shard_latent.reshape(all_rows, head_count, shard_latent.shape[-1])
    global_max = lax.pmax(shard_max, "ctx")
    factor = jnp.exp(shard_max - global_max)
    return (shard_latent * factor[..., None], shard_total * factor)


def body(queries, cache, w_uk, w_uv, selected, lengths):
    position = lax.axis_index("ctx")
    first_pos = position * cache.shape[0]
    up_keys, up_values = (
        lax.all_gather(w_uk, "ctx", axis=1, tiled=True),
        lax.all_gather(w_uv, "ctx", axis=1, tiled=True),
    )
    absorbed = jnp.einsum(
        "tbhd,hdc->tbhc", queries[..., :DN], up_keys, preferred_element_type=jnp.float32
    ).astype(jnp.bfloat16)
    query_full = jnp.concatenate([absorbed, queries[..., DN:]], axis=-1)
    results = []
    for step_index in range(STEPS):
        chosen_step = selected[step_index]
        scaled_latent, scaled_total = collect_terms(
            query_full[step_index], cache, chosen_step, lengths, first_pos, step_index
        )
        summed, norm_sum = (
            lax.psum_scatter(scaled_latent, "ctx", scatter_dimension=0, tiled=True),
            lax.psum_scatter(scaled_total, "ctx", scatter_dimension=0, tiled=True),
        )
        output = jnp.einsum(
            "bhc,hcv->bhv",
            summed / norm_sum[..., None],
            up_values.astype(jnp.float32),
            precision=lax.Precision.HIGHEST,
        )
        results.append(output.astype(jnp.bfloat16))
    return jnp.stack(results, 0)


def solution(mesh):
    in_specs = (
        P(None, "ctx", "head", None),
        P("ctx", None),
        P("head", "ctx", None),
        P("head", "ctx", None),
        P(),
        P(),
    )
    out_specs = P(None, "ctx", "head", None)
    return jax.shard_map(body, mesh=mesh, in_specs=in_specs, out_specs=out_specs, check_vma=False)
```

profile of v0, /device:TPU:1, one launch (start us, length us, event | category | flops | bytes accessed | tf_op | source)
XLA Modules:
  0.0 835.3 jit_solution(14364733300675791382)
XLA Ops:
  6.5 1.6 copy.99
  9.7 68.4 %all-gather.9.cloned.1.call-done = bf16[16,128,512]{2,0,1:T(8,128)(2,1)} async-done(((bf16[16,4,512]{2,0,1:T(8,128)(2,1)}), bf16[16,128,512]{2,0,1:T(8,128)(2,1)}) %all-gather.9.cloned.1.call-update) | async-done | bytes 2097168 | tf_op jit(solution)/shard_map/all_gather | solution.py:67
  78.1 3.9 fusion.32
  82.0 0.9 fusion.39
  84.7 63.1 %all-gather.13.cloned.1.call-done = bf16[1,64,16,576]{3,0,1,2:T(2,128)(2,1)} async-done(((bf16[1,2,16,576]{3,0,1,2:T(2,128)(2,1)}), bf16[1,64,16,576]{3,0,1,2:T(2,128)(2,1)}) %all-gather.13.cloned.1.call-update) | async-done | bytes 1179664 | tf_op jit(solution)/shard_map/all_gather | solution.py:40
  147.7 4.3 copy.173
  152.3 11.4 %while.51 = (s32[]{:T(128)}, f32[2,32,16]{2,1,0:T(8,128)S(1)}, f32[2,32,16]{2,1,0:T(8,128)S(1)}, f32[2,32,16,512]{3,2,1,0:T(8,128)S(1)}, s32[2]{0:T(128)S(1)}, /...) while((s32[]{:T(128)}, f32[2,32,16]{2,1,0:T(8,128)S(1)}, ...), condition=%wide.region_4.5_spmd, body=%wide.region_0.4_spmd.sunk | while | flops 1147739904 | bytes 10524323 | solution.py:52
  154.3 2.3 select_reduce_fusion.6
  159.9 2.3 select_reduce_fusion.6
  164.5 49.8 %all-gather.15.cloned.1.call-done = bf16[1,64,16,576]{3,0,1,2:T(2,128)(2,1)} async-done(((bf16[1,2,16,576]{3,0,1,2:T(2,128)(2,1)}), bf16[1,64,16,576]{3,0,1,2:T(2,128)(2,1)}) %all-gather.15.cloned.1.call-update) | async-done | bytes 1179664 | tf_op jit(solution)/shard_map/all_gather | solution.py:40
  214.3 4.2 copy.172
  218.5 1.6 broadcast.162.clone.1
  220.2 13.0 %while.52 = (s32[]{:T(128)}, f32[2,32,16]{2,1,0:T(8,128)S(1)}, f32[2,32,16]{2,1,0:T(8,128)S(1)}, f32[2,32,16,512]{3,2,1,0:T(8,128)}, s32[2]{0:T(128)S(1)}, /*ind...) while((s32[]{:T(128)}, f32[2,32,16]{2,1,0:T(8,128)S(1)}, ...), condition=%wide.region_12.13_spmd, body=%wide.region_8.12_spmd.sunk | while | flops 1147739904 | bytes 27301596 | solution.py:52
  222.1 2.4 select_reduce_fusion.7
  228.6 2.4 select_reduce_fusion.7
  233.9 46.9 %all-gather.17.cloned.1.call-done = bf16[1,64,16,576]{3,0,1,2:T(2,128)(2,1)} async-done(((bf16[1,2,16,576]{3,0,1,2:T(2,128)(2,1)}), bf16[1,64,16,576]{3,0,1,2:T(2,128)(2,1)}) %all-gather.17.cloned.1.call-update) | async-done | bytes 1179664 | tf_op jit(solution)/shard_map/all_gather | solution.py:40
  280.7 4.2 copy.171
  285.3 12.2 %while.53 = (s32[]{:T(128)}, f32[2,32,16]{2,1,0:T(8,128)S(1)}, f32[2,32,16]{2,1,0:T(8,128)S(1)}, f32[2,32,16,512]{3,2,1,0:T(8,128)S(1)}, s32[2]{0:T(128)S(1)}, /...) while((s32[]{:T(128)}, f32[2,32,16]{2,1,0:T(8,128)S(1)}, ...), condition=%wide.region_20.21_spmd, body=%wide.region_16.20_spmd.sunk | while | flops 1147739904 | bytes 10524443 | solution.py:52
  287.6 2.3 select_reduce_fusion.8
  293.8 2.3 select_reduce_fusion.8
  297.7 101.9 %all-reduce.4 = (f32[64,16]{0,1:T(8,128)S(1)}, f32[64,16]{0,1:T(8,128)S(1)}, f32[64,16]{0,1:T(8,128)S(1)}) all-reduce(f32[64,16]{0,1:T(8,128)S(1)} %copy.138, f32[64,16]{0,1:T(8,128)} %copy.136, f32[64,16]{0,1:T(8,128)} %copy.134), channel_id=1, replica_groups=mesh['ctx'=32,'head'=8] {'ctx'}, use_global_device_ids=true, to_apply=%region_21.22 | all-reduce | flops 3072 | bytes 24576 | tf_op jit(solution)/shard_map/pmax | solution.py:58
  400.4 3.1 bitcast_multiply_fusion.2
  404.5 3.2 bitcast_multiply_fusion.1
  407.9 1.5 bitcast_multiply_fusion
  411.3 104.7 %all-reduce.3 = (f32[64,16]{0,1:T(8,128)S(1)}, f32[64,16]{0,1:T(8,128)S(1)}, f32[64,16]{0,1:T(8,128)S(1)}) all-reduce(f32[64,16]{0,1:T(8,128)S(1)} %get-tuple-element.828, f32[64,16]{0,1:T(8,128)S(1)} %get-tuple-element.848, f32[64,16]{0,1:T(8,128)S(1)} %get-tuple-element.824), channel_id=10, replica_groups=mesh['ctx'=32,'head'=8] {'ctx'}, use_global_device_ids=true, to_apply=%region_23.24.clone | all-reduce | flops 3072 | bytes 24576
  516.5 5.1 reduce-scatter.7.cloned.1.call-done
  522.5 69.1 %all-gather.11.cloned.1.call-done = bf16[16,512,128]{2,1,0:T(8,128)(2,1)} async-done(((bf16[16,16,128]{2,1,0:T(8,128)(2,1)}), bf16[16,512,128]{2,1,0:T(8,128)(2,1)}) %all-gather.11.cloned.1.call-update) | async-done | bytes 2097168 | tf_op jit(solution)/shard_map/all_gather | solution.py:68
  591.7 2.7 fusion.35
  594.3 112.4 %reduce-scatter.9.cloned.1.call-done = f32[2,16,512]{2,1,0:T(8,128)} async-done(((f32[64,16,512]{2,1,0:T(8,128)}), f32[2,16,512]{2,1,0:T(8,128)}) %reduce-scatter.9.cloned.1.call-update) | async-done | bytes 65552 | tf_op jit(solution)/shard_map/reduce_scatter | solution.py:81
  707.6 0.9 fusion.36
  708.6 117.4 %reduce-scatter.11.cloned.1.call-done = f32[2,16,512]{2,1,0:T(8,128)} async-done(((f32[64,16,512]{2,1,0:T(8,128)}), f32[2,16,512]{2,1,0:T(8,128)}) %reduce-scatter.11.cloned.1.call-update) | async-done | bytes 65552 | tf_op jit(solution)/shard_map/reduce_scatter | solution.py:81
  826.9 0.9 fusion.37
  (157 shorter events, 30.8 us)
Async XLA Ops:
  6.5 77.3 %copy-start.4 = (bf16[1024,576]{0,1:T(8,128)(2,1)S(1)}, bf16[1024,576]{0,1:T(8,128)(2,1)}, u32[]{:S(2)}) copy-start(bf16[1024,576]{0,1:T(8,128)(2,1)} %param.13) | copy-start | bytes 3538948
  6.5 71.6 %all-gather.9.cloned.1.call-start = ((), (), s32[]{:S(2)}) async-start(), calls=%async_computation.3 | async-start | bytes 2162688 | tf_op jit(solution)/shard_map/all_gather | solution.py:67
  8.1 139.6 %all-gather.13.cloned.1.call-start = ((), (), s32[]{:S(2)}) async-start(), calls=%async_computation.8 | async-start | bytes 2703360 | tf_op jit(solution)/shard_map/all_gather | solution.py:40
  82.0 2.5 copy-start.5
  83.0 131.3 %all-gather.15.cloned.1.call-start = ((), (), s32[]{:S(2)}) async-start(), calls=%async_computation.9 | async-start | bytes 2703360 | tf_op jit(solution)/shard_map/all_gather | solution.py:40
  83.7 197.0 %all-gather.17.cloned.1.call-start = ((), (), s32[]{:S(2)}) async-start(), calls=%async_computation.10 | async-start | bytes 2703360 | tf_op jit(solution)/shard_map/all_gather | solution.py:40
  84.6 67.7 %copy-start.6 = (s32[64]{0:T(128)S(1)}, s32[64]{0:T(128)}, u32[]{:S(2)}) copy-start(s32[64]{0:T(128)} %param.17) | copy-start | bytes 772
  84.6 437.0 %reduce-scatter.7.cloned.1.call-start = ((), (), s32[]{:S(2)}) async-start(), calls=%async_computation.4 | async-start | bytes 2162688 | tf_op jit(solution)/shard_map/reduce_scatter | solution.py:81
  163.7 56.5 %copy-start.1 = (f32[2,32,16,512]{3,2,1,0:T(8,128)}, f32[2,32,16,512]{3,2,1,0:T(8,128)S(1)}, u32[]{:S(2)}) copy-start(f32[2,32,16,512]{3,2,1,0:T(8,128)S(1)} %get-tuple-element.611) | copy-start | bytes 6291460
  222.1 2.4 copy-start.2
  225.3 1.4 copy-start.3
  228.6 2.4 copy-start.2
  231.8 1.4 copy-start.3
  233.2 52.1 %copy-start.7 = (s32[64]{0:T(128)}, s32[64]{0:T(128)S(1)}, u32[]{:S(2)}) copy-start(s32[64]{0:T(128)S(1)} %get-tuple-element.1245) | copy-start | bytes 772
  285.3 1.2 copy-start.9
  290.7 0.7 copy-start.10
  291.4 1.2 copy-start.9
  296.8 0.7 copy-start.10
  403.6 188.1 %all-gather.11.cloned.1.call-start = ((), (), s32[]{:S(2)}) async-start(), calls=%async_computation.5 | async-start | bytes 2162688 | tf_op jit(solution)/shard_map/all_gather | solution.py:68
  404.1 302.6 %reduce-scatter.9.cloned.1.call-start = ((), (), s32[]{:S(2)}) async-start(), calls=%async_computation.6 | async-start | bytes 2162688 | tf_op jit(solution)/shard_map/reduce_scatter | solution.py:81
  407.7 418.3 %reduce-scatter.11.cloned.1.call-start = ((), (), s32[]{:S(2)}) async-start(), calls=%async_computation.7 | async-start | bytes 2162688 | tf_op jit(solution)/shard_map/reduce_scatter | solution.py:81
  409.4 0.7 copy-start.8
  591.7 116.0 %copy-start = (bf16[16,512,128]{2,1,0:T(8,128)(2,1)S(1)}, bf16[16,512,128]{2,1,0:T(8,128)(2,1)}, u32[]{:S(2)}) copy-start(bf16[16,512,128]{2,1,0:T(8,128)(2,1)} %all-gather.11.cloned.1.call-done) | copy-start | bytes 6291460
Sparse Core Ops, SparseCore 0:
  9.2 68.8 all-gather.8
  83.1 64.5 all-gather.12
  149.6 64.6 all-gather.14
  216.0 64.7 all-gather.16
  403.7 117.8 reduce-scatter.6
  523.4 68.2 all-gather.10
  594.3 112.3 reduce-scatter.8
  709.2 116.6 reduce-scatter.10
where the time goes:
time: 839 us; the launch traced here: 835 us
  waiting for transfers between devices  533 us (64%)
  blocking collectives  207 us (25%)
  local copies, waits for them, and re-layouts  29.9 us (4%)
  matrix products  27.1 us (3%)
  other arithmetic  19 us (2%)
  between operations  14.4 us (2%)
    reduce_scatter x3, waiting for transfers between devices, body(): lax.psum_scatter(scaled_latent, 'ctx', scatter_dimension=0, tiled=True)  235 us
    all_gather x3, waiting for transfers between devices, collect_terms(): gathered = lax.all_gather(query_block, 'ctx', axis=0, tiled=True)  160 us
    unnamed x1, blocking collectives  105 us
    pmax x1, blocking collectives, collect_terms(): global_max = lax.pmax(shard_max, 'ctx')  102 us
    all_gather x1, waiting for transfers between devices, body(): lax.all_gather(w_uv, 'ctx', axis=1, tiled=True)  69.1 us
    all_gather x1, waiting for transfers between devices, body(): lax.all_gather(w_uk, 'ctx', axis=1, tiled=True)  68.4 us
  transfers between devices with their start and end apart: 8, of which 8 were waited for; matrix products, arithmetic and copies ran while one was open for 5% of the time, Pallas kernels for 0%

commit v1 on v0

v1 whole, which is shorter than its diff:
```python
import functools

import jax
import jax.numpy as jnp
from jax import lax
from jax.experimental import pallas as pl
from jax.experimental.pallas import tpu as pltpu
from jax.sharding import Mesh
from jax.sharding import PartitionSpec as P

DN = 128
R = 64
C = 512
DV = 128
BLK = 128
STEPS = 3

NZ = 8
NQ = 4
HG = 4
BZ = 8
RZ = STEPS * BZ
RT = NZ * RZ
S_DEV = 1024
NBLK = S_DEV // BLK

QN0, QR0, UK0, UV0, PIECE = 0, 96, 144, 400, 656
HALF = 320
OUT_ROWS = 112

NEG = -1e30
SCALE = (DN + R) ** (-0.5)
LOG2E = 1.4426950408889634
LN2 = 0.6931471805599453

VMEM = pl.BlockSpec(memory_space=pltpu.VMEM)
SMEM = pl.BlockSpec(memory_space=pltpu.SMEM)
ANY = pl.BlockSpec(memory_space=pl.ANY)


def dot(a, b, dims):
    return lax.dot_general(a, b, (dims, ((), ())), preferred_element_type=jnp.float32)


def attention_kernel(
    zsrc, *refs
):
    pieces = refs[:9]
    lim = refs[9]
    caches = refs[10:16]
    out = refs[16]
    cache, qn, qr, wuk, wuv, probe, scores, top, total, latent, sems = refs[17:]

    copies = []
    for i, (part, first, count) in enumerate(
        ((0, 0, 1024), (1, 0, 1024), (2, 0, 512), (2, 512, 512), (3, 0, 512), (3, 512, 512))
    ):
        copy = pltpu.make_async_copy(
            caches[i], cache.at[part, pl.ds(first, count), :], sems.at[i]
        )
        copy.start()
        copies.append(copy)

    for p in range(NZ):
        z = zsrc[p]

        def rows(first, count, p=p):
            if p < NZ - 1:
                return pieces[p][first : first + count, :]
            if first + count <= HALF:
                return pieces[p][first : first + count, :]
            return pieces[p + 1][first - HALF : first - HALF + count, :]

        here = pl.ds(pl.multiple_of(z * RZ, RZ), RZ)
        block = rows(QN0, 96).astype(jnp.float32)
        for h in range(HG):
            qn[h, here, :] = block[h * RZ : (h + 1) * RZ]
        block = rows(QR0, 48).astype(jnp.float32)
        for j in range(HG // 2):
            qr[j, here, :] = block[j * RZ : (j + 1) * RZ]
        here = pl.ds(pl.multiple_of(z * 16, 16), 16)
        for h in range(HG):
            for cc in range(4):
                wuk[h, here, cc * 128 : (cc + 1) * 128] = rows(UK0 + (h * 4 + cc) * 16, 16)
        for h in range(HG):
            here = pl.ds(pl.multiple_of(z * 64, 64), 64)
            wuv[h, here, :] = rows(UV0 + h * 64, 64)

    for h in range(HG):
        mine = slice(h * RT, (h + 1) * RT)
        absorbed = dot(qn[h].astype(jnp.bfloat16), wuk[h], ((1,), (0,)))
        probe[mine, 0:C] = absorbed.astype(jnp.bfloat16)
        rope = qr[h // 2][:, (h % 2) * R : (h % 2 + 1) * R]
        probe[mine, C : C + R] = rope.astype(jnp.bfloat16)
    top[...] = jnp.full(top.shape, NEG, jnp.float32)
    total[...] = jnp.zeros(total.shape, jnp.float32)
    latent[...] = jnp.zeros(latent.shape, jnp.float32)
    lane = lax.broadcasted_iota(jnp.int32, (RT, BLK), 1)

    for copy in copies:
        copy.wait()

    def score(i, carry):
        for h in range(HG):
            mine = pl.ds(h * RT, RT)
            part = dot(probe[mine, :], cache[i], ((1,), (1,)))
            best = top[mine, :]
            for j in range(NBLK):
                seen = lane < lim[i, :, j : j + 1]
                block = jnp.where(seen, part[:, j * BLK : (j + 1) * BLK], NEG)
                scores[i, mine, j * BLK : (j + 1) * BLK] = block
                best = jnp.maximum(best, block)
            top[mine, :] = best
        return carry

    lax.fori_loop(0, NQ, score, 0)

    best = jnp.max(top[...], axis=1, keepdims=True)
    top[...] = jnp.broadcast_to(best, top.shape)

    def weigh(i, carry):
        for h in range(HG):
            mine = pl.ds(h * RT, RT)
            best = jnp.maximum(top[mine, :], 0.1 * NEG)
            summed = total[mine, :]
            blocks = []
            for j in range(NBLK):
                block = scores[i, mine, j * BLK : (j + 1) * BLK]
                weight = jnp.exp2((block - best) * (SCALE * LOG2E))
                summed = summed + weight
                blocks.append(weight.astype(jnp.bfloat16))
            total[mine, :] = summed
            weights = jnp.concatenate(blocks, axis=1)
            latent[mine, :] += dot(weights, cache[i, :, 0:C], ((1,), (0,)))
        return carry

    lax.fori_loop(0, NQ, weigh, 0)

    parts, logs = [], []
    for h in range(HG):
        mine = slice(h * RT, (h + 1) * RT)
        norm = jnp.sum(total[mine, :], axis=1, keepdims=True)
        some = norm > 0.0
        norm = jnp.where(some, norm, 1.0)
        mean = (latent[mine, :] / norm).astype(jnp.bfloat16)
        parts.append(dot(mean, wuv[h], ((1,), (0,))))
        logs.append(jnp.where(some, top[mine, 0:1] * SCALE + jnp.log(norm), NEG))
    diagonal = lax.broadcasted_iota(jnp.int32, (96, 128), 0) == lax.broadcasted_iota(
        jnp.int32, (96, 128), 1
    )
    for z in range(NZ):
        rows = slice(z * RZ, (z + 1) * RZ)
        block = jnp.concatenate([part[rows] for part in parts], axis=0)
        out[z, 0:96, :] = block.astype(jnp.bfloat16)
        column = jnp.concatenate([log[rows] for log in logs], axis=0)
        row = jnp.sum(jnp.where(diagonal, column, 0.0), axis=0, keepdims=True)
        high = row.astype(jnp.bfloat16).astype(jnp.float32)
        middle = (row - high).astype(jnp.bfloat16).astype(jnp.float32)
        low = row - high - middle
        which = lax.broadcasted_iota(jnp.int32, (16, 128), 0)
        packed = jnp.where(
            which == 0, high, jnp.where(which == 1, middle, jnp.where(which == 2, low, 0.0))
        )
        out[z, 96:112, :] = packed.astype(jnp.bfloat16)


def attention(zsrc, pieces, lim, caches):
    return pl.pallas_call(
        attention_kernel,
        out_shape=jax.ShapeDtypeStruct((NZ, OUT_ROWS, 128), jnp.bfloat16),
        in_specs=[SMEM] + [VMEM] * 10 + [ANY] * 6,
        out_specs=VMEM,
        scratch_shapes=[
            pltpu.VMEM((NQ, S_DEV, C + R), jnp.bfloat16),
            pltpu.VMEM((HG, RT, DN), jnp.float32),
            pltpu.VMEM((HG // 2, RT, 2 * R), jnp.float32),
            pltpu.VMEM((HG, DN, C), jnp.bfloat16),
            pltpu.VMEM((HG, C, DV), jnp.bfloat16),
            pltpu.VMEM((HG * RT, C + R), jnp.bfloat16),
            pltpu.VMEM((NQ, HG * RT, S_DEV), jnp.float32),
            pltpu.VMEM((HG * RT, 128), jnp.float32),
            pltpu.VMEM((HG * RT, 128), jnp.float32),
            pltpu.VMEM((HG * RT, C), jnp.float32),
            pltpu.SemaphoreType.DMA((6,)),
        ],
        compiler_params=pltpu.CompilerParams(vmem_limit_bytes=48 * 1024 * 1024),
        cost_estimate=pl.CostEstimate(
            flops=2 * HG * RT * NQ * S_DEV * (2 * C + R),
            bytes_accessed=8 * 1024 * 1024,
            transcendentals=HG * RT * NQ * S_DEV,
        ),
        name="attention",
    )(zsrc, *pieces, lim, *caches)


def combine_kernel(parts, out):
    logs = []
    for z in range(NZ):
        packed = parts[z, 96:112, :].astype(jnp.float32)
        logs.append(packed[0:1] + packed[1:2] + packed[2:3])
    best = functools.reduce(jnp.maximum, logs)
    shares = [jnp.exp(log - best) for log in logs]
    norm = functools.reduce(jnp.add, shares)
    diagonal = lax.broadcasted_iota(jnp.int32, (96, 128), 0) == lax.broadcasted_iota(
        jnp.int32, (96, 128), 1
    )
    summed = jnp.zeros((96, 128), jnp.float32)
    for z in range(NZ):
        share = jnp.where(diagonal, shares[z] / norm, 0.0)
        column = jnp.sum(share, axis=1, keepdims=True)
        summed += column * parts[z, 0:96, :].astype(jnp.float32)
    out[...] = summed.astype(jnp.bfloat16)


def combine(parts):
    return pl.pallas_call(
        combine_kernel,
        out_shape=jax.ShapeDtypeStruct((96, 128), jnp.bfloat16),
        in_specs=[VMEM],
        out_specs=VMEM,
        name="combine",
    )(parts)


def quad_swap(x, k):
    return lax.ppermute(x, ("x", "core"), [(i, i ^ k) for i in range(NQ)])


def z_shift(x, k):
    return lax.ppermute(x, "z", [(i, (i + k) % NZ) for i in range(NZ)])


def quad_exchange(parts, quad):
    got = [lax.dynamic_index_in_dim(parts, quad, 0, keepdims=False)]
    for k in range(1, NQ):
        got.append(quad_swap(lax.dynamic_index_in_dim(parts, quad ^ k, 0, keepdims=False), k))
    odd = quad % 2 == 1
    a, b, c, d = got
    a, b, c, d = (
        jnp.where(odd, b, a),
        jnp.where(odd, a, b),
        jnp.where(odd, d, c),
        jnp.where(odd, c, d),
    )
    upper = quad >= 2
    return jnp.stack(
        [jnp.where(upper, c, a), jnp.where(upper, d, b), jnp.where(upper, a, c), jnp.where(upper, b, d)]
    )


def visible_limits(selected, lengths, z, quad):
    chosen = selected.reshape(STEPS, NZ, NQ, 2, -1).transpose(1, 2, 0, 3, 4).reshape(RT, -1)
    ends = lengths.reshape(NZ, NQ, 1, 2) + jnp.arange(STEPS, dtype=jnp.int32)[:, None]
    ends = ends.reshape(RT)
    first = (z * NQ + (quad ^ jnp.arange(NQ, dtype=jnp.int32))) * NBLK
    blocks = first[:, None] + jnp.arange(NBLK, dtype=jnp.int32)
    hit = jnp.any(chosen[None, :, None, :] == blocks[:, None, :, None], axis=-1)
    count = jnp.clip(ends[None, :, None] - blocks[:, None, :] * BLK, 0, BLK)
    return jnp.where(hit, count, 0)


def body(queries, cache, w_uk, w_uv, selected, lengths):
    z = lax.axis_index("z")
    quad = lax.axis_index("x") * 2 + lax.axis_index("core")

    q = queries.reshape(STEPS, 2, NQ, HG, DN + R)
    qn = q[..., :DN].transpose(2, 3, 0, 1, 4).reshape(NQ, 24, 128)
    qr = q[..., DN:].reshape(STEPS, 2, NQ, 2, 2, R).transpose(2, 3, 0, 1, 4, 5).reshape(NQ, 12, 128)
    uk = w_uk.reshape(NQ, HG, 4, 4, 128).transpose(0, 1, 3, 2, 4).reshape(NQ, 64, 128)
    uv = w_uv.reshape(NQ, 64, 128)
    got = quad_exchange(jnp.concatenate([qn, qr, uk, uv], axis=1), quad)
    piece = jnp.concatenate(
        [
            got[:, 0:24].reshape(NQ, HG, 6, 128).transpose(1, 0, 2, 3).reshape(96, 128),
            got[:, 24:36].reshape(NQ, 2, 6, 128).transpose(1, 0, 2, 3).reshape(48, 128),
            got[:, 36:100].reshape(NQ, 16, 4, 128).transpose(1, 0, 2, 3).reshape(256, 128),
            got[:, 100:164].reshape(NQ, HG, 16, 128).transpose(1, 0, 2, 3).reshape(256, 128),
        ],
        axis=0,
    )

    mate = quad_swap(cache, 1)
    low, high = quad_swap(cache[:512], 2), quad_swap(cache[512:], 2)
    caches = [cache, mate, low, high, quad_swap(low, 1), quad_swap(high, 1)]
    lim = visible_limits(selected, lengths, z, quad)

    up = down = piece
    pieces, offsets = [piece], [0]
    for step in range(1, 4):
        up, down = z_shift(up, 1), z_shift(down, -1)
        pieces += [up, down]
        offsets += [-step, step]
    pieces += [z_shift(up[:HALF], 1), z_shift(down[HALF:], -1)]
    offsets.append(4)
    zsrc = (z + jnp.array(offsets, jnp.int32)) % NZ

    parts = attention(zsrc, pieces, lim, caches)
    parts = lax.all_to_all(parts, "z", 0, 0, tiled=True)
    mine = combine(parts)
    mine = mine.reshape(HG, NQ, 6, 128).transpose(1, 0, 2, 3).reshape(NQ, 24, 128)
    final = quad_exchange(mine, quad)
    final = final.reshape(NQ, HG, STEPS, 2, DV).transpose(2, 3, 0, 1, 4)
    return final.reshape(STEPS, 2, NQ * HG, DV)


def solution(mesh):
    fine = Mesh(mesh.devices.reshape(NZ, 2, 2, -1), ("z", "x", "core", "head"))
    ctx = ("z", "x", "core")
    in_specs = (
        P(None, ctx, "head", None),
        P(ctx, None),
        P("head", ctx, None),
        P("head", ctx, None),
        P(),
        P(),
    )
    out_specs = P(None, ctx, "head", None)
    return jax.shard_map(body, mesh=fine, in_specs=in_specs, out_specs=out_specs, check_vma=False)
```

time: 839 us -> 108 us (0.13)
  waiting for transfers between devices: 533 us -> 20.7 us
  blocking collectives: 207 us -> 12.7 us
  starting transfers between devices: 0.51 us -> 29.6 us
  matrix products: 27.1 us -> 0 us
  Pallas kernels: 0 us -> 17.6 us
  other arithmetic: 19 us -> 2.29 us
  between operations: 14.4 us -> 0.48 us
    all_gather x5 -> x0, waiting for transfers between devices: 297 us -> none  [the longest x3 160 us: collect_terms(): gathered = lax.all_gather(query_block, 'ctx', axis=0, tiled=True)]
    reduce_scatter x3 -> x0, waiting for transfers between devices: 235 us -> none  [body(): lax.psum_scatter(scaled_latent, 'ctx', scatter_dimension=0, tiled=True)]
    unnamed x1 -> x0, blocking collectives: 105 us -> none
    pmax x1 -> x0, blocking collectives: 102 us -> none  [collect_terms(): global_max = lax.pmax(shard_max, 'ctx')]
    ppermute x0 -> x19, starting transfers between devices: none -> 29.6 us  [the longest x11 14.9 us: quad_swap(): return lax.ppermute(x, ('x', 'core'), [(i, i ^ k) for i in range(NQ)])]
    dot_general x16 -> x0, matrix products: 27.1 us -> none  [the longest x6 13.9 us: shard_terms(): jnp.einsum('bhe,se->bhs', query_rows, cache, preferred_element_type=jnp.f...]
    ppermute x0 -> x19, waiting for transfers between devices: none -> 20.7 us  [the longest x11 15.3 us: quad_swap(): return lax.ppermute(x, ('x', 'core'), [(i, i ^ k) for i in range(NQ)])]
    pallas_call x0 -> x2, Pallas kernels: none -> 17.6 us  [the longest x1 15.8 us: attention(): pl.pallas_call(attention_kernel, out_shape=jax.ShapeDtypeStruct((NZ, OUT_...]
  transfers between devices with their start and end apart: 8 -> 19, of which waited for: 8 -> 6; matrix products, arithmetic and copies ran while one was open for 5% -> 13% of each run, Pallas kernels for 0% -> 0%
where the time goes in v1:
time: 108 us
  starting transfers between devices  29.6 us (27%)
  local copies, waits for them, and re-layouts  24.2 us (22%)
  waiting for transfers between devices  20.7 us (19%)
  Pallas kernels  17.6 us (16%)
  blocking collectives  12.7 us (12%)
  other arithmetic  2.29 us (2%)
    pallas_call x1, Pallas kernels, attention(): pl.pallas_call(attention_kernel, out_shape=jax.ShapeDtypeStruct((NZ, OUT_...  15.8 us
    ppermute x11, waiting for transfers between devices, quad_swap(): return lax.ppermute(x, ('x', 'core'), [(i, i ^ k) for i in range(NQ)])  15.3 us
    ppermute x11, starting transfers between devices, quad_swap(): return lax.ppermute(x, ('x', 'core'), [(i, i ^ k) for i in range(NQ)])  14.9 us
    ppermute x8, starting transfers between devices, z_shift(): return lax.ppermute(x, 'z', [(i, (i + k) % NZ) for i in range(NZ)])  14.7 us
    all_to_all x1, blocking collectives, body(): parts = lax.all_to_all(parts, 'z', 0, 0, tiled=True)  12.7 us
    unnamed x39, local copies, waits for them, and re-layouts  10.1 us
    ppermute x5, local copies, waits for them, and re-layouts, quad_swap(): return lax.ppermute(x, ('x', 'core'), [(i, i ^ k) for i in range(NQ)])  7.58 us
    ppermute x8, waiting for transfers between devices, z_shift(): return lax.ppermute(x, 'z', [(i, (i + k) % NZ) for i in range(NZ)])  5.44 us
  transfers between devices with their start and end apart: 19, of which 6 were waited for; matrix products, arithmetic and copies ran while one was open for 13% of the time, Pallas kernels for 0%

profile of v1, /device:TPU:1, one launch (start us, length us, event | category | flops | bytes accessed | tf_op | source)
XLA Modules:
  0.0 107.7 jit_solution(11730151391589254869)
XLA Ops:
  2.9 3.3 %collective-permute-start.2 = (bf16[164,128]{1,0:T(8,128)(2,1)S(1)}, bf16[164,128]{1,0:T(8,128)(2,1)S(1)}, u32[]{:S(2)}, u32[]{:S(2)}) collective-permute-start(bf16[164,128]{1,0:T(8,128)(2,1)S(1)} %get-tuple-element.17), channel_id=1, source_target_pairs={{0,8},{8,0},{16,24},{24,16},{1,9},{9,1},{17,25},{25,17},{2,10},{10... | collective-permute-start | bytes 125960 | tf_op jit(solution)/shard_map/ppermute | solution.py:226
  6.2 1.7 %collective-permute-start = (bf16[164,128]{1,0:T(8,128)(2,1)S(1)}, bf16[164,128]{1,0:T(8,128)(2,1)S(1)}, u32[]{:S(2)}, u32[]{:S(2)}) collective-permute-start(bf16[164,128]{1,0:T(8,128)(2,1)S(1)} %get-tuple-element.19), channel_id=1, source_target_pairs={{0,24},{8,16},{16,8},{24,0},{1,25},{9,17},{17,9},{25,1},{2,26},{10... | collective-permute-start | bytes 125960 | tf_op jit(solution)/shard_map/ppermute | solution.py:226
  8.1 1.3 %fusion.1 = (bf16[512,576]{0,1:T(8,128)(2,1)S(1)}, bf16[512,576]{0,1:T(8,128)(2,1)S(1)}) fusion(bf16[1024,576]{0,1:T(8,128)(2,1)} %param.8), kind=kLoop, calls=%fused_computation.46 | loop fusion | bytes 2359296 | tf_op jit(solution)/shard_map/slice | solution.py:283
  9.6 1.5 %collective-permute-start.12 = (bf16[512,576]{0,1:T(8,128)(2,1)S(1)}, bf16[512,576]{0,1:T(8,128)(2,1)}, u32[]{:S(2)}, u32[]{:S(2)}) collective-permute-start(bf16[512,576]{0,1:T(8,128)(2,1)S(1)} %get-tuple-element.10), channel_id=1, source_target_pairs={{0,16},{8,24},{16,0},{24,8},{1,17},{9,25},{17,1},{25,9},{2,18},{10... | collective-permute-start | bytes 1769480 | tf_op jit(solution)/shard_map/ppermute | solution.py:226
  11.5 3.9 %collective-permute-start.4 = (bf16[656,128]{1,0:T(8,128)(2,1)S(1)}, bf16[656,128]{1,0:T(8,128)(2,1)S(1)}, u32[]{:S(2)}, u32[]{:S(2)}) collective-permute-start(bf16[656,128]{1,0:T(8,128)(2,1)S(1)} %pad_maximum_fusion.1.refs_0_), channel_id=1, source_target_pairs={{0,224},{32,0},{64,32},{96,64},{128,96},{160,128},{192,160},{224,1... | collective-permute-start | bytes 503816 | tf_op jit(solution)/shard_map/ppermute | solution.py:230
  15.4 2.6 %collective-permute-done.4.refs_2_ = bf16[656,128]{1,0:T(8,128)(2,1)S(1)} collective-permute-done((bf16[656,128]{1,0:T(8,128)(2,1)S(1)}, bf16[656,128]{1,0:T(8,128)(2,1)S(1)}, u32[]{:S(2)}, u32[]{:S(2)}) %collective-permute-start.4) | collective-permute-done | bytes 167968 | tf_op jit(solution)/shard_map/ppermute | solution.py:230
  18.1 3.4 %collective-permute-start.6 = (bf16[656,128]{1,0:T(8,128)(2,1)S(1)}, bf16[656,128]{1,0:T(8,128)(2,1)S(1)}, u32[]{:S(2)}, u32[]{:S(2)}) collective-permute-start(bf16[656,128]{1,0:T(8,128)(2,1)S(1)} %collective-permute-done.4.refs_2_), channel_id=1, source_target_pairs={{0,224},{32,0},{64,32},{96,64},{128,96},{160,128},{192,160},{224,1... | collective-permute-start | bytes 503816 | tf_op jit(solution)/shard_map/ppermute | solution.py:230
  21.5 2.5 %collective-permute-done.13 = bf16[512,576]{0,1:T(8,128)(2,1)S(1)} collective-permute-done((bf16[512,576]{0,1:T(8,128)(2,1)S(1)}, bf16[512,576]{0,1:T(8,128)(2,1)S(1)}, u32[]{:S(2)}, u32[]{:S(2)}) %collective-permute-start.13) | collective-permute-done | bytes 589856 | tf_op jit(solution)/shard_map/ppermute | solution.py:226
  24.0 2.0 %collective-permute-start.15 = (bf16[512,576]{0,1:T(8,128)(2,1)S(1)}, bf16[512,576]{0,1:T(8,128)(2,1)}, u32[]{:S(2)}, u32[]{:S(2)}) collective-permute-start(bf16[512,576]{0,1:T(8,128)(2,1)S(1)} %collective-permute-done.13), channel_id=1, source_target_pairs={{0,8},{8,0},{16,24},{24,16},{1,9},{9,1},{17,25},{25,17},{2,10},{10... | collective-permute-start | bytes 1769480 | tf_op jit(solution)/shard_map/ppermute | solution.py:226
  26.0 10.8 %collective-permute-done.12 = bf16[512,576]{0,1:T(8,128)(2,1)} collective-permute-done((bf16[512,576]{0,1:T(8,128)(2,1)S(1)}, bf16[512,576]{0,1:T(8,128)(2,1)}, u32[]{:S(2)}, u32[]{:S(2)}) %collective-permute-start.12) | collective-permute-done | bytes 589856 | tf_op jit(solution)/shard_map/ppermute | solution.py:226
  36.8 1.2 %collective-permute-start.14 = (bf16[512,576]{0,1:T(8,128)(2,1)}, bf16[512,576]{0,1:T(8,128)(2,1)}, u32[]{:S(2)}, u32[]{:S(2)}) collective-permute-start(bf16[512,576]{0,1:T(8,128)(2,1)} %collective-permute-done.12), channel_id=1, source_target_pairs={{0,8},{8,0},{16,24},{24,16},{1,9},{9,1},{17,25},{25,17},{2,10},{10... | collective-permute-start | bytes 1769480 | tf_op jit(solution)/shard_map/ppermute | solution.py:226
  38.8 3.9 %collective-permute-start.8 = (bf16[656,128]{1,0:T(8,128)(2,1)S(1)}, bf16[656,128]{1,0:T(8,128)(2,1)S(1)}, u32[]{:S(2)}, u32[]{:S(2)}) collective-permute-start(bf16[656,128]{1,0:T(8,128)(2,1)S(1)} %collective-permute-done.6.refs_4_), channel_id=1, source_target_pairs={{0,224},{32,0},{64,32},{96,64},{128,96},{160,128},{192,160},{224,1... | collective-permute-start | bytes 503816 | tf_op jit(solution)/shard_map/ppermute | solution.py:230
  42.8 0.9 clamp_select_fusion.refs_9_
  43.7 2.8 %collective-permute-done.8.refs_6_ = bf16[656,128]{1,0:T(8,128)(2,1)S(1)} collective-permute-done((bf16[656,128]{1,0:T(8,128)(2,1)S(1)}, bf16[656,128]{1,0:T(8,128)(2,1)S(1)}, u32[]{:S(2)}, u32[]{:S(2)}) %collective-permute-start.8) | collective-permute-done | bytes 167968 | tf_op jit(solution)/shard_map/ppermute | solution.py:230
  47.1 3.4 %collective-permute-start.10 = (bf16[336,128]{1,0:T(8,128)(2,1)}, bf16[336,128]{1,0:T(8,128)(2,1)S(1)}, u32[]{:S(2)}, u32[]{:S(2)}) collective-permute-start(bf16[336,128]{1,0:T(8,128)(2,1)} %slice.43), channel_id=1, source_target_pairs={{0,224},{32,0},{64,32},{96,64},{128,96},{160,128},{192,160},{224,1... | collective-permute-start | bytes 258056 | tf_op jit(solution)/shard_map/ppermute | solution.py:230
  51.9 1.7 %copy.101.refs_10_ = bf16[1024,576]{1,0:T(8,128)(2,1)S(1)} copy(bf16[1024,576]{0,1:T(8,128)(2,1)} %param.8) | data formatting | bytes 2359296 | tf_op args[1]
  53.6 1.4 %copy.103.refs_12_ = bf16[512,576]{1,0:T(8,128)(2,1)S(1)} copy(bf16[512,576]{0,1:T(8,128)(2,1)} %collective-permute-done.12) | data formatting | bytes 1179648 | tf_op jit(solution)/shard_map/ppermute | solution.py:226
  55.3 1.4 %copy.106.refs_15_ = bf16[512,576]{1,0:T(8,128)(2,1)S(1)} copy(bf16[512,576]{0,1:T(8,128)(2,1)} %collective-permute-done.15) | data formatting | bytes 1179648 | tf_op jit(solution)/shard_map/ppermute | solution.py:226
  56.7 2.1 %copy.105.refs_14_ = bf16[512,576]{1,0:T(8,128)(2,1)} copy(bf16[512,576]{0,1:T(8,128)(2,1)} %collective-permute-done.14) | data formatting | bytes 1179648 | tf_op jit(solution)/shard_map/ppermute | solution.py:226
  58.8 2.4 %copy.102.refs_11_ = bf16[1024,576]{1,0:T(8,128)(2,1)} copy(bf16[1024,576]{0,1:T(8,128)(2,1)} %collective-permute-done.11) | data formatting | bytes 2359296 | tf_op jit(solution)/shard_map/ppermute | solution.py:226
  61.2 1.1 %copy-done = bf16[512,576]{1,0:T(8,128)(2,1)S(1)} copy-done((bf16[512,576]{1,0:T(8,128)(2,1)S(1)}, bf16[512,576]{1,0:T(8,128)(2,1)}, u32[]{:S(2)}) %copy-start) | copy-done | bytes 589848
  62.3 1.0 copy-done.1
  63.3 0.9 copy-done.3
  64.3 0.9 copy-done.5
  65.2 0.9 copy-done.7
  66.1 0.9 copy-done.9
  67.9 0.9 copy-done.13
  68.8 15.8 %attention.1 = bf16[8,112,128]{2,1,0:T(8,128)(2,1)S(1)} custom-call(s32[8]{0:T(128)S(1)} %and_select_fusion.zsrc, bf16[656,128]{1,0:T(8,128)(2,1)S(1)} %pad_maximum_fusion.1.refs_0_, bf16[656,128]{1,0:T(8,128)(2,1)S(1)} %copy-done.9, bf16[656,128]{1,0:T(8,128)(2,1)S(1)} %copy-done.7, bf16[656,128]{1,0:T(8,128)(2,1)S(1)} %copy-done.13, ...), custom_call_target="tpu_custom_call" | custom-call | flops 6845104128 | bytes 8388608 | tf_op jit(solution)/shard_map/attention/pallas_call | solution.py:168
  84.7 12.7 %all_to_all.5.parts = bf16[8,112,128]{2,1,0:T(8,128)(2,1)} all-to-all(bf16[8,112,128]{2,1,0:T(8,128)(2,1)S(1)} %attention.1), channel_id=1, replica_groups=mesh['z'=8,'x'=2,'core'=2,'head'=8] {'z'}, dimensions={0} | all-to-all | bytes 458752 | tf_op jit(solution)/shard_map/all_to_all | solution.py:298
  97.4 1.8 %combine.1 = bf16[96,128]{1,0:T(8,128)(2,1)} custom-call(bf16[8,112,128]{2,1,0:T(8,128)(2,1)} %all_to_all.5.parts), custom_call_target="tpu_custom_call" | custom-call | tf_op jit(solution)/shard_map/combine/pallas_call | solution.py:216
  100.0 4.4 %collective-permute-start.16 = (bf16[24,128]{1,0:T(8,128)(2,1)S(1)}, bf16[24,128]{1,0:T(8,128)(2,1)S(1)}, u32[]{:S(2)}, u32[]{:S(2)}) collective-permute-start(bf16[24,128]{1,0:T(8,128)(2,1)S(1)} %bitcast.99), channel_id=1, source_target_pairs={{0,24},{8,16},{16,8},{24,0},{1,25},{9,17},{17,9},{25,1},{2,26},{10... | collective-permute-start | bytes 18440 | tf_op jit(solution)/shard_map/ppermute | solution.py:226
  105.0 1.1 %collective-permute-done.16 = bf16[24,128]{1,0:T(8,128)(2,1)S(1)} collective-permute-done((bf16[24,128]{1,0:T(8,128)(2,1)S(1)}, bf16[24,128]{1,0:T(8,128)(2,1)S(1)}, u32[]{:S(2)}, u32[]{:S(2)}) %collective-permute-start.16) | collective-permute-done | bytes 6176 | tf_op jit(solution)/shard_map/ppermute | solution.py:226
  (97 shorter events, 10.4 us)
Async XLA Ops:
  2.9 6.8 %collective-permute-start.2 = (bf16[164,128]{1,0:T(8,128)(2,1)S(1)}, bf16[164,128]{1,0:T(8,128)(2,1)S(1)}, u32[]{:S(2)}, u32[]{:S(2)}) collective-permute-start(bf16[164,128]{1,0:T(8,128)(2,1)S(1)} %get-tuple-element.17), channel_id=1, source_target_pairs={{0,8},{8,0},{16,24},{24,16},{1,9},{9,1},{17,25},{25,17},{2,10},{10... | collective-permute-start | bytes 125960 | tf_op jit(solution)/shard_map/ppermute | solution.py:226
  6.2 5.0 %collective-permute-start.1 = (bf16[164,128]{1,0:T(8,128)(2,1)S(1)}, bf16[164,128]{1,0:T(8,128)(2,1)S(1)}, u32[]{:S(2)}, u32[]{:S(2)}) collective-permute-start(bf16[164,128]{1,0:T(8,128)(2,1)S(1)} %get-tuple-element.18), channel_id=1, source_target_pairs={{0,16},{8,24},{16,0},{24,8},{1,17},{9,25},{17,1},{25,9},{2,18},{10... | collective-permute-start | bytes 125960 | tf_op jit(solution)/shard_map/ppermute | solution.py:226
  6.2 3.3 %copy-start.15 = (s32[64]{0:T(128)S(1)}, s32[64]{0:T(128)}, u32[]{:S(2)}) copy-start(s32[64]{0:T(128)} %param.12) | copy-start | bytes 772
  6.2 5.0 %collective-permute-start = (bf16[164,128]{1,0:T(8,128)(2,1)S(1)}, bf16[164,128]{1,0:T(8,128)(2,1)S(1)}, u32[]{:S(2)}, u32[]{:S(2)}) collective-permute-start(bf16[164,128]{1,0:T(8,128)(2,1)S(1)} %get-tuple-element.19), channel_id=1, source_target_pairs={{0,24},{8,16},{16,8},{24,0},{1,25},{9,17},{17,9},{25,1},{2,26},{10... | collective-permute-start | bytes 125960 | tf_op jit(solution)/shard_map/ppermute | solution.py:226
  7.9 50.9 %collective-permute-start.11 = (bf16[1024,576]{0,1:T(8,128)(2,1)}, bf16[1024,576]{0,1:T(8,128)(2,1)}, u32[]{:S(2)}, u32[]{:S(2)}) collective-permute-start(bf16[1024,576]{0,1:T(8,128)(2,1)} %param.8), channel_id=1, source_target_pairs={{0,8},{8,0},{16,24},{24,16},{1,9},{9,1},{17,25},{25,17},{2,10},{10... | collective-permute-start | bytes 3538952 | tf_op jit(solution)/shard_map/ppermute | solution.py:226
  9.4 28.8 %copy-start.14 = (s32[3,64,16]{1,2,0:T(8,128)S(1)}, s32[3,64,16]{1,2,0:T(8,128)}, u32[]{:S(2)}) copy-start(s32[3,64,16]{1,2,0:T(8,128)} %param.11) | copy-start | bytes 36868
  9.4 14.6 %collective-permute-start.13 = (bf16[512,576]{0,1:T(8,128)(2,1)S(1)}, bf16[512,576]{0,1:T(8,128)(2,1)S(1)}, u32[]{:S(2)}, u32[]{:S(2)}) collective-permute-start(bf16[512,576]{0,1:T(8,128)(2,1)S(1)} %get-tuple-element.9), channel_id=1, source_target_pairs={{0,16},{8,24},{16,0},{24,8},{1,17},{9,25},{17,1},{25,9},{2,18},{10... | collective-permute-start | bytes 1769480 | tf_op jit(solution)/shard_map/ppermute | solution.py:226
  9.6 27.1 %collective-permute-start.12 = (bf16[512,576]{0,1:T(8,128)(2,1)S(1)}, bf16[512,576]{0,1:T(8,128)(2,1)}, u32[]{:S(2)}, u32[]{:S(2)}) collective-permute-start(bf16[512,576]{0,1:T(8,128)(2,1)S(1)} %get-tuple-element.10), channel_id=1, source_target_pairs={{0,16},{8,24},{16,0},{24,8},{1,17},{9,25},{17,1},{25,9},{2,18},{10... | collective-permute-start | bytes 1769480 | tf_op jit(solution)/shard_map/ppermute | solution.py:226
  11.4 40.5 %copy-start.16 = (s32[8]{0:T(128)S(1)}, s32[8]{0:T(128)}, u32[]{:S(2)}) copy-start(s32[8]{0:T(128)} %constant.78.clone) | copy-start | bytes 100
  11.5 6.6 %collective-permute-start.4 = (bf16[656,128]{1,0:T(8,128)(2,1)S(1)}, bf16[656,128]{1,0:T(8,128)(2,1)S(1)}, u32[]{:S(2)}, u32[]{:S(2)}) collective-permute-start(bf16[656,128]{1,0:T(8,128)(2,1)S(1)} %pad_maximum_fusion.1.refs_0_), channel_id=1, source_target_pairs={{0,224},{32,0},{64,32},{96,64},{128,96},{160,128},{192,160},{224,1... | collective-permute-start | bytes 503816 | tf_op jit(solution)/shard_map/ppermute | solution.py:230
  15.4 6.1 %collective-permute-start.3 = (bf16[656,128]{1,0:T(8,128)(2,1)S(1)}, bf16[656,128]{1,0:T(8,128)(2,1)S(1)}, u32[]{:S(2)}, u32[]{:S(2)}) collective-permute-start(bf16[656,128]{1,0:T(8,128)(2,1)S(1)} %pad_maximum_fusion.1.refs_0_), channel_id=1, source_target_pairs={{0,32},{32,64},{64,96},{96,128},{128,160},{160,192},{192,224},{224... | collective-permute-start | bytes 503816 | tf_op jit(solution)/shard_map/ppermute | solution.py:230
  18.1 33.8 %copy-start.6 = (bf16[656,128]{1,0:T(8,128)(2,1)}, bf16[656,128]{1,0:T(8,128)(2,1)S(1)}, u32[]{:S(2)}) copy-start(bf16[656,128]{1,0:T(8,128)(2,1)S(1)} %collective-permute-done.4.refs_2_) | copy-start | bytes 503812
  18.1 20.7 %collective-permute-start.6 = (bf16[656,128]{1,0:T(8,128)(2,1)S(1)}, bf16[656,128]{1,0:T(8,128)(2,1)S(1)}, u32[]{:S(2)}, u32[]{:S(2)}) collective-permute-start(bf16[656,128]{1,0:T(8,128)(2,1)S(1)} %collective-permute-done.4.refs_2_), channel_id=1, source_target_pairs={{0,224},{32,0},{64,32},{96,64},{128,96},{160,128},{192,160},{224,1... | collective-permute-start | bytes 503816 | tf_op jit(solution)/shard_map/ppermute | solution.py:230
  21.5 30.4 %copy-start.8 = (bf16[656,128]{1,0:T(8,128)(2,1)}, bf16[656,128]{1,0:T(8,128)(2,1)S(1)}, u32[]{:S(2)}) copy-start(bf16[656,128]{1,0:T(8,128)(2,1)S(1)} %collective-permute-done.3.refs_1_) | copy-start | bytes 503812
  21.5 21.3 %collective-permute-start.5 = (bf16[656,128]{1,0:T(8,128)(2,1)S(1)}, bf16[656,128]{1,0:T(8,128)(2,1)S(1)}, u32[]{:S(2)}, u32[]{:S(2)}) collective-permute-start(bf16[656,128]{1,0:T(8,128)(2,1)S(1)} %collective-permute-done.3.refs_1_), channel_id=1, source_target_pairs={{0,32},{32,64},{64,96},{96,128},{128,160},{160,192},{192,224},{224... | collective-permute-start | bytes 503816 | tf_op jit(solution)/shard_map/ppermute | solution.py:230
  24.0 31.2 %collective-permute-start.15 = (bf16[512,576]{0,1:T(8,128)(2,1)S(1)}, bf16[512,576]{0,1:T(8,128)(2,1)}, u32[]{:S(2)}, u32[]{:S(2)}) collective-permute-start(bf16[512,576]{0,1:T(8,128)(2,1)S(1)} %collective-permute-done.13), channel_id=1, source_target_pairs={{0,8},{8,0},{16,24},{24,16},{1,9},{9,1},{17,25},{25,17},{2,10},{10... | collective-permute-start | bytes 1769480 | tf_op jit(solution)/shard_map/ppermute | solution.py:226
  36.8 19.9 %collective-permute-start.14 = (bf16[512,576]{0,1:T(8,128)(2,1)}, bf16[512,576]{0,1:T(8,128)(2,1)}, u32[]{:S(2)}, u32[]{:S(2)}) collective-permute-start(bf16[512,576]{0,1:T(8,128)(2,1)} %collective-permute-done.12), channel_id=1, source_target_pairs={{0,8},{8,0},{16,24},{24,16},{1,9},{9,1},{17,25},{25,17},{2,10},{10... | collective-permute-start | bytes 1769480 | tf_op jit(solution)/shard_map/ppermute | solution.py:226
  38.8 13.0 %copy-start.10 = (bf16[656,128]{1,0:T(8,128)(2,1)}, bf16[656,128]{1,0:T(8,128)(2,1)S(1)}, u32[]{:S(2)}) copy-start(bf16[656,128]{1,0:T(8,128)(2,1)S(1)} %collective-permute-done.6.refs_4_) | copy-start | bytes 503812
  38.8 7.6 %collective-permute-start.8 = (bf16[656,128]{1,0:T(8,128)(2,1)S(1)}, bf16[656,128]{1,0:T(8,128)(2,1)S(1)}, u32[]{:S(2)}, u32[]{:S(2)}) collective-permute-start(bf16[656,128]{1,0:T(8,128)(2,1)S(1)} %collective-permute-done.6.refs_4_), channel_id=1, source_target_pairs={{0,224},{32,0},{64,32},{96,64},{128,96},{160,128},{192,160},{224,1... | collective-permute-start | bytes 503816 | tf_op jit(solution)/shard_map/ppermute | solution.py:230
  42.8 9.1 %copy-start.12 = (bf16[656,128]{1,0:T(8,128)(2,1)}, bf16[656,128]{1,0:T(8,128)(2,1)S(1)}, u32[]{:S(2)}) copy-start(bf16[656,128]{1,0:T(8,128)(2,1)S(1)} %collective-permute-done.5.refs_3_) | copy-start | bytes 503812
  42.8 7.8 %collective-permute-start.7 = (bf16[656,128]{1,0:T(8,128)(2,1)S(1)}, bf16[656,128]{1,0:T(8,128)(2,1)S(1)}, u32[]{:S(2)}, u32[]{:S(2)}) collective-permute-start(bf16[656,128]{1,0:T(8,128)(2,1)S(1)} %collective-permute-done.5.refs_3_), channel_id=1, source_target_pairs={{0,32},{32,64},{64,96},{96,128},{128,160},{160,192},{192,224},{224... | collective-permute-start | bytes 503816 | tf_op jit(solution)/shard_map/ppermute | solution.py:230
  46.5 5.4 %copy-start.2 = (bf16[656,128]{1,0:T(8,128)(2,1)}, bf16[656,128]{1,0:T(8,128)(2,1)S(1)}, u32[]{:S(2)}) copy-start(bf16[656,128]{1,0:T(8,128)(2,1)S(1)} %collective-permute-done.8.refs_6_) | copy-start | bytes 503812
  47.1 14.1 %collective-permute-start.10 = (bf16[336,128]{1,0:T(8,128)(2,1)}, bf16[336,128]{1,0:T(8,128)(2,1)S(1)}, u32[]{:S(2)}, u32[]{:S(2)}) collective-permute-start(bf16[336,128]{1,0:T(8,128)(2,1)} %slice.43), channel_id=1, source_target_pairs={{0,224},{32,0},{64,32},{96,64},{128,96},{160,128},{192,160},{224,1... | collective-permute-start | bytes 258056 | tf_op jit(solution)/shard_map/ppermute | solution.py:230
  51.9 9.4 %collective-permute-start.9 = (bf16[320,128]{1,0:T(8,128)(2,1)}, bf16[320,128]{1,0:T(8,128)(2,1)}, u32[]{:S(2)}, u32[]{:S(2)}) collective-permute-start(bf16[320,128]{1,0:T(8,128)(2,1)} %slice.42), channel_id=1, source_target_pairs={{0,32},{32,64},{64,96},{96,128},{128,160},{160,192},{192,224},{224... | collective-permute-start | bytes 245768 | tf_op jit(solution)/shard_map/ppermute | solution.py:230
  61.2 1.1 %copy-start = (bf16[512,576]{1,0:T(8,128)(2,1)S(1)}, bf16[512,576]{1,0:T(8,128)(2,1)}, u32[]{:S(2)}) copy-start(bf16[512,576]{1,0:T(8,128)(2,1)} %copy.105.refs_14_) | copy-start | bytes 1769476
  62.3 1.0 copy-start.1
  63.3 0.9 copy-start.3
  64.2 0.9 copy-start.5
  65.2 0.9 copy-start.7
  100.0 6.0 %collective-permute-start.16 = (bf16[24,128]{1,0:T(8,128)(2,1)S(1)}, bf16[24,128]{1,0:T(8,128)(2,1)S(1)}, u32[]{:S(2)}, u32[]{:S(2)}) collective-permute-start(bf16[24,128]{1,0:T(8,128)(2,1)S(1)} %bitcast.99), channel_id=1, source_target_pairs={{0,24},{8,16},{16,8},{24,0},{1,25},{9,17},{17,9},{25,1},{2,26},{10... | collective-permute-start | bytes 18440 | tf_op jit(solution)/shard_map/ppermute | solution.py:226
  104.5 2.5 %collective-permute-start.17 = (bf16[24,128]{1,0:T(8,128)(2,1)S(1)}, bf16[24,128]{1,0:T(8,128)(2,1)S(1)}, u32[]{:S(2)}, u32[]{:S(2)}) collective-permute-start(bf16[24,128]{1,0:T(8,128)(2,1)S(1)} %bitcast.98), channel_id=1, source_target_pairs={{0,16},{8,24},{16,0},{24,8},{1,17},{9,25},{17,1},{25,9},{2,18},{10... | collective-permute-start | bytes 18440 | tf_op jit(solution)/shard_map/ppermute | solution.py:226
  104.7 2.2 %collective-permute-start.18 = (bf16[24,128]{1,0:T(8,128)(2,1)S(1)}, bf16[24,128]{1,0:T(8,128)(2,1)S(1)}, u32[]{:S(2)}, u32[]{:S(2)}) collective-permute-start(bf16[24,128]{1,0:T(8,128)(2,1)S(1)} %bitcast.97), channel_id=1, source_target_pairs={{0,8},{8,0},{16,24},{24,16},{1,9},{9,1},{17,25},{25,17},{2,10},{10... | collective-permute-start | bytes 18440 | tf_op jit(solution)/shard_map/ppermute | solution.py:226
  (4 other events, 3.4 us)

commit v2 on v1

v2 whole, which is shorter than its diff:
```python
import functools

import jax
import jax.numpy as jnp
from jax import lax
from jax.experimental import pallas as pl
from jax.experimental.pallas import tpu as pltpu
from jax.sharding import Mesh
from jax.sharding import PartitionSpec as P

DN = 128
R = 64
C = 512
DV = 128
BLK = 128
STEPS = 3
TOPK = 16

NZ = 8
NQ = 4
HG = 4
BZ = 8
RZ = STEPS * BZ
RT = NZ * RZ
RH = HG * RT
S_DEV = 1024
NBLK = S_DEV // BLK

QN0, QR0, UK0, UV0, PIECE = 0, 96, 144, 400, 656
HALF = 320
OFFSETS = (0, -1, 1, -2, 2, -3, 3, 4)
OUT_ROWS = 112

NEG = -1e30
SCALE = (DN + R) ** (-0.5)
LOG2E = 1.4426950408889634

VMEM = pl.BlockSpec(memory_space=pltpu.VMEM)


def dot(a, b, dims):
    return lax.dot_general(a, b, (dims, ((), ())), preferred_element_type=jnp.float32)


def iota(shape, dim):
    return lax.broadcasted_iota(jnp.int32, shape, dim)


def params():
    return pltpu.CompilerParams(vmem_limit_bytes=24 * 1024 * 1024)


def my_z():
    return lax.axis_index("z")


def my_quad():
    return lax.axis_index("x") * 2 + lax.axis_index("core")


def limits_kernel(chosen, lengths, out):
    z, quad = my_z(), my_quad()
    length = lengths[...]
    columns = [
        jnp.concatenate(
            [chosen[t], length >> 8, length & 255, jnp.zeros((14, 64), jnp.int32)], axis=0
        )
        for t in range(STEPS)
    ]
    table = jnp.concatenate(columns, axis=1).astype(jnp.float32).astype(jnp.bfloat16)
    row = iota((RT, RT), 0)
    row_z = (row * 2731) >> 16
    rest = row - row_z * RZ
    row_quad = (rest * 43) >> 8
    rest = rest - row_quad * 6
    source = (rest >> 1) * 64 + row_z * BZ + row_quad * 2 + (rest & 1)
    pick = jnp.where(source == iota((RT, RT), 1), 1.0, 0.0).astype(jnp.bfloat16)
    rows = dot(pick, table, ((1,), (1,))).astype(jnp.int32)
    row = iota((RT, 1), 0)
    within = row - ((row * 10923) >> 16) * 6
    ends = rows[:, 16:17] * 256 + rows[:, 17:18] + (within >> 1)
    lane = iota((RT, 128), 1)
    for i in range(NQ):
        block = (z * NQ + (quad ^ i)) * NBLK + lane
        hit = block == rows[:, 0:1]
        for k in range(1, TOPK):
            hit = jnp.logical_or(hit, block == rows[:, k : k + 1])
        count = jnp.clip(ends - block * BLK, 0, BLK)
        out[i] = jnp.where(hit, count, 0)


def visible_limits(selected, lengths):
    return pl.pallas_call(
        limits_kernel,
        out_shape=jax.ShapeDtypeStruct((NQ, RT, 128), jnp.int32),
        in_specs=[VMEM] * 2,
        out_specs=VMEM,
        name="limits",
    )(selected.transpose(0, 2, 1), lengths.reshape(1, -1))


def attend(parts, first, lim, probe, scores, top, total, latent):
    lane = iota((RT, BLK), 1)
    old = top[...]
    for i, part in enumerate(parts):
        whole = dot(probe[...], part[...], ((1,), (0,)))
        for h in range(HG):
            mine = slice(h * RT, (h + 1) * RT)
            best = top[mine, :]
            for j in range(NBLK):
                seen = lane < lim[first + i, :, j : j + 1]
                block = jnp.where(seen, whole[mine, j * BLK : (j + 1) * BLK], NEG)
                scores[i, mine, j * BLK : (j + 1) * BLK] = block
                best = jnp.maximum(best, block)
            top[mine, :] = best
    best = jnp.broadcast_to(jnp.max(top[...], axis=1, keepdims=True), top.shape)
    top[...] = best
    if first:
        fade = jnp.exp2((old - jnp.maximum(best, 0.1 * NEG)) * (SCALE * LOG2E))
        total[...] = total[...] * fade
        for c in range(C // 128):
            here = slice(c * 128, (c + 1) * 128)
            latent[:, here] = latent[:, here] * fade
    for i, part in enumerate(parts):
        weights = []
        for h in range(HG):
            mine = slice(h * RT, (h + 1) * RT)
            best = jnp.maximum(top[mine, :], 0.1 * NEG)
            summed = total[mine, :]
            blocks = []
            for j in range(NBLK):
                block = scores[i, mine, j * BLK : (j + 1) * BLK]
                weight = jnp.exp2((block - best) * (SCALE * LOG2E))
                summed = summed + weight
                blocks.append(weight.astype(jnp.bfloat16))
            total[mine, :] = summed
            weights.append(jnp.concatenate(blocks, axis=1))
        latent[...] += dot(jnp.concatenate(weights, axis=0), part[0:C, :], ((1,), (1,)))


def piece_rows(pieces, p, first, count):
    if p < NZ - 1 or first + count <= HALF:
        return pieces[p][first : first + count, :]
    return pieces[p + 1][first - HALF : first - HALF + count, :]


def near_kernel(*refs):
    pieces, (lim, own, mate), (probe, top, total, latent), (qn, qr, wuk, scores) = (
        refs[:9],
        refs[9:12],
        refs[12:16],
        refs[16:],
    )
    for p, offset in enumerate(OFFSETS):
        z = (my_z() + offset) & (NZ - 1)
        here = pl.ds(pl.multiple_of(z * RZ, RZ), RZ)
        block = piece_rows(pieces, p, QN0, 96).astype(jnp.float32)
        for h in range(HG):
            qn[h, here, :] = block[h * RZ : (h + 1) * RZ]
        block = piece_rows(pieces, p, QR0, 48).astype(jnp.float32)
        for j in range(HG // 2):
            qr[j, here, :] = block[j * RZ : (j + 1) * RZ]
        here = pl.ds(pl.multiple_of(z * 16, 16), 16)
        for h in range(HG):
            for cc in range(4):
                wuk[h, here, cc * 128 : (cc + 1) * 128] = piece_rows(
                    pieces, p, UK0 + (h * 4 + cc) * 16, 16
                )
    for h in range(HG):
        mine = slice(h * RT, (h + 1) * RT)
        absorbed = dot(qn[h].astype(jnp.bfloat16), wuk[h], ((1,), (0,)))
        probe[mine, 0:C] = absorbed.astype(jnp.bfloat16)
        rope = qr[h // 2][:, (h % 2) * R : (h % 2 + 1) * R]
        probe[mine, C : C + R] = rope.astype(jnp.bfloat16)
    top[...] = jnp.full(top.shape, NEG, jnp.float32)
    total[...] = jnp.zeros(total.shape, jnp.float32)
    latent[...] = jnp.zeros(latent.shape, jnp.float32)
    attend((own, mate), 0, lim, probe, scores, top, total, latent)


def near_positions(pieces, lim, own, mate):
    return pl.pallas_call(
        near_kernel,
        out_shape=(
            jax.ShapeDtypeStruct((RH, C + R), jnp.bfloat16),
            jax.ShapeDtypeStruct((RH, 128), jnp.float32),
            jax.ShapeDtypeStruct((RH, 128), jnp.float32),
            jax.ShapeDtypeStruct((RH, C), jnp.float32),
        ),
        in_specs=[VMEM] * 12,
        out_specs=(VMEM,) * 4,
        scratch_shapes=[
            pltpu.VMEM((HG, RT, DN), jnp.float32),
            pltpu.VMEM((HG // 2, RT, 2 * R), jnp.float32),
            pltpu.VMEM((HG, DN, C), jnp.bfloat16),
            pltpu.VMEM((2, RH, S_DEV), jnp.float32),
        ],
        compiler_params=params(),
        cost_estimate=pl.CostEstimate(
            flops=2 * RH * (2 * S_DEV * (2 * C + R) + DN * C),
            bytes_accessed=8 * 1024 * 1024,
            transcendentals=RH * 2 * S_DEV,
        ),
        name="near_positions",
    )(*pieces, lim, own, mate)


def middle_kernel(lim, low, probe, top_in, total_in, latent_in, top, total, latent, scores):
    top[...] = top_in[...]
    total[...] = total_in[...]
    latent[...] = latent_in[...]
    attend((low,), 2, lim, probe, scores, top, total, latent)


def middle_positions(lim, low, state):
    return pl.pallas_call(
        middle_kernel,
        out_shape=(
            jax.ShapeDtypeStruct((RH, 128), jnp.float32),
            jax.ShapeDtypeStruct((RH, 128), jnp.float32),
            jax.ShapeDtypeStruct((RH, C), jnp.float32),
        ),
        in_specs=[VMEM] * 6,
        out_specs=(VMEM,) * 3,
        scratch_shapes=[pltpu.VMEM((1, RH, S_DEV), jnp.float32)],
        compiler_params=params(),
        cost_estimate=pl.CostEstimate(
            flops=2 * RH * S_DEV * (2 * C + R),
            bytes_accessed=8 * 1024 * 1024,
            transcendentals=RH * S_DEV,
        ),
        name="middle_positions",
    )(lim, low, *state)


def far_kernel(*refs):
    pieces, (lim, high, probe, top_in, total_in, latent_in), out, (
        wuv,
        scores,
        top,
        total,
        latent,
    ) = refs[:9], refs[9:15], refs[15], refs[16:]
    for p, offset in enumerate(OFFSETS):
        z = (my_z() + offset) & (NZ - 1)
        here = pl.ds(pl.multiple_of(z * 64, 64), 64)
        for h in range(HG):
            wuv[h, here, :] = piece_rows(pieces, p, UV0 + h * 64, 64)
    top[...] = top_in[...]
    total[...] = total_in[...]
    latent[...] = latent_in[...]
    attend((high,), 3, lim, probe, scores, top, total, latent)

    parts, logs = [], []
    for h in range(HG):
        mine = slice(h * RT, (h + 1) * RT)
        norm = jnp.sum(total[mine, :], axis=1, keepdims=True)
        some = norm > 0.0
        norm = jnp.where(some, norm, 1.0)
        mean = (latent[mine, :] / norm).astype(jnp.bfloat16)
        parts.append(dot(mean, wuv[h], ((1,), (0,))))
        logs.append(jnp.where(some, top[mine, 0:1] * SCALE + jnp.log(norm), NEG))
    diagonal = iota((96, 128), 0) == iota((96, 128), 1)
    which = iota((16, 128), 0)
    for z in range(NZ):
        rows = slice(z * RZ, (z + 1) * RZ)
        block = jnp.concatenate([part[rows] for part in parts], axis=0)
        out[z, 0:96, :] = block.astype(jnp.bfloat16)
        column = jnp.concatenate([log[rows] for log in logs], axis=0)
        row = jnp.sum(jnp.where(diagonal, column, 0.0), axis=0, keepdims=True)
        high_part = row.astype(jnp.bfloat16).astype(jnp.float32)
        middle = (row - high_part).astype(jnp.bfloat16).astype(jnp.float32)
        rest = row - high_part - middle
        packed = jnp.where(
            which == 0,
            high_part,
            jnp.where(which == 1, middle, jnp.where(which == 2, rest, 0.0)),
        )
        out[z, 96:112, :] = packed.astype(jnp.bfloat16)


def far_positions(pieces, lim, high, state):
    return pl.pallas_call(
        far_kernel,
        out_shape=jax.ShapeDtypeStruct((NZ, OUT_ROWS, 128), jnp.bfloat16),
        in_specs=[VMEM] * 15,
        out_specs=VMEM,
        scratch_shapes=[
            pltpu.VMEM((HG, C, DV), jnp.bfloat16),
            pltpu.VMEM((1, RH, S_DEV), jnp.float32),
            pltpu.VMEM((RH, 128), jnp.float32),
            pltpu.VMEM((RH, 128), jnp.float32),
            pltpu.VMEM((RH, C), jnp.float32),
        ],
        compiler_params=params(),
        cost_estimate=pl.CostEstimate(
            flops=2 * RH * (S_DEV * (2 * C + R) + DV * C),
            bytes_accessed=8 * 1024 * 1024,
            transcendentals=RH * S_DEV,
        ),
        name="far_positions",
    )(*pieces, lim, high, *state)


def combine_kernel(parts, *outs):
    logs = []
    for z in range(NZ):
        packed = parts[z, 96:112, :].astype(jnp.float32)
        logs.append(packed[0:1] + packed[1:2] + packed[2:3])
    best = functools.reduce(jnp.maximum, logs)
    shares = [jnp.exp(log - best) for log in logs]
    norm = functools.reduce(jnp.add, shares)
    diagonal = iota((96, 128), 0) == iota((96, 128), 1)
    summed = jnp.zeros((96, 128), jnp.float32)
    for z in range(NZ):
        share = jnp.where(diagonal, shares[z] / norm, 0.0)
        column = jnp.sum(share, axis=1, keepdims=True)
        summed += column * parts[z, 0:96, :].astype(jnp.float32)
    row = iota((128, 96), 0)
    which, rest = row >> 5, row & 31
    head = (rest * 43) >> 8
    source = jnp.where(rest < 24, head * 24 + (my_quad() ^ which) * 6 + rest - head * 6, -1)
    pick = jnp.where(source == iota((128, 96), 1), 1.0, 0.0).astype(jnp.bfloat16)
    rows = dot(pick, summed.astype(jnp.bfloat16), ((1,), (0,))).astype(jnp.bfloat16)
    for k in range(NQ):
        outs[k][...] = rows[32 * k : 32 * (k + 1)]


def combine(parts):
    return pl.pallas_call(
        combine_kernel,
        out_shape=(jax.ShapeDtypeStruct((32, 128), jnp.bfloat16),) * NQ,
        in_specs=[VMEM],
        out_specs=(VMEM,) * NQ,
        name="combine",
    )(parts)


def quad_swap(x, k):
    return lax.ppermute(x, ("x", "core"), [(i, i ^ k) for i in range(NQ)])


def z_shift(x, k):
    return lax.ppermute(x, "z", [(i, (i + k) % NZ) for i in range(NZ)])


def by_sender(got):
    quad = my_quad()
    odd, upper = quad % 2 == 1, quad >= 2
    a, b, c, d = got
    a, b, c, d = (
        jnp.where(odd, b, a),
        jnp.where(odd, a, b),
        jnp.where(odd, d, c),
        jnp.where(odd, c, d),
    )
    return [
        jnp.where(upper, c, a),
        jnp.where(upper, d, b),
        jnp.where(upper, a, c),
        jnp.where(upper, b, d),
    ]


def quad_exchange(parts):
    quad = my_quad()
    got = [lax.dynamic_index_in_dim(parts, quad, 0, keepdims=False)]
    for k in range(1, NQ):
        got.append(quad_swap(lax.dynamic_index_in_dim(parts, quad ^ k, 0, keepdims=False), k))
    return jnp.stack(by_sender(got))


def body(queries, cache, w_uk, w_uv, selected, lengths):
    q = queries.reshape(STEPS, 2, NQ, HG, DN + R)
    qn = q[..., :DN].transpose(2, 3, 0, 1, 4).reshape(NQ, 24, 128)
    qr = q[..., DN:].reshape(STEPS, 2, NQ, 2, 2, R).transpose(2, 3, 0, 1, 4, 5).reshape(NQ, 12, 128)
    uk = w_uk.reshape(NQ, HG, 4, 4, 128).transpose(0, 1, 3, 2, 4).reshape(NQ, 64, 128)
    uv = w_uv.reshape(NQ, 64, 128)
    got = quad_exchange(jnp.concatenate([qn, qr, uk, uv], axis=1))
    piece = jnp.concatenate(
        [
            got[:, 0:24].reshape(NQ, HG, 6, 128).transpose(1, 0, 2, 3).reshape(96, 128),
            got[:, 24:36].reshape(NQ, 2, 6, 128).transpose(1, 0, 2, 3).reshape(48, 128),
            got[:, 36:100].reshape(NQ, 16, 4, 128).transpose(1, 0, 2, 3).reshape(256, 128),
            got[:, 100:164].reshape(NQ, HG, 16, 128).transpose(1, 0, 2, 3).reshape(256, 128),
        ],
        axis=0,
    )
    lim = visible_limits(selected, lengths)
    piece, lim, cache = lax.optimization_barrier((piece, lim, cache.T))

    up2, down2 = z_shift(piece, 2), z_shift(piece, -2)
    up1, down1 = z_shift(piece, 1), z_shift(piece, -1)
    mate, low = quad_swap(cache, 1), quad_swap(cache, 2)
    up2, down2, up1, down1, mate = lax.optimization_barrier((up2, down2, up1, down1, mate))
    up4, down4 = z_shift(up2[:HALF], 2), z_shift(down2[HALF:], -2)
    up3, down3 = z_shift(up2, 1), z_shift(down2, -1)
    pieces = [piece, up1, down1, up2, down2, up3, down3, up4, down4]

    probe, *state = near_positions(pieces, lim, cache, mate)
    low, probe, *state = lax.optimization_barrier((low, probe, *state))
    high = quad_swap(low, 1)
    state = middle_positions(lim, low, (probe, *state))
    parts = far_positions(pieces, lim, high, (probe, *state))
    parts = lax.all_to_all(parts, "z", 0, 0, tiled=True)
    mine = combine(parts)
    got = [mine[0]] + [quad_swap(mine[k], k) for k in range(1, NQ)]
    final = jnp.stack(by_sender(got))[:, :24]
    final = final.reshape(NQ, HG, STEPS, 2, DV).transpose(2, 3, 0, 1, 4)
    return final.reshape(STEPS, 2, NQ * HG, DV)


def solution(mesh):
    fine = Mesh(mesh.devices.reshape(NZ, 2, 2, -1), ("z", "x", "core", "head"))
    ctx = ("z", "x", "core")
    in_specs = (
        P(None, ctx, "head", None),
        P(ctx, None),
        P("head", ctx, None),
        P("head", ctx, None),
        P(),
        P(),
    )
    out_specs = P(None, ctx, "head", None)
    return jax.shard_map(body, mesh=fine, in_specs=in_specs, out_specs=out_specs, check_vma=False)
```

time: 108 us -> 79.6 us (0.74)
  local copies, waits for them, and re-layouts: 24.2 us -> 2.62 us
  waiting for transfers between devices: 20.7 us -> 14 us
  blocking collectives: 12.7 us -> 16.9 us
  starting transfers between devices: 29.6 us -> 26.9 us
    ppermute x11 -> x9, waiting for transfers between devices: 15.3 us -> 1.28 us  [quad_swap(): return lax.ppermute(x, ('x', 'core'), [(i, i ^ k) for i in range(NQ)])]
    unnamed x39 -> x4, local copies, waits for them, and re-layouts: 10.1 us -> 0.01 us
    ppermute x5 -> x0, local copies, waits for them, and re-layouts: 7.58 us -> none  [quad_swap(): return lax.ppermute(x, ('x', 'core'), [(i, i ^ k) for i in range(NQ)])]
    ppermute x8, waiting for transfers between devices: 5.44 us -> 12.8 us  [z_shift(): return lax.ppermute(x, 'z', [(i, (i + k) % NZ) for i in range(NZ)])]
    all_to_all x1, blocking collectives: 12.7 us -> 16.9 us  [body(): parts = lax.all_to_all(parts, 'z', 0, 0, tiled=True)]
    ppermute x8, starting transfers between devices: 14.7 us -> 11.9 us  [z_shift(): return lax.ppermute(x, 'z', [(i, (i + k) % NZ) for i in range(NZ)])]
    slice x3 -> x2, local copies, waits for them, and re-layouts: 2.62 us -> 0.01 us  [body(): up4, down4 = (z_shift(up2[:HALF], 2), z_shift(down2[HALF:], -2))]
    reshape x2 -> x0, local copies, waits for them, and re-layouts: 1.36 us -> none  [the longest x1 0.75 us: body(): mine.reshape(HG, NQ, 6, 128).transpose(1, 0, 2, 3).reshape(NQ, 24, 128)]
  transfers between devices with their start and end apart: 19 -> 17, of which waited for: 6 -> 5; matrix products, arithmetic and copies ran while one was open for 13% -> 0% of each run, Pallas kernels for 0% -> 14%
where the time goes in v2:
time: 79.6 us; the launch traced here: 79.2 us
  starting transfers between devices  26.9 us (34%)
  blocking collectives  16.9 us (21%)
  Pallas kernels  16.7 us (21%)
  waiting for transfers between devices  14 us (18%)
  local copies, waits for them, and re-layouts  2.62 us (3%)
  other arithmetic  1.72 us (2%)
    all_to_all x1, blocking collectives, body(): parts = lax.all_to_all(parts, 'z', 0, 0, tiled=True)  16.9 us
    ppermute x9, starting transfers between devices, quad_swap(): return lax.ppermute(x, ('x', 'core'), [(i, i ^ k) for i in range(NQ)])  15 us
    ppermute x8, waiting for transfers between devices, z_shift(): return lax.ppermute(x, 'z', [(i, (i + k) % NZ) for i in range(NZ)])  12.8 us
    ppermute x8, starting transfers between devices, z_shift(): return lax.ppermute(x, 'z', [(i, (i + k) % NZ) for i in range(NZ)])  11.9 us
    pallas_call x1, Pallas kernels, near_positions(): pl.pallas_call(near_kernel, out_shape=(jax.ShapeDtypeStruct((RH, C + R),...  5.37 us
    pallas_call x1, Pallas kernels, far_positions(): pl.pallas_call(far_kernel, out_shape=jax.ShapeDtypeStruct((NZ, OUT_ROWS,...  3.37 us
    pallas_call x1, Pallas kernels, middle_positions(): pl.pallas_call(middle_kernel, out_shape=(jax.ShapeDtypeStruct((RH, 128),...  3.18 us
    pallas_call x1, Pallas kernels, visible_limits(): pl.pallas_call(limits_kernel, out_shape=jax.ShapeDtypeStruct((NQ, RT, 128...  2.9 us
  transfers between devices with their start and end apart: 17, of which 5 were waited for; matrix products, arithmetic and copies ran while one was open for 0% of the time, Pallas kernels for 14%

profile of v2, /device:TPU:1, one launch (start us, length us, event | category | flops | bytes accessed | tf_op | source)
XLA Modules:
  0.0 79.2 jit_solution(11021515982910179763)
XLA Ops:
  0.0 0.8 %reshape.54 = bf16[3,2,4,4,192]{4,3,2,1,0:T(4,128)(2,1)S(1)} reshape(bf16[3,2,16,192]{3,2,1,0:T(8,128)(2,1)} %param.6) | data formatting | bytes 73728 | tf_op jit(solution)/shard_map/reshape | solution.py:374
  0.9 0.1 reshape.72
  1.0 0.9 %reshape.58 = bf16[4,4,4,4,128]{4,3,2,1,0:T(4,128)(2,1)S(1)} reshape(bf16[16,4,512]{2,1,0:T(4,128)(2,1)} %param.8) | data formatting | bytes 131072 | tf_op jit(solution)/shard_map/reshape | solution.py:377
  1.9 0.9 %pad_maximum_fusion = bf16[4,164,128]{2,1,0:T(8,128)(2,1)S(1)} fusion(bf16[4,64,128]{2,1,0:T(8,128)(2,1)} %bitcast.78, bf16[4,64,128]{2,1,0:T(8,128)(2,1)S(1)} %bitcast.71, bf16[4,12,128]{2,1,0:T(8,128)(2,1)S(1)} %reshape.72, bf16[4,24,128]{2,1,0:T(8,128)(2,1)S(1)} %bitcast.77), kind=kLoop, calls=%fused_computation | loop fusion | flops 671744 | bytes 335872 | tf_op jit(solution)/shard_map/concatenate | solution.py:379
  2.9 3.3 %collective-permute-start.2 = (bf16[164,128]{1,0:T(8,128)(2,1)S(1)}, bf16[164,128]{1,0:T(8,128)(2,1)S(1)}, u32[]{:S(2)}, u32[]{:S(2)}) collective-permute-start(bf16[164,128]{1,0:T(8,128)(2,1)S(1)} %get-tuple-element.59), channel_id=1, source_target_pairs={{0,8},{8,0},{16,24},{24,16},{1,9},{9,1},{17,25},{25,17},{2,10},{10... | collective-permute-start | bytes 125960 | tf_op jit(solution)/shard_map/ppermute | solution.py:340
  6.2 1.7 %collective-permute-start = (bf16[164,128]{1,0:T(8,128)(2,1)S(1)}, bf16[164,128]{1,0:T(8,128)(2,1)S(1)}, u32[]{:S(2)}, u32[]{:S(2)}) collective-permute-start(bf16[164,128]{1,0:T(8,128)(2,1)S(1)} %get-tuple-element.61), channel_id=1, source_target_pairs={{0,24},{8,16},{16,8},{24,0},{1,25},{9,17},{17,9},{25,1},{2,26},{10... | collective-permute-start | bytes 125960 | tf_op jit(solution)/shard_map/ppermute | solution.py:340
  7.9 2.9 %limits.1.refs_9_.lim = s32[4,192,128]{2,1,0:T(8,128)} custom-call(s32[3,16,64]{2,1,0:T(8,128)} %bitcast.80, s32[1,64]{1,0:T(1,128)} %bitcast.81), custom_call_target="tpu_custom_call" | custom-call | tf_op jit(solution)/shard_map/limits/pallas_call | solution.py:93
  10.8 0.0 collective-permute-done.2
  10.8 0.1 select_bitcast_fusion.3
  11.2 0.2 collective-permute-start.7
  11.4 0.6 collective-permute-start.12
  12.0 4.4 %collective-permute-start.6 = (bf16[656,128]{1,0:T(8,128)(2,1)S(1)}, bf16[656,128]{1,0:T(8,128)(2,1)S(1)}, u32[]{:S(2)}, u32[]{:S(2)}) collective-permute-start(bf16[656,128]{1,0:T(8,128)(2,1)S(1)} %pad_maximum_fusion.1.refs_0_), channel_id=1, source_target_pairs={{0,224},{32,0},{64,32},{96,64},{128,96},{160,128},{192,160},{224,1... | collective-permute-start | bytes 503816 | tf_op jit(solution)/shard_map/ppermute | solution.py:344
  16.4 1.9 %collective-permute-start.4 = (bf16[656,128]{1,0:T(8,128)(2,1)S(1)}, bf16[656,128]{1,0:T(8,128)(2,1)S(1)}, u32[]{:S(2)}, u32[]{:S(2)}) collective-permute-start(bf16[656,128]{1,0:T(8,128)(2,1)S(1)} %pad_maximum_fusion.1.refs_0_), channel_id=1, source_target_pairs={{0,192},{32,224},{64,0},{96,32},{128,64},{160,96},{192,128},{224,1... | collective-permute-start | bytes 503816 | tf_op jit(solution)/shard_map/ppermute | solution.py:344
  18.4 1.1 %collective-permute-done.6.refs_2_ = bf16[656,128]{1,0:T(8,128)(2,1)S(1)} collective-permute-done((bf16[656,128]{1,0:T(8,128)(2,1)S(1)}, bf16[656,128]{1,0:T(8,128)(2,1)S(1)}, u32[]{:S(2)}, u32[]{:S(2)}) %collective-permute-start.6) | collective-permute-done | bytes 167968 | tf_op jit(solution)/shard_map/ppermute | solution.py:344
  19.4 3.1 %collective-permute-done.5.refs_1_ = bf16[656,128]{1,0:T(8,128)(2,1)S(1)} collective-permute-done((bf16[656,128]{1,0:T(8,128)(2,1)S(1)}, bf16[656,128]{1,0:T(8,128)(2,1)S(1)}, u32[]{:S(2)}, u32[]{:S(2)}) %collective-permute-start.5) | collective-permute-done | bytes 167968 | tf_op jit(solution)/shard_map/ppermute | solution.py:344
  22.5 3.9 %collective-permute-done.4.refs_4_ = bf16[656,128]{1,0:T(8,128)(2,1)S(1)} collective-permute-done((bf16[656,128]{1,0:T(8,128)(2,1)S(1)}, bf16[656,128]{1,0:T(8,128)(2,1)S(1)}, u32[]{:S(2)}, u32[]{:S(2)}) %collective-permute-start.4) | collective-permute-done | bytes 167968 | tf_op jit(solution)/shard_map/ppermute | solution.py:344
  26.4 2.3 %collective-permute-start.8 = (bf16[656,128]{1,0:T(8,128)(2,1)S(1)}, bf16[656,128]{1,0:T(8,128)(2,1)S(1)}, u32[]{:S(2)}, u32[]{:S(2)}) collective-permute-start(bf16[656,128]{1,0:T(8,128)(2,1)S(1)} %collective-permute-done.3.refs_3_), channel_id=1, source_target_pairs={{0,32},{32,64},{64,96},{96,128},{128,160},{160,192},{192,224},{224... | collective-permute-start | bytes 503816 | tf_op jit(solution)/shard_map/ppermute | solution.py:344
  28.7 0.9 %collective-permute-start.9 = (bf16[656,128]{1,0:T(8,128)(2,1)S(1)}, bf16[656,128]{1,0:T(8,128)(2,1)S(1)}, u32[]{:S(2)}, u32[]{:S(2)}) collective-permute-start(bf16[656,128]{1,0:T(8,128)(2,1)S(1)} %collective-permute-done.4.refs_4_), channel_id=1, source_target_pairs={{0,224},{32,0},{64,32},{96,64},{128,96},{160,128},{192,160},{224,1... | collective-permute-start | bytes 503816 | tf_op jit(solution)/shard_map/ppermute | solution.py:344
  29.6 1.4 %collective-permute-start.11 = (bf16[336,128]{1,0:T(8,128)(2,1)S(1)}, bf16[336,128]{1,0:T(8,128)(2,1)S(1)}, u32[]{:S(2)}, u32[]{:S(2)}) collective-permute-start(bf16[336,128]{1,0:T(8,128)(2,1)S(1)} %slice.34), channel_id=1, source_target_pairs={{0,192},{32,224},{64,0},{96,32},{128,64},{160,96},{192,128},{224,1... | collective-permute-start | bytes 258056 | tf_op jit(solution)/shard_map/ppermute | solution.py:344
  31.0 1.0 %collective-permute-start.10 = (bf16[320,128]{1,0:T(8,128)(2,1)S(1)}, bf16[320,128]{1,0:T(8,128)(2,1)S(1)}, u32[]{:S(2)}, u32[]{:S(2)}) collective-permute-start(bf16[320,128]{1,0:T(8,128)(2,1)S(1)} %slice.33), channel_id=1, source_target_pairs={{0,64},{32,96},{64,128},{96,160},{128,192},{160,224},{192,0},{224,... | collective-permute-start | bytes 245768 | tf_op jit(solution)/shard_map/ppermute | solution.py:344
  32.0 4.7 %collective-permute-done.10.refs_7_ = bf16[320,128]{1,0:T(8,128)(2,1)S(1)} collective-permute-done((bf16[320,128]{1,0:T(8,128)(2,1)S(1)}, bf16[320,128]{1,0:T(8,128)(2,1)S(1)}, u32[]{:S(2)}, u32[]{:S(2)}) %collective-permute-start.10) | collective-permute-done | bytes 81952 | tf_op jit(solution)/shard_map/ppermute | solution.py:344
  36.7 5.4 %near_positions.1 = (bf16[768,576]{1,0:T(8,128)(2,1)S(1)}, f32[768,128]{1,0:T(8,128)S(1)}, f32[768,128]{1,0:T(8,128)S(1)}, f32[768,512]{1,0:T(8,128)S(1)}) custom-call(bf16[656,128]{1,0:T(8,128)(2,1)S(1)} %pad_maximum_fusion.1.refs_0_, bf16[656,128]{1,0:T(8,128)(2,1)S(1)} %collective-permute-done.5.refs_1_, ...), custom_call_target="tpu_custom_call" | custom-call | flops 3523215360 | bytes 8388608 | tf_op jit(solution)/shard_map/near_positions/pallas_call | solution.py:182
  42.1 7.0 %collective-permute-start.13 = (bf16[576,1024]{1,0:T(8,128)(2,1)S(1)}, bf16[576,1024]{1,0:T(8,128)(2,1)S(1)}, u32[]{:S(2)}, u32[]{:S(2)}) collective-permute-start(bf16[576,1024]{1,0:T(8,128)(2,1)S(1)} %collective-permute-done.12.low), channel_id=1, source_target_pairs={{0,8},{8,0},{16,24},{24,16},{1,9},{9,1},{17,25},{25,17},{2,10},{10... | collective-permute-start | bytes 3538952 | tf_op jit(solution)/shard_map/ppermute | solution.py:340
  49.1 3.2 %middle_positions.1 = (f32[768,128]{1,0:T(8,128)S(1)}, f32[768,128]{1,0:T(8,128)S(1)}, f32[768,512]{1,0:T(8,128)S(1)}) custom-call(s32[4,192,128]{2,1,0:T(8,128)S(1)} %copy-done, bf16[576,1024]{1,0:T(8,128)(2,1)S(1)} %collective-permute-done.12.low, bf16[768,576]{1,0:T(8,128)(2,1)S(1)} %get-tuple-element.42.probe.refs_11_, ...), custom_call_target="tpu_custom_call" | custom-call | flops 1711276032 | bytes 8388608 | tf_op jit(solution)/shard_map/middle_positions/pallas_call | solution.py:216
  52.3 3.4 %far_positions.1 = bf16[8,112,128]{2,1,0:T(8,128)(2,1)S(1)} custom-call(bf16[656,128]{1,0:T(8,128)(2,1)S(1)} %pad_maximum_fusion.1.refs_0_, bf16[656,128]{1,0:T(8,128)(2,1)S(1)} %collective-permute-done.5.refs_1_, bf16[656,128]{1,0:T(8,128)(2,1)S(1)} %collective-permute-done.6.refs_2_, bf16[656,128]{1,0:T(8,128)(2,1)S(1)} %collective-permute-done.3.refs_3_, ...), custom_call_target="tpu_custom_call" | custom-call | flops 1811939328 | bytes 8388608 | tf_op jit(solution)/shard_map/far_positions/pallas_call | solution.py:283
  55.7 16.9 %all_to_all.5.parts = bf16[8,112,128]{2,1,0:T(8,128)(2,1)} all-to-all(bf16[8,112,128]{2,1,0:T(8,128)(2,1)S(1)} %far_positions.1), channel_id=1, replica_groups=mesh['z'=8,'x'=2,'core'=2,'head'=8] {'z'}, dimensions={0} | all-to-all | bytes 458752 | tf_op jit(solution)/shard_map/all_to_all | solution.py:405
  72.6 1.9 %combine.1 = (bf16[32,128]{1,0:T(8,128)(2,1)}, bf16[32,128]{1,0:T(8,128)(2,1)}, bf16[32,128]{1,0:T(8,128)(2,1)}, bf16[32,128]{1,0:T(8,128)(2,1)}) custom-call(bf16[8,112,128]{2,1,0:T(8,128)(2,1)} %all_to_all.5.parts), custom_call_target="tpu_custom_call" | custom-call | tf_op jit(solution)/shard_map/combine/pallas_call | solution.py:330
  74.5 1.9 %collective-permute-start.15 = (bf16[32,128]{1,0:T(8,128)(2,1)}, bf16[32,128]{1,0:T(8,128)(2,1)S(1)}, u32[]{:S(2)}, u32[]{:S(2)}) collective-permute-start(bf16[32,128]{1,0:T(8,128)(2,1)} %get-tuple-element.50), channel_id=1, source_target_pairs={{0,16},{8,24},{16,0},{24,8},{1,17},{9,25},{17,1},{25,9},{2,18},{10... | collective-permute-start | bytes 24584 | tf_op jit(solution)/shard_map/ppermute | solution.py:340
  76.3 0.3 collective-permute-start.16
  76.6 1.3 %collective-permute-done.14 = bf16[32,128]{1,0:T(8,128)(2,1)S(1)} collective-permute-done((bf16[32,128]{1,0:T(8,128)(2,1)}, bf16[32,128]{1,0:T(8,128)(2,1)S(1)}, u32[]{:S(2)}, u32[]{:S(2)}) %collective-permute-start.14) | collective-permute-done | bytes 8224 | tf_op jit(solution)/shard_map/ppermute | solution.py:340
  77.9 0.7 select_bitcast_fusion.7
  78.6 0.6 copy.41
  (40 shorter events, 0.3 us)
Async XLA Ops:
  2.9 8.0 %collective-permute-start.2 = (bf16[164,128]{1,0:T(8,128)(2,1)S(1)}, bf16[164,128]{1,0:T(8,128)(2,1)S(1)}, u32[]{:S(2)}, u32[]{:S(2)}) collective-permute-start(bf16[164,128]{1,0:T(8,128)(2,1)S(1)} %get-tuple-element.59), channel_id=1, source_target_pairs={{0,8},{8,0},{16,24},{24,16},{1,9},{9,1},{17,25},{25,17},{2,10},{10... | collective-permute-start | bytes 125960 | tf_op jit(solution)/shard_map/ppermute | solution.py:340
  6.2 4.6 %collective-permute-start.1 = (bf16[164,128]{1,0:T(8,128)(2,1)S(1)}, bf16[164,128]{1,0:T(8,128)(2,1)S(1)}, u32[]{:S(2)}, u32[]{:S(2)}) collective-permute-start(bf16[164,128]{1,0:T(8,128)(2,1)S(1)} %get-tuple-element.60), channel_id=1, source_target_pairs={{0,16},{8,24},{16,0},{24,8},{1,17},{9,25},{17,1},{25,9},{2,18},{10... | collective-permute-start | bytes 125960 | tf_op jit(solution)/shard_map/ppermute | solution.py:340
  6.2 5.0 %copy-start.1 = (bf16[1024,576]{0,1:T(8,128)(2,1)S(1)}, bf16[1024,576]{0,1:T(8,128)(2,1)}, u32[]{:S(2)}) copy-start(bf16[1024,576]{0,1:T(8,128)(2,1)} %param.7) | copy-start | bytes 3538948
  6.2 4.6 %collective-permute-start = (bf16[164,128]{1,0:T(8,128)(2,1)S(1)}, bf16[164,128]{1,0:T(8,128)(2,1)S(1)}, u32[]{:S(2)}, u32[]{:S(2)}) collective-permute-start(bf16[164,128]{1,0:T(8,128)(2,1)S(1)} %get-tuple-element.61), channel_id=1, source_target_pairs={{0,24},{8,16},{16,8},{24,0},{1,25},{9,17},{17,9},{25,1},{2,26},{10... | collective-permute-start | bytes 125960 | tf_op jit(solution)/shard_map/ppermute | solution.py:340
  10.8 25.9 %copy-start = (s32[4,192,128]{2,1,0:T(8,128)S(1)}, s32[4,192,128]{2,1,0:T(8,128)}, u32[]{:S(2)}) copy-start(s32[4,192,128]{2,1,0:T(8,128)} %limits.1.refs_9_.lim) | copy-start | bytes 1179652
  11.2 15.3 %collective-permute-start.7 = (bf16[576,1024]{1,0:T(8,128)(2,1)S(1)}, bf16[576,1024]{1,0:T(8,128)(2,1)S(1)}, u32[]{:S(2)}, u32[]{:S(2)}) collective-permute-start(bf16[576,1024]{1,0:T(8,128)(2,1)S(1)} %bitcast.65), channel_id=1, source_target_pairs={{0,8},{8,0},{16,24},{24,16},{1,9},{9,1},{17,25},{25,17},{2,10},{10... | collective-permute-start | bytes 3538952 | tf_op jit(solution)/shard_map/ppermute | solution.py:340
  11.4 30.7 %collective-permute-start.12 = (bf16[576,1024]{1,0:T(8,128)(2,1)S(1)}, bf16[576,1024]{1,0:T(8,128)(2,1)S(1)}, u32[]{:S(2)}, u32[]{:S(2)}) collective-permute-start(bf16[576,1024]{1,0:T(8,128)(2,1)S(1)} %bitcast.66), channel_id=1, source_target_pairs={{0,16},{8,24},{16,0},{24,8},{1,17},{9,25},{17,1},{25,9},{2,18},{10... | collective-permute-start | bytes 3538952 | tf_op jit(solution)/shard_map/ppermute | solution.py:340
  12.0 7.4 %collective-permute-start.6 = (bf16[656,128]{1,0:T(8,128)(2,1)S(1)}, bf16[656,128]{1,0:T(8,128)(2,1)S(1)}, u32[]{:S(2)}, u32[]{:S(2)}) collective-permute-start(bf16[656,128]{1,0:T(8,128)(2,1)S(1)} %pad_maximum_fusion.1.refs_0_), channel_id=1, source_target_pairs={{0,224},{32,0},{64,32},{96,64},{128,96},{160,128},{192,160},{224,1... | collective-permute-start | bytes 503816 | tf_op jit(solution)/shard_map/ppermute | solution.py:344
  16.4 6.1 %collective-permute-start.5 = (bf16[656,128]{1,0:T(8,128)(2,1)S(1)}, bf16[656,128]{1,0:T(8,128)(2,1)S(1)}, u32[]{:S(2)}, u32[]{:S(2)}) collective-permute-start(bf16[656,128]{1,0:T(8,128)(2,1)S(1)} %pad_maximum_fusion.1.refs_0_), channel_id=1, source_target_pairs={{0,32},{32,64},{64,96},{96,128},{128,160},{160,192},{192,224},{224... | collective-permute-start | bytes 503816 | tf_op jit(solution)/shard_map/ppermute | solution.py:344
  16.4 10.0 %collective-permute-start.4 = (bf16[656,128]{1,0:T(8,128)(2,1)S(1)}, bf16[656,128]{1,0:T(8,128)(2,1)S(1)}, u32[]{:S(2)}, u32[]{:S(2)}) collective-permute-start(bf16[656,128]{1,0:T(8,128)(2,1)S(1)} %pad_maximum_fusion.1.refs_0_), channel_id=1, source_target_pairs={{0,192},{32,224},{64,0},{96,32},{128,64},{160,96},{192,128},{224,1... | collective-permute-start | bytes 503816 | tf_op jit(solution)/shard_map/ppermute | solution.py:344
  19.4 7.0 %collective-permute-start.3 = (bf16[656,128]{1,0:T(8,128)(2,1)S(1)}, bf16[656,128]{1,0:T(8,128)(2,1)S(1)}, u32[]{:S(2)}, u32[]{:S(2)}) collective-permute-start(bf16[656,128]{1,0:T(8,128)(2,1)S(1)} %pad_maximum_fusion.1.refs_0_), channel_id=1, source_target_pairs={{0,64},{32,96},{64,128},{96,160},{128,192},{160,224},{192,0},{224,... | collective-permute-start | bytes 503816 | tf_op jit(solution)/shard_map/ppermute | solution.py:344
  26.4 10.3 %collective-permute-start.8 = (bf16[656,128]{1,0:T(8,128)(2,1)S(1)}, bf16[656,128]{1,0:T(8,128)(2,1)S(1)}, u32[]{:S(2)}, u32[]{:S(2)}) collective-permute-start(bf16[656,128]{1,0:T(8,128)(2,1)S(1)} %collective-permute-done.3.refs_3_), channel_id=1, source_target_pairs={{0,32},{32,64},{64,96},{96,128},{128,160},{160,192},{192,224},{224... | collective-permute-start | bytes 503816 | tf_op jit(solution)/shard_map/ppermute | solution.py:344
  28.7 8.0 %collective-permute-start.9 = (bf16[656,128]{1,0:T(8,128)(2,1)S(1)}, bf16[656,128]{1,0:T(8,128)(2,1)S(1)}, u32[]{:S(2)}, u32[]{:S(2)}) collective-permute-start(bf16[656,128]{1,0:T(8,128)(2,1)S(1)} %collective-permute-done.4.refs_4_), channel_id=1, source_target_pairs={{0,224},{32,0},{64,32},{96,64},{128,96},{160,128},{192,160},{224,1... | collective-permute-start | bytes 503816 | tf_op jit(solution)/shard_map/ppermute | solution.py:344
  29.6 7.1 %collective-permute-start.11 = (bf16[336,128]{1,0:T(8,128)(2,1)S(1)}, bf16[336,128]{1,0:T(8,128)(2,1)S(1)}, u32[]{:S(2)}, u32[]{:S(2)}) collective-permute-start(bf16[336,128]{1,0:T(8,128)(2,1)S(1)} %slice.34), channel_id=1, source_target_pairs={{0,192},{32,224},{64,0},{96,32},{128,64},{160,96},{192,128},{224,1... | collective-permute-start | bytes 258056 | tf_op jit(solution)/shard_map/ppermute | solution.py:344
  31.0 5.6 %collective-permute-start.10 = (bf16[320,128]{1,0:T(8,128)(2,1)S(1)}, bf16[320,128]{1,0:T(8,128)(2,1)S(1)}, u32[]{:S(2)}, u32[]{:S(2)}) collective-permute-start(bf16[320,128]{1,0:T(8,128)(2,1)S(1)} %slice.33), channel_id=1, source_target_pairs={{0,64},{32,96},{64,128},{96,160},{128,192},{160,224},{192,0},{224,... | collective-permute-start | bytes 245768 | tf_op jit(solution)/shard_map/ppermute | solution.py:344
  42.1 10.2 %collective-permute-start.13 = (bf16[576,1024]{1,0:T(8,128)(2,1)S(1)}, bf16[576,1024]{1,0:T(8,128)(2,1)S(1)}, u32[]{:S(2)}, u32[]{:S(2)}) collective-permute-start(bf16[576,1024]{1,0:T(8,128)(2,1)S(1)} %collective-permute-done.12.low), channel_id=1, source_target_pairs={{0,8},{8,0},{16,24},{24,16},{1,9},{9,1},{17,25},{25,17},{2,10},{10... | collective-permute-start | bytes 3538952 | tf_op jit(solution)/shard_map/ppermute | solution.py:340
  74.5 3.4 %collective-permute-start.14 = (bf16[32,128]{1,0:T(8,128)(2,1)}, bf16[32,128]{1,0:T(8,128)(2,1)S(1)}, u32[]{:S(2)}, u32[]{:S(2)}) collective-permute-start(bf16[32,128]{1,0:T(8,128)(2,1)} %get-tuple-element.49), channel_id=1, source_target_pairs={{0,24},{8,16},{16,8},{24,0},{1,25},{9,17},{17,9},{25,1},{2,26},{10... | collective-permute-start | bytes 24584 | tf_op jit(solution)/shard_map/ppermute | solution.py:340
  74.5 3.4 %collective-permute-start.15 = (bf16[32,128]{1,0:T(8,128)(2,1)}, bf16[32,128]{1,0:T(8,128)(2,1)S(1)}, u32[]{:S(2)}, u32[]{:S(2)}) collective-permute-start(bf16[32,128]{1,0:T(8,128)(2,1)} %get-tuple-element.50), channel_id=1, source_target_pairs={{0,16},{8,24},{16,0},{24,8},{1,17},{9,25},{17,1},{25,9},{2,18},{10... | collective-permute-start | bytes 24584 | tf_op jit(solution)/shard_map/ppermute | solution.py:340
  76.3 1.5 %collective-permute-start.16 = (bf16[32,128]{1,0:T(8,128)(2,1)}, bf16[32,128]{1,0:T(8,128)(2,1)S(1)}, u32[]{:S(2)}, u32[]{:S(2)}) collective-permute-start(bf16[32,128]{1,0:T(8,128)(2,1)} %get-tuple-element.51), channel_id=1, source_target_pairs={{0,8},{8,0},{16,24},{24,16},{1,9},{9,1},{17,25},{25,17},{2,10},{10... | collective-permute-start | bytes 24584 | tf_op jit(solution)/shard_map/ppermute | solution.py:340

commit v3 on v2

--- a/solution.py
+++ b/solution.py
@@ -27,8 +27,8 @@
 NBLK = S_DEV // BLK
 
 QN0, QR0, UK0, UV0, PIECE = 0, 96, 144, 400, 656
-HALF = 320
 OFFSETS = (0, -1, 1, -2, 2, -3, 3, 4)
+EARLY = 5
 OUT_ROWS = 112
 
 NEG = -1e30
@@ -36,6 +36,7 @@
 LOG2E = 1.4426950408889634
 
 VMEM = pl.BlockSpec(memory_space=pltpu.VMEM)
+HBM = pl.BlockSpec(memory_space=pltpu.HBM)
 
 
 def dot(a, b, dims):
@@ -99,10 +100,13 @@
     )(selected.transpose(0, 2, 1), lengths.reshape(1, -1))
 
 
-def attend(parts, first, lim, probe, scores, top, total, latent):
+def attend(parts, first, lim, probe, scores, top, total, latent, copies=()):
     lane = iota((RT, BLK), 1)
     old = top[...]
     for i, part in enumerate(parts):
+        if i == len(parts) - 1:
+            for copy in copies:
+                copy.wait()
         whole = dot(probe[...], part[...], ((1,), (0,)))
         for h in range(HG):
             mine = slice(h * RT, (h + 1) * RT)
@@ -138,34 +142,113 @@
         latent[...] += dot(jnp.concatenate(weights, axis=0), part[0:C, :], ((1,), (1,)))
 
 
-def piece_rows(pieces, p, first, count):
-    if p < NZ - 1 or first + count <= HALF:
-        return pieces[p][first : first + count, :]
-    return pieces[p + 1][first - HALF : first - HALF + count, :]
+def prepare_kernel(queries, keys, values, *refs):
+    outs, (q, uk, uv, sems) = refs[:NQ], refs[NQ:]
+    copies = [
+        pltpu.make_async_copy(source, target, sems.at[i])
+        for i, (source, target) in enumerate(((queries, q), (keys, uk), (values, uv)))
+    ]
+    for copy in copies:
+        copy.start()
+    quad = my_quad()
+    row = iota((128, 96), 0)
+    rest = row & 31
+    head = (rest * 43) >> 8
+    source = (rest - head * 6) * 16 + (quad ^ (row >> 5)) * HG + head
+    source = jnp.where(rest < 24, source, -1)
+    pick = jnp.where(source == iota((128, 96), 1), 1.0, 0.0).astype(jnp.bfloat16)
+    row = iota((64, 96), 0)
+    rest = row & 15
+    pair = jnp.where(rest < 6, 0, 1)
+    source = (rest - pair * 6) * 16 + (quad ^ (row >> 4)) * HG + pair * 2
+    source = jnp.where(rest < 12, source, -1)
+    column = iota((64, 96), 1)
+    pick_even = jnp.where(source == column, 1.0, 0.0).astype(jnp.bfloat16)
+    pick_odd = jnp.where(source == column - 1, 1.0, 0.0).astype(jnp.bfloat16)
+    pick_odd = jnp.where(rest < 12, pick_odd, 0.0).astype(jnp.bfloat16)
+    row = iota((64, 64), 0)
+    source = (quad ^ (row >> 4)) * 16 + (row & 15)
+    pick_keys = jnp.where(source == iota((64, 64), 1), 1.0, 0.0).astype(jnp.bfloat16)
+    copies[0].wait()
+    table = q[...].reshape(96, DN + R)
+    plain = dot(pick, table[:, :DN], ((1,), (0,))).astype(jnp.bfloat16)
+    rope = table[:, DN:]
+    rope = jnp.concatenate(
+        [dot(pick_even, rope, ((1,), (0,))), dot(pick_odd, rope, ((1,), (0,)))], axis=1
+    ).astype(jnp.bfloat16)
+    copies[1].wait()
+    table = uk[...].astype(jnp.float32).reshape(64, C).astype(jnp.bfloat16)
+    table = dot(pick_keys, table, ((1,), (0,))).astype(jnp.bfloat16)
+    copies[2].wait()
+    for k in range(NQ):
+        for cc in range(4):
+            outs[k][cc * 16 : (cc + 1) * 16, :] = table[
+                k * 16 : (k + 1) * 16, cc * 128 : (cc + 1) * 128
+            ]
+        for h in range(HG):
+            outs[k][64 + h * 16 : 80 + h * 16, :] = uv[(quad ^ k) * HG + h]
+        outs[k][128:160, :] = plain[k * 32 : (k + 1) * 32]
+        outs[k][160:176, :] = rope[k * 16 : (k + 1) * 16]
+
+
+def prepare(queries, w_uk, w_uv):
+    return pl.pallas_call(
+        prepare_kernel,
+        out_shape=(jax.ShapeDtypeStruct((176, 128), jnp.bfloat16),) * NQ,
+        in_specs=[HBM] * 3,
+        out_specs=(VMEM,) * NQ,
+        scratch_shapes=[
+            pltpu.VMEM((STEPS * 2, 16, DN + R), jnp.bfloat16),
+            pltpu.VMEM((16, 4, C), jnp.bfloat16),
+            pltpu.VMEM((16, 16, DV), jnp.bfloat16),
+            pltpu.SemaphoreType.DMA((3,)),
+        ],
+        compiler_params=params(),
+        name="prepare",
+    )(queries.reshape(STEPS * 2, 16, DN + R), w_uk, w_uv)
+
+
+def settle_kernel(*refs):
+    arrived, mate_in, pieces, mate = refs[:EARLY], refs[EARLY], refs[EARLY + 1], refs[EARLY + 2]
+    for p in range(EARLY):
+        pieces[p] = arrived[p][...]
+    mate[...] = mate_in[...]
+
+
+def settle(arrived, mate):
+    return pl.pallas_call(
+        settle_kernel,
+        out_shape=(
+            jax.ShapeDtypeStruct((EARLY, PIECE, 128), jnp.bfloat16),
+            jax.ShapeDtypeStruct(mate.shape, mate.dtype),
+        ),
+        in_specs=[VMEM] * (EARLY + 1),
+        out_specs=(VMEM,) * 2,
+        compiler_params=params(),
+        name="settle",
+    )(*arrived, mate)
 
 
 def near_kernel(*refs):
-    pieces, (lim, own, mate), (probe, top, total, latent), (qn, qr, wuk, scores) = (
-        refs[:9],
-        refs[9:12],
-        refs[12:16],
-        refs[16:],
-    )
+    early, late, (lim, own, mate, low) = refs[0], refs[1:4], refs[4:8]
+    probe, top, total, latent, qn, qr, wuk, scores, other, sem = refs[8:]
+    copy = pltpu.make_async_copy(low, other, sem)
+    copy.start()
+    pieces = [early.at[p] for p in range(EARLY)] + list(late)
     for p, offset in enumerate(OFFSETS):
         z = (my_z() + offset) & (NZ - 1)
         here = pl.ds(pl.multiple_of(z * RZ, RZ), RZ)
-        block = piece_rows(pieces, p, QN0, 96).astype(jnp.float32)
+        block = pieces[p][QN0 : QN0 + 96, :].astype(jnp.float32)
         for h in range(HG):
             qn[h, here, :] = block[h * RZ : (h + 1) * RZ]
-        block = piece_rows(pieces, p, QR0, 48).astype(jnp.float32)
+        block = pieces[p][QR0 : QR0 + 48, :].astype(jnp.float32)
         for j in range(HG // 2):
             qr[j, here, :] = block[j * RZ : (j + 1) * RZ]
         here = pl.ds(pl.multiple_of(z * 16, 16), 16)
         for h in range(HG):
             for cc in range(4):
-                wuk[h, here, cc * 128 : (cc + 1) * 128] = piece_rows(
-                    pieces, p, UK0 + (h * 4 + cc) * 16, 16
-                )
+                first = UK0 + (cc * HG + h) * 16
+                wuk[h, here, cc * 128 : (cc + 1) * 128] = pieces[p][first : first + 16, :]
     for h in range(HG):
         mine = slice(h * RT, (h + 1) * RT)
         absorbed = dot(qn[h].astype(jnp.bfloat16), wuk[h], ((1,), (0,)))
@@ -175,10 +258,10 @@
     top[...] = jnp.full(top.shape, NEG, jnp.float32)
     total[...] = jnp.zeros(total.shape, jnp.float32)
     latent[...] = jnp.zeros(latent.shape, jnp.float32)
-    attend((own, mate), 0, lim, probe, scores, top, total, latent)
-
-
-def near_positions(pieces, lim, own, mate):
+    attend((own, mate, other), 0, lim, probe, scores, top, total, latent, (copy,))
+
+
+def near_positions(pieces, lim, own, mate, low):
     return pl.pallas_call(
         near_kernel,
         out_shape=(
@@ -187,65 +270,35 @@
             jax.ShapeDtypeStruct((RH, 128), jnp.float32),
             jax.ShapeDtypeStruct((RH, C), jnp.float32),
         ),
-        in_specs=[VMEM] * 12,
+        in_specs=[VMEM] * 7 + [HBM],
         out_specs=(VMEM,) * 4,
         scratch_shapes=[
             pltpu.VMEM((HG, RT, DN), jnp.float32),
             pltpu.VMEM((HG // 2, RT, 2 * R), jnp.float32),
             pltpu.VMEM((HG, DN, C), jnp.bfloat16),
-            pltpu.VMEM((2, RH, S_DEV), jnp.float32),
+            pltpu.VMEM((3, RH, S_DEV), jnp.float32),
+            pltpu.VMEM((C + R, S_DEV), jnp.bfloat16),
+            pltpu.SemaphoreType.DMA(()),
         ],
         compiler_params=params(),
         cost_estimate=pl.CostEstimate(
-            flops=2 * RH * (2 * S_DEV * (2 * C + R) + DN * C),
+            flops=2 * RH * (3 * S_DEV * (2 * C + R) + DN * C),
             bytes_accessed=8 * 1024 * 1024,
-            transcendentals=RH * 2 * S_DEV,
+            transcendentals=RH * 3 * S_DEV,
         ),
         name="near_positions",
-    )(*pieces, lim, own, mate)
-
-
-def middle_kernel(lim, low, probe, top_in, total_in, latent_in, top, total, latent, scores):
-    top[...] = top_in[...]
-    total[...] = total_in[...]
-    latent[...] = latent_in[...]
-    attend((low,), 2, lim, probe, scores, top, total, latent)
-
-
-def middle_positions(lim, low, state):
-    return pl.pallas_call(
-        middle_kernel,
-        out_shape=(
-            jax.ShapeDtypeStruct((RH, 128), jnp.float32),
-            jax.ShapeDtypeStruct((RH, 128), jnp.float32),
-            jax.ShapeDtypeStruct((RH, C), jnp.float32),
-        ),
-        in_specs=[VMEM] * 6,
-        out_specs=(VMEM,) * 3,
-        scratch_shapes=[pltpu.VMEM((1, RH, S_DEV), jnp.float32)],
-        compiler_params=params(),
-        cost_estimate=pl.CostEstimate(
-            flops=2 * RH * S_DEV * (2 * C + R),
-            bytes_accessed=8 * 1024 * 1024,
-            transcendentals=RH * S_DEV,
-        ),
-        name="middle_positions",
-    )(lim, low, *state)
+    )(*pieces, lim, own, mate, low)
 
 
 def far_kernel(*refs):
-    pieces, (lim, high, probe, top_in, total_in, latent_in), out, (
-        wuv,
-        scores,
-        top,
-        total,
-        latent,
-    ) = refs[:9], refs[9:15], refs[15], refs[16:]
+    early, late, (lim, high, probe, top_in, total_in, latent_in) = refs[0], refs[1:4], refs[4:10]
+    out, wuv, scores, top, total, latent = refs[10:]
+    pieces = [early.at[p] for p in range(EARLY)] + list(late)
     for p, offset in enumerate(OFFSETS):
         z = (my_z() + offset) & (NZ - 1)
         here = pl.ds(pl.multiple_of(z * 64, 64), 64)
         for h in range(HG):
-            wuv[h, here, :] = piece_rows(pieces, p, UV0 + h * 64, 64)
+            wuv[h, here, :] = pieces[p][UV0 + h * 64 : UV0 + (h + 1) * 64, :]
     top[...] = top_in[...]
     total[...] = total_in[...]
     latent[...] = latent_in[...]
@@ -283,7 +336,7 @@
     return pl.pallas_call(
         far_kernel,
         out_shape=jax.ShapeDtypeStruct((NZ, OUT_ROWS, 128), jnp.bfloat16),
-        in_specs=[VMEM] * 15,
+        in_specs=[VMEM] * 10,
         out_specs=VMEM,
         scratch_shapes=[
             pltpu.VMEM((HG, C, DV), jnp.bfloat16),
@@ -344,6 +397,14 @@
     return lax.ppermute(x, "z", [(i, (i + k) % NZ) for i in range(NZ)])
 
 
+def opposite(up2, down2):
+    core = lax.axis_index("core")
+    pairs = [
+        (2 * i + c, 2 * ((i + (2 if c == 0 else -2)) % NZ) + c) for i in range(NZ) for c in range(2)
+    ]
+    return lax.ppermute(jnp.where(core == 0, up2, down2), ("z", "core"), pairs)
+
+
 def by_sender(got):
     quad = my_quad()
     odd, upper = quad % 2 == 1, quad >= 2
@@ -362,46 +423,32 @@
     ]
 
 
-def quad_exchange(parts):
-    quad = my_quad()
-    got = [lax.dynamic_index_in_dim(parts, quad, 0, keepdims=False)]
-    for k in range(1, NQ):
-        got.append(quad_swap(lax.dynamic_index_in_dim(parts, quad ^ k, 0, keepdims=False), k))
-    return jnp.stack(by_sender(got))
-
-
 def body(queries, cache, w_uk, w_uv, selected, lengths):
-    q = queries.reshape(STEPS, 2, NQ, HG, DN + R)
-    qn = q[..., :DN].transpose(2, 3, 0, 1, 4).reshape(NQ, 24, 128)
-    qr = q[..., DN:].reshape(STEPS, 2, NQ, 2, 2, R).transpose(2, 3, 0, 1, 4, 5).reshape(NQ, 12, 128)
-    uk = w_uk.reshape(NQ, HG, 4, 4, 128).transpose(0, 1, 3, 2, 4).reshape(NQ, 64, 128)
-    uv = w_uv.reshape(NQ, 64, 128)
-    got = quad_exchange(jnp.concatenate([qn, qr, uk, uv], axis=1))
+    sent = prepare(queries, w_uk, w_uv)
+    got = jnp.stack(by_sender([sent[0]] + [quad_swap(sent[k], k) for k in range(1, NQ)]))
     piece = jnp.concatenate(
         [
-            got[:, 0:24].reshape(NQ, HG, 6, 128).transpose(1, 0, 2, 3).reshape(96, 128),
-            got[:, 24:36].reshape(NQ, 2, 6, 128).transpose(1, 0, 2, 3).reshape(48, 128),
-            got[:, 36:100].reshape(NQ, 16, 4, 128).transpose(1, 0, 2, 3).reshape(256, 128),
-            got[:, 100:164].reshape(NQ, HG, 16, 128).transpose(1, 0, 2, 3).reshape(256, 128),
+            got[:, 128:152].reshape(NQ, HG, 6, 128).transpose(1, 0, 2, 3).reshape(96, 128),
+            got[:, 160:172].reshape(NQ, 2, 6, 128).transpose(1, 0, 2, 3).reshape(48, 128),
+            got[:, 0:64].reshape(NQ, 16, 4, 128).transpose(1, 0, 2, 3).reshape(256, 128),
+            got[:, 64:128].reshape(NQ, HG, 16, 128).transpose(1, 0, 2, 3).reshape(256, 128),
         ],
         axis=0,
     )
     lim = visible_limits(selected, lengths)
     piece, lim, cache = lax.optimization_barrier((piece, lim, cache.T))
-
+    low, mate = quad_swap(cache, 2), quad_swap(cache, 1)
+    up1, down1 = z_shift(piece, 1), z_shift(piece, -1)
     up2, down2 = z_shift(piece, 2), z_shift(piece, -2)
-    up1, down1 = z_shift(piece, 1), z_shift(piece, -1)
-    mate, low = quad_swap(cache, 1), quad_swap(cache, 2)
-    up2, down2, up1, down1, mate = lax.optimization_barrier((up2, down2, up1, down1, mate))
-    up4, down4 = z_shift(up2[:HALF], 2), z_shift(down2[HALF:], -2)
+    mate, up1, down1, up2, down2 = lax.optimization_barrier((mate, up1, down1, up2, down2))
     up3, down3 = z_shift(up2, 1), z_shift(down2, -1)
-    pieces = [piece, up1, down1, up2, down2, up3, down3, up4, down4]
-
-    probe, *state = near_positions(pieces, lim, cache, mate)
-    low, probe, *state = lax.optimization_barrier((low, probe, *state))
+    late = [up3, down3, opposite(up2, down2)]
+    early, mate = settle([piece, up1, down1, up2, down2], mate)
+
+    low, late = lax.optimization_barrier((low, late))
     high = quad_swap(low, 1)
-    state = middle_positions(lim, low, (probe, *state))
-    parts = far_positions(pieces, lim, high, (probe, *state))
+    probe, *state = near_positions([early] + late, lim, cache, mate, low)
+    parts = far_positions([early] + late, lim, high, (probe, *state))
     parts = lax.all_to_all(parts, "z", 0, 0, tiled=True)
     mine = combine(parts)
     got = [mine[0]] + [quad_swap(mine[k], k) for k in range(1, NQ)]

time: 79.6 us -> 78.3 us (0.984)
  starting transfers between devices: 26.9 us -> 20.1 us
  waiting for transfers between devices: 14 us -> 19.9 us
  other arithmetic: 1.72 us -> 0.8 us
    ppermute x9, waiting for transfers between devices: 1.28 us -> 9.33 us  [quad_swap(): return lax.ppermute(x, ('x', 'core'), [(i, i ^ k) for i in range(NQ)])]
    ppermute x9, starting transfers between devices: 15 us -> 10.5 us  [quad_swap(): return lax.ppermute(x, ('x', 'core'), [(i, i ^ k) for i in range(NQ)])]
    pallas_call x1, Pallas kernels: 5.37 us -> 8.44 us  [near_positions(): pl.pallas_call(near_kernel, out_shape=(jax.ShapeDtypeStruct((RH, C + R),...]
    ppermute x8 -> x6, starting transfers between devices: 11.9 us -> 9.03 us  [z_shift(): return lax.ppermute(x, 'z', [(i, (i + k) % NZ) for i in range(NZ)])]
    unnamed x4 -> x10, local copies, waits for them, and re-layouts: 0.01 us -> 2.48 us
    pallas_call x1 -> x2, Pallas kernels: 3.18 us -> 0.8 us  [the longest x1 0.67 us: prepare(): pl.pallas_call(prepare_kernel, out_shape=(jax.ShapeDtypeStruct((176, 128)...]
    ppermute x8 -> x6, waiting for transfers between devices: 12.8 us -> 10.6 us  [z_shift(): return lax.ppermute(x, 'z', [(i, (i + k) % NZ) for i in range(NZ)])]
    reshape x6 -> x4, local copies, waits for them, and re-layouts: 1.83 us -> 0.06 us  [the longest x1 0.03 us: body(): got[:, 0:64].reshape(NQ, 16, 4, 128).transpose(1, 0, 2, 3).reshape(256, 128)]
  transfers between devices with their start and end apart: 17 -> 16, of which waited for: 5 -> 6; matrix products, arithmetic and copies ran while one was open for 0% -> 0% of each run, Pallas kernels for 14% -> 15%
where the time goes in v3:
time: 78.3 us; the launch traced here: 78 us
  starting transfers between devices  20.1 us (26%)
  waiting for transfers between devices  19.9 us (25%)
  Pallas kernels  17.4 us (22%)
  blocking collectives  16.4 us (21%)
  local copies, waits for them, and re-layouts  3.19 us (4%)
  other arithmetic  0.8 us (1%)
    all_to_all x1, blocking collectives, body(): parts = lax.all_to_all(parts, 'z', 0, 0, tiled=True)  16.4 us
    ppermute x6, waiting for transfers between devices, z_shift(): return lax.ppermute(x, 'z', [(i, (i + k) % NZ) for i in range(NZ)])  10.6 us
    ppermute x9, starting transfers between devices, quad_swap(): return lax.ppermute(x, ('x', 'core'), [(i, i ^ k) for i in range(NQ)])  10.5 us
    ppermute x9, waiting for transfers between devices, quad_swap(): return lax.ppermute(x, ('x', 'core'), [(i, i ^ k) for i in range(NQ)])  9.33 us
    ppermute x6, starting transfers between devices, z_shift(): return lax.ppermute(x, 'z', [(i, (i + k) % NZ) for i in range(NZ)])  9.03 us
    pallas_call x1, Pallas kernels, near_positions(): pl.pallas_call(near_kernel, out_shape=(jax.ShapeDtypeStruct((RH, C + R),...  8.44 us
    pallas_call x1, Pallas kernels, far_positions(): pl.pallas_call(far_kernel, out_shape=jax.ShapeDtypeStruct((NZ, OUT_ROWS,...  3.29 us
    pallas_call x1, Pallas kernels, visible_limits(): pl.pallas_call(limits_kernel, out_shape=jax.ShapeDtypeStruct((NQ, RT, 128...  3.01 us
  transfers between devices with their start and end apart: 16, of which 6 were waited for; matrix products, arithmetic and copies ran while one was open for 0% of the time, Pallas kernels for 15%

profile of v3, /device:TPU:1, one launch (start us, length us, event | category | flops | bytes accessed | tf_op | source)
XLA Modules:
  0.0 78.0 jit_solution(12957324387903916535)
XLA Ops:
  0.0 0.8 %copy-done.1 = bf16[16,4,512]{2,1,0:T(4,128)(2,1)S(1)} copy-done((bf16[16,4,512]{2,1,0:T(4,128)(2,1)S(1)}, bf16[16,4,512]{2,1,0:T(4,128)(2,1)}, u32[]{:S(2)}) %copy-start.1) | copy-done | bytes 65560
  0.8 0.8 %copy-done.2 = bf16[16,16,128]{2,1,0:T(8,128)(2,1)S(1)} copy-done((bf16[16,16,128]{2,1,0:T(8,128)(2,1)S(1)}, bf16[16,16,128]{2,1,0:T(8,128)(2,1)}, u32[]{:S(2)}) %copy-start.2) | copy-done | bytes 65560
  1.7 0.8 %copy-done.3 = bf16[3,2,16,192]{3,2,1,0:T(8,128)(2,1)S(1)} copy-done((bf16[3,2,16,192]{3,2,1,0:T(8,128)(2,1)S(1)}, bf16[3,2,16,192]{3,2,1,0:T(8,128)(2,1)}, u32[]{:S(2)}) %copy-start.3) | copy-done | bytes 36888
  2.5 0.7 prepare.1
  3.2 2.7 %collective-permute-start = (bf16[176,128]{1,0:T(8,128)(2,1)S(1)}, bf16[176,128]{1,0:T(8,128)(2,1)S(1)}, u32[]{:S(2)}, u32[]{:S(2)}) collective-permute-start(bf16[176,128]{1,0:T(8,128)(2,1)S(1)} %get-tuple-element.31), channel_id=1, source_target_pairs={{0,24},{8,16},{16,8},{24,0},{1,25},{9,17},{17,9},{25,1},{2,26},{10... | collective-permute-start | bytes 135176 | tf_op jit(solution)/shard_map/ppermute | solution.py:393
  5.8 2.0 %collective-permute-start.1 = (bf16[176,128]{1,0:T(8,128)(2,1)S(1)}, bf16[176,128]{1,0:T(8,128)(2,1)S(1)}, u32[]{:S(2)}, u32[]{:S(2)}) collective-permute-start(bf16[176,128]{1,0:T(8,128)(2,1)S(1)} %get-tuple-element.32), channel_id=1, source_target_pairs={{0,16},{8,24},{16,0},{24,8},{1,17},{9,25},{17,1},{25,9},{2,18},{10... | collective-permute-start | bytes 135176 | tf_op jit(solution)/shard_map/ppermute | solution.py:393
  7.8 3.0 %limits.1.refs_4_ = s32[4,192,128]{2,1,0:T(8,128)} custom-call(s32[3,16,64]{2,1,0:T(8,128)} %bitcast.49, s32[1,64]{1,0:T(1,128)} %bitcast.50), custom_call_target="tpu_custom_call" | custom-call | tf_op jit(solution)/shard_map/limits/pallas_call | solution.py:94
  11.1 0.6 collective-permute-start.3
  11.7 0.1 collective-permute-start.8
  11.8 1.1 %collective-permute-start.4 = (bf16[656,128]{1,0:T(8,128)(2,1)S(1)}, bf16[656,128]{1,0:T(8,128)(2,1)S(1)}, u32[]{:S(2)}, u32[]{:S(2)}) collective-permute-start(bf16[656,128]{1,0:T(8,128)(2,1)S(1)} %pad_maximum_fusion.refs_0_), channel_id=1, source_target_pairs={{0,32},{32,64},{64,96},{96,128},{128,160},{160,192},{192,224},{224... | collective-permute-start | bytes 503816 | tf_op jit(solution)/shard_map/ppermute | solution.py:397
  12.9 3.9 %collective-permute-start.5 = (bf16[656,128]{1,0:T(8,128)(2,1)S(1)}, bf16[656,128]{1,0:T(8,128)(2,1)S(1)}, u32[]{:S(2)}, u32[]{:S(2)}) collective-permute-start(bf16[656,128]{1,0:T(8,128)(2,1)S(1)} %pad_maximum_fusion.refs_0_), channel_id=1, source_target_pairs={{0,224},{32,0},{64,32},{96,64},{128,96},{160,128},{192,160},{224,1... | collective-permute-start | bytes 503816 | tf_op jit(solution)/shard_map/ppermute | solution.py:397
  16.8 4.4 %collective-permute-done.4.refs_1_ = bf16[656,128]{1,0:T(8,128)(2,1)S(1)} collective-permute-done((bf16[656,128]{1,0:T(8,128)(2,1)S(1)}, bf16[656,128]{1,0:T(8,128)(2,1)S(1)}, u32[]{:S(2)}, u32[]{:S(2)}) %collective-permute-start.4) | collective-permute-done | bytes 167968 | tf_op jit(solution)/shard_map/ppermute | solution.py:397
  21.2 1.7 %collective-permute-start.7 = (bf16[656,128]{1,0:T(8,128)(2,1)S(1)}, bf16[656,128]{1,0:T(8,128)(2,1)S(1)}, u32[]{:S(2)}, u32[]{:S(2)}) collective-permute-start(bf16[656,128]{1,0:T(8,128)(2,1)S(1)} %pad_maximum_fusion.refs_0_), channel_id=1, source_target_pairs={{0,192},{32,224},{64,0},{96,32},{128,64},{160,96},{192,128},{224,1... | collective-permute-start | bytes 503816 | tf_op jit(solution)/shard_map/ppermute | solution.py:397
  22.9 3.7 %collective-permute-done.6.refs_3_ = bf16[656,128]{1,0:T(8,128)(2,1)S(1)} collective-permute-done((bf16[656,128]{1,0:T(8,128)(2,1)S(1)}, bf16[656,128]{1,0:T(8,128)(2,1)S(1)}, u32[]{:S(2)}, u32[]{:S(2)}) %collective-permute-start.6) | collective-permute-done | bytes 167968 | tf_op jit(solution)/shard_map/ppermute | solution.py:397
  26.6 2.5 %collective-permute-done.7.refs_4_ = bf16[656,128]{1,0:T(8,128)(2,1)S(1)} collective-permute-done((bf16[656,128]{1,0:T(8,128)(2,1)S(1)}, bf16[656,128]{1,0:T(8,128)(2,1)S(1)}, u32[]{:S(2)}, u32[]{:S(2)}) %collective-permute-start.7) | collective-permute-done | bytes 167968 | tf_op jit(solution)/shard_map/ppermute | solution.py:397
  29.1 0.5 collective-permute-start.11
  29.6 1.2 %collective-permute-start.10 = (bf16[656,128]{1,0:T(8,128)(2,1)S(1)}, bf16[656,128]{1,0:T(8,128)(2,1)S(1)}, u32[]{:S(2)}, u32[]{:S(2)}) collective-permute-start(bf16[656,128]{1,0:T(8,128)(2,1)S(1)} %collective-permute-done.7.refs_4_), channel_id=1, source_target_pairs={{0,224},{32,0},{64,32},{96,64},{128,96},{160,128},{192,160},{224,1... | collective-permute-start | bytes 503816 | tf_op jit(solution)/shard_map/ppermute | solution.py:397
  30.9 1.1 %collective-permute-start.9 = (bf16[656,128]{1,0:T(8,128)(2,1)S(1)}, bf16[656,128]{1,0:T(8,128)(2,1)S(1)}, u32[]{:S(2)}, u32[]{:S(2)}) collective-permute-start(bf16[656,128]{1,0:T(8,128)(2,1)S(1)} %collective-permute-done.6.refs_3_), channel_id=1, source_target_pairs={{0,32},{32,64},{64,96},{96,128},{128,160},{160,192},{192,224},{224... | collective-permute-start | bytes 503816 | tf_op jit(solution)/shard_map/ppermute | solution.py:397
  32.0 7.4 %collective-permute-done.8.refs_7_ = bf16[576,1024]{1,0:T(8,128)(2,1)} collective-permute-done((bf16[576,1024]{1,0:T(8,128)(2,1)S(1)}, bf16[576,1024]{1,0:T(8,128)(2,1)}, u32[]{:S(2)}, u32[]{:S(2)}) %collective-permute-start.8) | collective-permute-done | bytes 1179680 | tf_op jit(solution)/shard_map/ppermute | solution.py:393
  39.4 3.0 %collective-permute-start.12 = (bf16[576,1024]{1,0:T(8,128)(2,1)}, bf16[576,1024]{1,0:T(8,128)(2,1)S(1)}, u32[]{:S(2)}, u32[]{:S(2)}) collective-permute-start(bf16[576,1024]{1,0:T(8,128)(2,1)} %collective-permute-done.8.refs_7_), channel_id=1, source_target_pairs={{0,8},{8,0},{16,24},{24,16},{1,9},{9,1},{17,25},{25,17},{2,10},{10... | collective-permute-start | bytes 3538952 | tf_op jit(solution)/shard_map/ppermute | solution.py:393
  42.4 0.1 settle.1
  42.5 8.4 %near_positions.1 = (bf16[768,576]{1,0:T(8,128)(2,1)S(1)}, f32[768,128]{1,0:T(8,128)S(1)}, f32[768,128]{1,0:T(8,128)S(1)}, f32[768,512]{1,0:T(8,128)S(1)}) custom-call(bf16[5,656,128]{2,1,0:T(8,128)(2,1)S(1)} %get-tuple-element.42.refs_0_, bf16[656,128]{1,0:T(8,128)(2,1)S(1)} %collective-permute-done.9.refs_1_, ...), custom_call_target="tpu_custom_call" | custom-call | flops 5234491392 | bytes 8388608 | tf_op jit(solution)/shard_map/near_positions/pallas_call | solution.py:265
  51.0 3.3 %far_positions.1 = bf16[8,112,128]{2,1,0:T(8,128)(2,1)S(1)} custom-call(bf16[5,656,128]{2,1,0:T(8,128)(2,1)S(1)} %get-tuple-element.42.refs_0_, bf16[656,128]{1,0:T(8,128)(2,1)S(1)} %collective-permute-done.9.refs_1_, bf16[656,128]{1,0:T(8,128)(2,1)S(1)} %collective-permute-done.10.refs_2_, bf16[656,128]{1,0:T(8,128)(2,1)S(1)} %collective-permute-done.11.refs_3_, ...), custom_call_target="tpu_custom_call" | custom-call | flops 1811939328 | bytes 8388608 | tf_op jit(solution)/shard_map/far_positions/pallas_call | solution.py:336
  54.3 16.4 %all_to_all.5.parts = bf16[8,112,128]{2,1,0:T(8,128)(2,1)} all-to-all(bf16[8,112,128]{2,1,0:T(8,128)(2,1)S(1)} %far_positions.1), channel_id=1, replica_groups=mesh['z'=8,'x'=2,'core'=2,'head'=8] {'z'}, dimensions={0} | all-to-all | bytes 458752 | tf_op jit(solution)/shard_map/all_to_all | solution.py:452
  70.7 1.9 %combine.1 = (bf16[32,128]{1,0:T(8,128)(2,1)}, bf16[32,128]{1,0:T(8,128)(2,1)}, bf16[32,128]{1,0:T(8,128)(2,1)}, bf16[32,128]{1,0:T(8,128)(2,1)}) custom-call(bf16[8,112,128]{2,1,0:T(8,128)(2,1)} %all_to_all.5.parts), custom_call_target="tpu_custom_call" | custom-call | tf_op jit(solution)/shard_map/combine/pallas_call | solution.py:383
  72.6 1.3 %collective-permute-start.13 = (bf16[32,128]{1,0:T(8,128)(2,1)}, bf16[32,128]{1,0:T(8,128)(2,1)S(1)}, u32[]{:S(2)}, u32[]{:S(2)}) collective-permute-start(bf16[32,128]{1,0:T(8,128)(2,1)} %get-tuple-element.53), channel_id=1, source_target_pairs={{0,24},{8,16},{16,8},{24,0},{1,25},{9,17},{17,9},{25,1},{2,26},{10... | collective-permute-start | bytes 24584 | tf_op jit(solution)/shard_map/ppermute | solution.py:393
  73.9 0.5 collective-permute-start.14
  74.4 0.3 collective-permute-start.15
  74.7 1.3 %collective-permute-done.13 = bf16[32,128]{1,0:T(8,128)(2,1)S(1)} collective-permute-done((bf16[32,128]{1,0:T(8,128)(2,1)}, bf16[32,128]{1,0:T(8,128)(2,1)S(1)}, u32[]{:S(2)}, u32[]{:S(2)}) %collective-permute-start.13) | collective-permute-done | bytes 8224 | tf_op jit(solution)/shard_map/ppermute | solution.py:393
  76.0 0.7 collective-permute-done.14
  76.6 0.7 select_bitcast_fusion.7
  77.3 0.6 copy.18
  (34 shorter events, 0.2 us)
Async XLA Ops:
  0.0 0.8 %copy-start.1 = (bf16[16,4,512]{2,1,0:T(4,128)(2,1)S(1)}, bf16[16,4,512]{2,1,0:T(4,128)(2,1)}, u32[]{:S(2)}) copy-start(bf16[16,4,512]{2,1,0:T(4,128)(2,1)} %keys.1) | copy-start | bytes 196612
  0.8 0.8 %copy-start.2 = (bf16[16,16,128]{2,1,0:T(8,128)(2,1)S(1)}, bf16[16,16,128]{2,1,0:T(8,128)(2,1)}, u32[]{:S(2)}) copy-start(bf16[16,16,128]{2,1,0:T(8,128)(2,1)} %values.1) | copy-start | bytes 196612
  1.7 0.8 %copy-start.3 = (bf16[3,2,16,192]{3,2,1,0:T(8,128)(2,1)S(1)}, bf16[3,2,16,192]{3,2,1,0:T(8,128)(2,1)}, u32[]{:S(2)}) copy-start(bf16[3,2,16,192]{3,2,1,0:T(8,128)(2,1)} %param.6) | copy-start | bytes 110596
  3.2 7.7 %collective-permute-start = (bf16[176,128]{1,0:T(8,128)(2,1)S(1)}, bf16[176,128]{1,0:T(8,128)(2,1)S(1)}, u32[]{:S(2)}, u32[]{:S(2)}) collective-permute-start(bf16[176,128]{1,0:T(8,128)(2,1)S(1)} %get-tuple-element.31), channel_id=1, source_target_pairs={{0,24},{8,16},{16,8},{24,0},{1,25},{9,17},{17,9},{25,1},{2,26},{10... | collective-permute-start | bytes 135176 | tf_op jit(solution)/shard_map/ppermute | solution.py:393
  5.8 5.0 %collective-permute-start.1 = (bf16[176,128]{1,0:T(8,128)(2,1)S(1)}, bf16[176,128]{1,0:T(8,128)(2,1)S(1)}, u32[]{:S(2)}, u32[]{:S(2)}) collective-permute-start(bf16[176,128]{1,0:T(8,128)(2,1)S(1)} %get-tuple-element.32), channel_id=1, source_target_pairs={{0,16},{8,24},{16,0},{24,8},{1,17},{9,25},{17,1},{25,9},{2,18},{10... | collective-permute-start | bytes 135176 | tf_op jit(solution)/shard_map/ppermute | solution.py:393
  7.8 3.0 %collective-permute-start.2 = (bf16[176,128]{1,0:T(8,128)(2,1)S(1)}, bf16[176,128]{1,0:T(8,128)(2,1)S(1)}, u32[]{:S(2)}, u32[]{:S(2)}) collective-permute-start(bf16[176,128]{1,0:T(8,128)(2,1)S(1)} %get-tuple-element.33), channel_id=1, source_target_pairs={{0,8},{8,0},{16,24},{24,16},{1,9},{9,1},{17,25},{25,17},{2,10},{10... | collective-permute-start | bytes 135176 | tf_op jit(solution)/shard_map/ppermute | solution.py:393
  7.8 3.3 %copy-start.4 = (bf16[1024,576]{0,1:T(8,128)(2,1)S(1)}, bf16[1024,576]{0,1:T(8,128)(2,1)}, u32[]{:S(2)}) copy-start(bf16[1024,576]{0,1:T(8,128)(2,1)} %param.7) | copy-start | bytes 3538948
  11.1 18.0 %collective-permute-start.3 = (bf16[576,1024]{1,0:T(8,128)(2,1)S(1)}, bf16[576,1024]{1,0:T(8,128)(2,1)S(1)}, u32[]{:S(2)}, u32[]{:S(2)}) collective-permute-start(bf16[576,1024]{1,0:T(8,128)(2,1)S(1)} %bitcast.39), channel_id=1, source_target_pairs={{0,8},{8,0},{16,24},{24,16},{1,9},{9,1},{17,25},{25,17},{2,10},{10... | collective-permute-start | bytes 3538952 | tf_op jit(solution)/shard_map/ppermute | solution.py:393
  11.7 27.6 %collective-permute-start.8 = (bf16[576,1024]{1,0:T(8,128)(2,1)S(1)}, bf16[576,1024]{1,0:T(8,128)(2,1)}, u32[]{:S(2)}, u32[]{:S(2)}) collective-permute-start(bf16[576,1024]{1,0:T(8,128)(2,1)S(1)} %bitcast.40), channel_id=1, source_target_pairs={{0,16},{8,24},{16,0},{24,8},{1,17},{9,25},{17,1},{25,9},{2,18},{10... | collective-permute-start | bytes 3538952 | tf_op jit(solution)/shard_map/ppermute | solution.py:393
  11.8 9.4 %collective-permute-start.4 = (bf16[656,128]{1,0:T(8,128)(2,1)S(1)}, bf16[656,128]{1,0:T(8,128)(2,1)S(1)}, u32[]{:S(2)}, u32[]{:S(2)}) collective-permute-start(bf16[656,128]{1,0:T(8,128)(2,1)S(1)} %pad_maximum_fusion.refs_0_), channel_id=1, source_target_pairs={{0,32},{32,64},{64,96},{96,128},{128,160},{160,192},{192,224},{224... | collective-permute-start | bytes 503816 | tf_op jit(solution)/shard_map/ppermute | solution.py:397
  12.9 10.0 %collective-permute-start.5 = (bf16[656,128]{1,0:T(8,128)(2,1)S(1)}, bf16[656,128]{1,0:T(8,128)(2,1)S(1)}, u32[]{:S(2)}, u32[]{:S(2)}) collective-permute-start(bf16[656,128]{1,0:T(8,128)(2,1)S(1)} %pad_maximum_fusion.refs_0_), channel_id=1, source_target_pairs={{0,224},{32,0},{64,32},{96,64},{128,96},{160,128},{192,160},{224,1... | collective-permute-start | bytes 503816 | tf_op jit(solution)/shard_map/ppermute | solution.py:397
  16.8 9.8 %collective-permute-start.6 = (bf16[656,128]{1,0:T(8,128)(2,1)S(1)}, bf16[656,128]{1,0:T(8,128)(2,1)S(1)}, u32[]{:S(2)}, u32[]{:S(2)}) collective-permute-start(bf16[656,128]{1,0:T(8,128)(2,1)S(1)} %pad_maximum_fusion.refs_0_), channel_id=1, source_target_pairs={{0,64},{32,96},{64,128},{96,160},{128,192},{160,224},{192,0},{224,... | collective-permute-start | bytes 503816 | tf_op jit(solution)/shard_map/ppermute | solution.py:397
  21.2 7.9 %collective-permute-start.7 = (bf16[656,128]{1,0:T(8,128)(2,1)S(1)}, bf16[656,128]{1,0:T(8,128)(2,1)S(1)}, u32[]{:S(2)}, u32[]{:S(2)}) collective-permute-start(bf16[656,128]{1,0:T(8,128)(2,1)S(1)} %pad_maximum_fusion.refs_0_), channel_id=1, source_target_pairs={{0,192},{32,224},{64,0},{96,32},{128,64},{160,96},{192,128},{224,1... | collective-permute-start | bytes 503816 | tf_op jit(solution)/shard_map/ppermute | solution.py:397
  22.9 19.6 %copy-start = (s32[4,192,128]{2,1,0:T(8,128)S(1)}, s32[4,192,128]{2,1,0:T(8,128)}, u32[]{:S(2)}) copy-start(s32[4,192,128]{2,1,0:T(8,128)} %limits.1.refs_4_) | copy-start | bytes 1179652
  29.1 10.2 %collective-permute-start.11 = (bf16[656,128]{1,0:T(8,128)(2,1)S(1)}, bf16[656,128]{1,0:T(8,128)(2,1)S(1)}, u32[]{:S(2)}, u32[]{:S(2)}) collective-permute-start(bf16[656,128]{1,0:T(8,128)(2,1)S(1)} %broadcast_select_fusion), channel_id=1, source_target_pairs={{0,64},{8,200},{32,96},{40,232},{64,128},{72,8},{96,160},{104,40},... | collective-permute-start | bytes 503816 | tf_op jit(solution)/shard_map/ppermute | solution.py:405
  29.6 9.7 %collective-permute-start.10 = (bf16[656,128]{1,0:T(8,128)(2,1)S(1)}, bf16[656,128]{1,0:T(8,128)(2,1)S(1)}, u32[]{:S(2)}, u32[]{:S(2)}) collective-permute-start(bf16[656,128]{1,0:T(8,128)(2,1)S(1)} %collective-permute-done.7.refs_4_), channel_id=1, source_target_pairs={{0,224},{32,0},{64,32},{96,64},{128,96},{160,128},{192,160},{224,1... | collective-permute-start | bytes 503816 | tf_op jit(solution)/shard_map/ppermute | solution.py:397
  30.9 8.5 %collective-permute-start.9 = (bf16[656,128]{1,0:T(8,128)(2,1)S(1)}, bf16[656,128]{1,0:T(8,128)(2,1)S(1)}, u32[]{:S(2)}, u32[]{:S(2)}) collective-permute-start(bf16[656,128]{1,0:T(8,128)(2,1)S(1)} %collective-permute-done.6.refs_3_), channel_id=1, source_target_pairs={{0,32},{32,64},{64,96},{96,128},{128,160},{160,192},{192,224},{224... | collective-permute-start | bytes 503816 | tf_op jit(solution)/shard_map/ppermute | solution.py:397
  39.4 11.6 %collective-permute-start.12 = (bf16[576,1024]{1,0:T(8,128)(2,1)}, bf16[576,1024]{1,0:T(8,128)(2,1)S(1)}, u32[]{:S(2)}, u32[]{:S(2)}) collective-permute-start(bf16[576,1024]{1,0:T(8,128)(2,1)} %collective-permute-done.8.refs_7_), channel_id=1, source_target_pairs={{0,8},{8,0},{16,24},{24,16},{1,9},{9,1},{17,25},{25,17},{2,10},{10... | collective-permute-start | bytes 3538952 | tf_op jit(solution)/shard_map/ppermute | solution.py:393
  72.6 3.4 %collective-permute-start.13 = (bf16[32,128]{1,0:T(8,128)(2,1)}, bf16[32,128]{1,0:T(8,128)(2,1)S(1)}, u32[]{:S(2)}, u32[]{:S(2)}) collective-permute-start(bf16[32,128]{1,0:T(8,128)(2,1)} %get-tuple-element.53), channel_id=1, source_target_pairs={{0,24},{8,16},{16,8},{24,0},{1,25},{9,17},{17,9},{25,1},{2,26},{10... | collective-permute-start | bytes 24584 | tf_op jit(solution)/shard_map/ppermute | solution.py:393
  73.9 2.7 %collective-permute-start.14 = (bf16[32,128]{1,0:T(8,128)(2,1)}, bf16[32,128]{1,0:T(8,128)(2,1)S(1)}, u32[]{:S(2)}, u32[]{:S(2)}) collective-permute-start(bf16[32,128]{1,0:T(8,128)(2,1)} %get-tuple-element.54), channel_id=1, source_target_pairs={{0,16},{8,24},{16,0},{24,8},{1,17},{9,25},{17,1},{25,9},{2,18},{10... | collective-permute-start | bytes 24584 | tf_op jit(solution)/shard_map/ppermute | solution.py:393
  74.4 2.2 %collective-permute-start.15 = (bf16[32,128]{1,0:T(8,128)(2,1)}, bf16[32,128]{1,0:T(8,128)(2,1)S(1)}, u32[]{:S(2)}, u32[]{:S(2)}) collective-permute-start(bf16[32,128]{1,0:T(8,128)(2,1)} %get-tuple-element.55), channel_id=1, source_target_pairs={{0,8},{8,0},{16,24},{24,16},{1,9},{9,1},{17,25},{25,17},{2,10},{10... | collective-permute-start | bytes 24584 | tf_op jit(solution)/shard_map/ppermute | solution.py:393

commit v4 on v3

--- a/solution.py
+++ b/solution.py
@@ -47,8 +47,8 @@
     return lax.broadcasted_iota(jnp.int32, shape, dim)
 
 
-def params():
-    return pltpu.CompilerParams(vmem_limit_bytes=24 * 1024 * 1024)
+def params(mebibytes=24):
+    return pltpu.CompilerParams(vmem_limit_bytes=mebibytes * 1024 * 1024)
 
 
 def my_z():
@@ -203,7 +203,7 @@
             pltpu.VMEM((16, 16, DV), jnp.bfloat16),
             pltpu.SemaphoreType.DMA((3,)),
         ],
-        compiler_params=params(),
+        compiler_params=params(8),
         name="prepare",
     )(queries.reshape(STEPS * 2, 16, DN + R), w_uk, w_uv)
 
@@ -224,7 +224,7 @@
         ),
         in_specs=[VMEM] * (EARLY + 1),
         out_specs=(VMEM,) * 2,
-        compiler_params=params(),
+        compiler_params=params(8),
         name="settle",
     )(*arrived, mate)
 
@@ -385,6 +385,7 @@
         out_shape=(jax.ShapeDtypeStruct((32, 128), jnp.bfloat16),) * NQ,
         in_specs=[VMEM],
         out_specs=(VMEM,) * NQ,
+        compiler_params=params(8),
         name="combine",
     )(parts)
 

time: 78.3 us -> 75.7 us (0.967)
  Pallas kernels: 17.4 us -> 15.9 us
    pallas_call x1, Pallas kernels: 1.88 us -> 0.33 us  [combine(): pl.pallas_call(combine_kernel, out_shape=(jax.ShapeDtypeStruct((32, 128),...]
where the time goes in v4:
time: 75.7 us; the launch traced here: 75.4 us
  starting transfers between devices  20.1 us (27%)
  waiting for transfers between devices  19.7 us (26%)
  blocking collectives  16.3 us (22%)
  Pallas kernels  15.9 us (21%)
  local copies, waits for them, and re-layouts  3.19 us (4%)
    all_to_all x1, blocking collectives, body(): parts = lax.all_to_all(parts, 'z', 0, 0, tiled=True)  16.3 us
    ppermute x6, waiting for transfers between devices, z_shift(): return lax.ppermute(x, 'z', [(i, (i + k) % NZ) for i in range(NZ)])  10.6 us
    ppermute x9, starting transfers between devices, quad_swap(): return lax.ppermute(x, ('x', 'core'), [(i, i ^ k) for i in range(NQ)])  10.5 us
    ppermute x9, waiting for transfers between devices, quad_swap(): return lax.ppermute(x, ('x', 'core'), [(i, i ^ k) for i in range(NQ)])  9.14 us
    ppermute x6, starting transfers between devices, z_shift(): return lax.ppermute(x, 'z', [(i, (i + k) % NZ) for i in range(NZ)])  9.03 us
    pallas_call x1, Pallas kernels, near_positions(): pl.pallas_call(near_kernel, out_shape=(jax.ShapeDtypeStruct((RH, C + R),...  8.44 us
    pallas_call x1, Pallas kernels, far_positions(): pl.pallas_call(far_kernel, out_shape=jax.ShapeDtypeStruct((NZ, OUT_ROWS,...  3.33 us
    pallas_call x1, Pallas kernels, visible_limits(): pl.pallas_call(limits_kernel, out_shape=jax.ShapeDtypeStruct((NQ, RT, 128...  3.01 us
  transfers between devices with their start and end apart: 16, of which 6 were waited for; matrix products, arithmetic and copies ran while one was open for 0% of the time, Pallas kernels for 15%

profile of v4, /device:TPU:1, one launch (start us, length us, event | category | flops | bytes accessed | tf_op | source)
XLA Modules:
  0.0 75.4 jit_solution(16521215077420929862)
XLA Ops:
  0.0 0.8 %copy-done.1 = bf16[16,4,512]{2,1,0:T(4,128)(2,1)S(1)} copy-done((bf16[16,4,512]{2,1,0:T(4,128)(2,1)S(1)}, bf16[16,4,512]{2,1,0:T(4,128)(2,1)}, u32[]{:S(2)}) %copy-start.1) | copy-done | bytes 65560
  0.8 0.8 %copy-done.2 = bf16[16,16,128]{2,1,0:T(8,128)(2,1)S(1)} copy-done((bf16[16,16,128]{2,1,0:T(8,128)(2,1)S(1)}, bf16[16,16,128]{2,1,0:T(8,128)(2,1)}, u32[]{:S(2)}) %copy-start.2) | copy-done | bytes 65560
  1.7 0.8 %copy-done.3 = bf16[3,2,16,192]{3,2,1,0:T(8,128)(2,1)S(1)} copy-done((bf16[3,2,16,192]{3,2,1,0:T(8,128)(2,1)S(1)}, bf16[3,2,16,192]{3,2,1,0:T(8,128)(2,1)}, u32[]{:S(2)}) %copy-start.3) | copy-done | bytes 36888
  2.5 0.7 prepare.1
  3.2 2.7 %collective-permute-start = (bf16[176,128]{1,0:T(8,128)(2,1)S(1)}, bf16[176,128]{1,0:T(8,128)(2,1)S(1)}, u32[]{:S(2)}, u32[]{:S(2)}) collective-permute-start(bf16[176,128]{1,0:T(8,128)(2,1)S(1)} %get-tuple-element.31), channel_id=1, source_target_pairs={{0,24},{8,16},{16,8},{24,0},{1,25},{9,17},{17,9},{25,1},{2,26},{10... | collective-permute-start | bytes 135176 | tf_op jit(solution)/shard_map/ppermute | solution.py:394
  5.8 2.0 %collective-permute-start.1 = (bf16[176,128]{1,0:T(8,128)(2,1)S(1)}, bf16[176,128]{1,0:T(8,128)(2,1)S(1)}, u32[]{:S(2)}, u32[]{:S(2)}) collective-permute-start(bf16[176,128]{1,0:T(8,128)(2,1)S(1)} %get-tuple-element.32), channel_id=1, source_target_pairs={{0,16},{8,24},{16,0},{24,8},{1,17},{9,25},{17,1},{25,9},{2,18},{10... | collective-permute-start | bytes 135176 | tf_op jit(solution)/shard_map/ppermute | solution.py:394
  7.8 0.0 collective-permute-start.2
  7.8 3.0 %limits.1.refs_4_ = s32[4,192,128]{2,1,0:T(8,128)} custom-call(s32[3,16,64]{2,1,0:T(8,128)} %bitcast.49, s32[1,64]{1,0:T(1,128)} %bitcast.50), custom_call_target="tpu_custom_call" | custom-call | tf_op jit(solution)/shard_map/limits/pallas_call | solution.py:94
  11.1 0.6 collective-permute-start.3
  11.7 0.1 collective-permute-start.8
  11.8 1.1 %collective-permute-start.4 = (bf16[656,128]{1,0:T(8,128)(2,1)S(1)}, bf16[656,128]{1,0:T(8,128)(2,1)S(1)}, u32[]{:S(2)}, u32[]{:S(2)}) collective-permute-start(bf16[656,128]{1,0:T(8,128)(2,1)S(1)} %pad_maximum_fusion.refs_0_), channel_id=1, source_target_pairs={{0,32},{32,64},{64,96},{96,128},{128,160},{160,192},{192,224},{224... | collective-permute-start | bytes 503816 | tf_op jit(solution)/shard_map/ppermute | solution.py:398
  12.9 3.9 %collective-permute-start.5 = (bf16[656,128]{1,0:T(8,128)(2,1)S(1)}, bf16[656,128]{1,0:T(8,128)(2,1)S(1)}, u32[]{:S(2)}, u32[]{:S(2)}) collective-permute-start(bf16[656,128]{1,0:T(8,128)(2,1)S(1)} %pad_maximum_fusion.refs_0_), channel_id=1, source_target_pairs={{0,224},{32,0},{64,32},{96,64},{128,96},{160,128},{192,160},{224,1... | collective-permute-start | bytes 503816 | tf_op jit(solution)/shard_map/ppermute | solution.py:398
  16.8 4.4 %collective-permute-done.4.refs_1_ = bf16[656,128]{1,0:T(8,128)(2,1)S(1)} collective-permute-done((bf16[656,128]{1,0:T(8,128)(2,1)S(1)}, bf16[656,128]{1,0:T(8,128)(2,1)S(1)}, u32[]{:S(2)}, u32[]{:S(2)}) %collective-permute-start.4) | collective-permute-done | bytes 167968 | tf_op jit(solution)/shard_map/ppermute | solution.py:398
  21.2 1.7 %collective-permute-start.7 = (bf16[656,128]{1,0:T(8,128)(2,1)S(1)}, bf16[656,128]{1,0:T(8,128)(2,1)S(1)}, u32[]{:S(2)}, u32[]{:S(2)}) collective-permute-start(bf16[656,128]{1,0:T(8,128)(2,1)S(1)} %pad_maximum_fusion.refs_0_), channel_id=1, source_target_pairs={{0,192},{32,224},{64,0},{96,32},{128,64},{160,96},{192,128},{224,1... | collective-permute-start | bytes 503816 | tf_op jit(solution)/shard_map/ppermute | solution.py:398
  22.9 3.7 %collective-permute-done.6.refs_3_ = bf16[656,128]{1,0:T(8,128)(2,1)S(1)} collective-permute-done((bf16[656,128]{1,0:T(8,128)(2,1)S(1)}, bf16[656,128]{1,0:T(8,128)(2,1)S(1)}, u32[]{:S(2)}, u32[]{:S(2)}) %collective-permute-start.6) | collective-permute-done | bytes 167968 | tf_op jit(solution)/shard_map/ppermute | solution.py:398
  26.6 2.5 %collective-permute-done.7.refs_4_ = bf16[656,128]{1,0:T(8,128)(2,1)S(1)} collective-permute-done((bf16[656,128]{1,0:T(8,128)(2,1)S(1)}, bf16[656,128]{1,0:T(8,128)(2,1)S(1)}, u32[]{:S(2)}, u32[]{:S(2)}) %collective-permute-start.7) | collective-permute-done | bytes 167968 | tf_op jit(solution)/shard_map/ppermute | solution.py:398
  29.1 0.5 collective-permute-start.11
  29.6 1.2 %collective-permute-start.10 = (bf16[656,128]{1,0:T(8,128)(2,1)S(1)}, bf16[656,128]{1,0:T(8,128)(2,1)S(1)}, u32[]{:S(2)}, u32[]{:S(2)}) collective-permute-start(bf16[656,128]{1,0:T(8,128)(2,1)S(1)} %collective-permute-done.7.refs_4_), channel_id=1, source_target_pairs={{0,224},{32,0},{64,32},{96,64},{128,96},{160,128},{192,160},{224,1... | collective-permute-start | bytes 503816 | tf_op jit(solution)/shard_map/ppermute | solution.py:398
  30.9 1.1 %collective-permute-start.9 = (bf16[656,128]{1,0:T(8,128)(2,1)S(1)}, bf16[656,128]{1,0:T(8,128)(2,1)S(1)}, u32[]{:S(2)}, u32[]{:S(2)}) collective-permute-start(bf16[656,128]{1,0:T(8,128)(2,1)S(1)} %collective-permute-done.6.refs_3_), channel_id=1, source_target_pairs={{0,32},{32,64},{64,96},{96,128},{128,160},{160,192},{192,224},{224... | collective-permute-start | bytes 503816 | tf_op jit(solution)/shard_map/ppermute | solution.py:398
  32.0 7.4 %collective-permute-done.8.refs_7_ = bf16[576,1024]{1,0:T(8,128)(2,1)} collective-permute-done((bf16[576,1024]{1,0:T(8,128)(2,1)S(1)}, bf16[576,1024]{1,0:T(8,128)(2,1)}, u32[]{:S(2)}, u32[]{:S(2)}) %collective-permute-start.8) | collective-permute-done | bytes 1179680 | tf_op jit(solution)/shard_map/ppermute | solution.py:394
  39.4 3.0 %collective-permute-start.12 = (bf16[576,1024]{1,0:T(8,128)(2,1)}, bf16[576,1024]{1,0:T(8,128)(2,1)S(1)}, u32[]{:S(2)}, u32[]{:S(2)}) collective-permute-start(bf16[576,1024]{1,0:T(8,128)(2,1)} %collective-permute-done.8.refs_7_), channel_id=1, source_target_pairs={{0,8},{8,0},{16,24},{24,16},{1,9},{9,1},{17,25},{25,17},{2,10},{10... | collective-permute-start | bytes 3538952 | tf_op jit(solution)/shard_map/ppermute | solution.py:394
  42.4 0.1 settle.1
  42.5 8.4 %near_positions.1 = (bf16[768,576]{1,0:T(8,128)(2,1)S(1)}, f32[768,128]{1,0:T(8,128)S(1)}, f32[768,128]{1,0:T(8,128)S(1)}, f32[768,512]{1,0:T(8,128)S(1)}) custom-call(bf16[5,656,128]{2,1,0:T(8,128)(2,1)S(1)} %get-tuple-element.42.refs_0_, bf16[656,128]{1,0:T(8,128)(2,1)S(1)} %collective-permute-done.9.refs_1_, ...), custom_call_target="tpu_custom_call" | custom-call | flops 5234491392 | bytes 8388608 | tf_op jit(solution)/shard_map/near_positions/pallas_call | solution.py:265
  51.0 3.3 %far_positions.1 = bf16[8,112,128]{2,1,0:T(8,128)(2,1)S(1)} custom-call(bf16[5,656,128]{2,1,0:T(8,128)(2,1)S(1)} %get-tuple-element.42.refs_0_, bf16[656,128]{1,0:T(8,128)(2,1)S(1)} %collective-permute-done.9.refs_1_, bf16[656,128]{1,0:T(8,128)(2,1)S(1)} %collective-permute-done.10.refs_2_, bf16[656,128]{1,0:T(8,128)(2,1)S(1)} %collective-permute-done.11.refs_3_, ...), custom_call_target="tpu_custom_call" | custom-call | flops 1811939328 | bytes 8388608 | tf_op jit(solution)/shard_map/far_positions/pallas_call | solution.py:336
  54.3 16.3 %all_to_all.5.parts = bf16[8,112,128]{2,1,0:T(8,128)(2,1)S(1)} all-to-all(bf16[8,112,128]{2,1,0:T(8,128)(2,1)S(1)} %far_positions.1), channel_id=1, replica_groups=mesh['z'=8,'x'=2,'core'=2,'head'=8] {'z'}, dimensions={0} | all-to-all | bytes 458752 | tf_op jit(solution)/shard_map/all_to_all | solution.py:453
  70.6 0.3 combine.1
  70.9 1.4 %collective-permute-start.13 = (bf16[32,128]{1,0:T(8,128)(2,1)S(1)}, bf16[32,128]{1,0:T(8,128)(2,1)S(1)}, u32[]{:S(2)}, u32[]{:S(2)}) collective-permute-start(bf16[32,128]{1,0:T(8,128)(2,1)S(1)} %get-tuple-element.53), channel_id=1, source_target_pairs={{0,24},{8,16},{16,8},{24,0},{1,25},{9,17},{17,9},{25,1},{2,26},{10... | collective-permute-start | bytes 24584 | tf_op jit(solution)/shard_map/ppermute | solution.py:394
  72.3 0.5 collective-permute-start.14
  72.8 0.3 collective-permute-start.15
  73.1 1.0 %collective-permute-done.13 = bf16[32,128]{1,0:T(8,128)(2,1)S(1)} collective-permute-done((bf16[32,128]{1,0:T(8,128)(2,1)S(1)}, bf16[32,128]{1,0:T(8,128)(2,1)S(1)}, u32[]{:S(2)}, u32[]{:S(2)}) %collective-permute-start.13) | collective-permute-done | bytes 8224 | tf_op jit(solution)/shard_map/ppermute | solution.py:394
  74.1 0.7 collective-permute-done.14
  74.8 0.6 copy.18
  (34 shorter events, 0.2 us)
Async XLA Ops:
  0.0 0.8 %copy-start.1 = (bf16[16,4,512]{2,1,0:T(4,128)(2,1)S(1)}, bf16[16,4,512]{2,1,0:T(4,128)(2,1)}, u32[]{:S(2)}) copy-start(bf16[16,4,512]{2,1,0:T(4,128)(2,1)} %keys.1) | copy-start | bytes 196612
  0.8 0.8 %copy-start.2 = (bf16[16,16,128]{2,1,0:T(8,128)(2,1)S(1)}, bf16[16,16,128]{2,1,0:T(8,128)(2,1)}, u32[]{:S(2)}) copy-start(bf16[16,16,128]{2,1,0:T(8,128)(2,1)} %values.1) | copy-start | bytes 196612
  1.7 0.8 %copy-start.3 = (bf16[3,2,16,192]{3,2,1,0:T(8,128)(2,1)S(1)}, bf16[3,2,16,192]{3,2,1,0:T(8,128)(2,1)}, u32[]{:S(2)}) copy-start(bf16[3,2,16,192]{3,2,1,0:T(8,128)(2,1)} %param.6) | copy-start | bytes 110596
  3.2 7.7 %collective-permute-start = (bf16[176,128]{1,0:T(8,128)(2,1)S(1)}, bf16[176,128]{1,0:T(8,128)(2,1)S(1)}, u32[]{:S(2)}, u32[]{:S(2)}) collective-permute-start(bf16[176,128]{1,0:T(8,128)(2,1)S(1)} %get-tuple-element.31), channel_id=1, source_target_pairs={{0,24},{8,16},{16,8},{24,0},{1,25},{9,17},{17,9},{25,1},{2,26},{10... | collective-permute-start | bytes 135176 | tf_op jit(solution)/shard_map/ppermute | solution.py:394
  5.8 5.0 %collective-permute-start.1 = (bf16[176,128]{1,0:T(8,128)(2,1)S(1)}, bf16[176,128]{1,0:T(8,128)(2,1)S(1)}, u32[]{:S(2)}, u32[]{:S(2)}) collective-permute-start(bf16[176,128]{1,0:T(8,128)(2,1)S(1)} %get-tuple-element.32), channel_id=1, source_target_pairs={{0,16},{8,24},{16,0},{24,8},{1,17},{9,25},{17,1},{25,9},{2,18},{10... | collective-permute-start | bytes 135176 | tf_op jit(solution)/shard_map/ppermute | solution.py:394
  7.8 3.0 %collective-permute-start.2 = (bf16[176,128]{1,0:T(8,128)(2,1)S(1)}, bf16[176,128]{1,0:T(8,128)(2,1)S(1)}, u32[]{:S(2)}, u32[]{:S(2)}) collective-permute-start(bf16[176,128]{1,0:T(8,128)(2,1)S(1)} %get-tuple-element.33), channel_id=1, source_target_pairs={{0,8},{8,0},{16,24},{24,16},{1,9},{9,1},{17,25},{25,17},{2,10},{10... | collective-permute-start | bytes 135176 | tf_op jit(solution)/shard_map/ppermute | solution.py:394
  7.8 3.3 %copy-start.4 = (bf16[1024,576]{0,1:T(8,128)(2,1)S(1)}, bf16[1024,576]{0,1:T(8,128)(2,1)}, u32[]{:S(2)}) copy-start(bf16[1024,576]{0,1:T(8,128)(2,1)} %param.7) | copy-start | bytes 3538948
  11.1 18.0 %collective-permute-start.3 = (bf16[576,1024]{1,0:T(8,128)(2,1)S(1)}, bf16[576,1024]{1,0:T(8,128)(2,1)S(1)}, u32[]{:S(2)}, u32[]{:S(2)}) collective-permute-start(bf16[576,1024]{1,0:T(8,128)(2,1)S(1)} %bitcast.39), channel_id=1, source_target_pairs={{0,8},{8,0},{16,24},{24,16},{1,9},{9,1},{17,25},{25,17},{2,10},{10... | collective-permute-start | bytes 3538952 | tf_op jit(solution)/shard_map/ppermute | solution.py:394
  11.7 27.6 %collective-permute-start.8 = (bf16[576,1024]{1,0:T(8,128)(2,1)S(1)}, bf16[576,1024]{1,0:T(8,128)(2,1)}, u32[]{:S(2)}, u32[]{:S(2)}) collective-permute-start(bf16[576,1024]{1,0:T(8,128)(2,1)S(1)} %bitcast.40), channel_id=1, source_target_pairs={{0,16},{8,24},{16,0},{24,8},{1,17},{9,25},{17,1},{25,9},{2,18},{10... | collective-permute-start | bytes 3538952 | tf_op jit(solution)/shard_map/ppermute | solution.py:394
  11.8 9.4 %collective-permute-start.4 = (bf16[656,128]{1,0:T(8,128)(2,1)S(1)}, bf16[656,128]{1,0:T(8,128)(2,1)S(1)}, u32[]{:S(2)}, u32[]{:S(2)}) collective-permute-start(bf16[656,128]{1,0:T(8,128)(2,1)S(1)} %pad_maximum_fusion.refs_0_), channel_id=1, source_target_pairs={{0,32},{32,64},{64,96},{96,128},{128,160},{160,192},{192,224},{224... | collective-permute-start | bytes 503816 | tf_op jit(solution)/shard_map/ppermute | solution.py:398
  12.9 10.0 %collective-permute-start.5 = (bf16[656,128]{1,0:T(8,128)(2,1)S(1)}, bf16[656,128]{1,0:T(8,128)(2,1)S(1)}, u32[]{:S(2)}, u32[]{:S(2)}) collective-permute-start(bf16[656,128]{1,0:T(8,128)(2,1)S(1)} %pad_maximum_fusion.refs_0_), channel_id=1, source_target_pairs={{0,224},{32,0},{64,32},{96,64},{128,96},{160,128},{192,160},{224,1... | collective-permute-start | bytes 503816 | tf_op jit(solution)/shard_map/ppermute | solution.py:398
  16.8 9.8 %collective-permute-start.6 = (bf16[656,128]{1,0:T(8,128)(2,1)S(1)}, bf16[656,128]{1,0:T(8,128)(2,1)S(1)}, u32[]{:S(2)}, u32[]{:S(2)}) collective-permute-start(bf16[656,128]{1,0:T(8,128)(2,1)S(1)} %pad_maximum_fusion.refs_0_), channel_id=1, source_target_pairs={{0,64},{32,96},{64,128},{96,160},{128,192},{160,224},{192,0},{224,... | collective-permute-start | bytes 503816 | tf_op jit(solution)/shard_map/ppermute | solution.py:398
  21.2 7.9 %collective-permute-start.7 = (bf16[656,128]{1,0:T(8,128)(2,1)S(1)}, bf16[656,128]{1,0:T(8,128)(2,1)S(1)}, u32[]{:S(2)}, u32[]{:S(2)}) collective-permute-start(bf16[656,128]{1,0:T(8,128)(2,1)S(1)} %pad_maximum_fusion.refs_0_), channel_id=1, source_target_pairs={{0,192},{32,224},{64,0},{96,32},{128,64},{160,96},{192,128},{224,1... | collective-permute-start | bytes 503816 | tf_op jit(solution)/shard_map/ppermute | solution.py:398
  22.9 19.6 %copy-start = (s32[4,192,128]{2,1,0:T(8,128)S(1)}, s32[4,192,128]{2,1,0:T(8,128)}, u32[]{:S(2)}) copy-start(s32[4,192,128]{2,1,0:T(8,128)} %limits.1.refs_4_) | copy-start | bytes 1179652
  29.1 10.2 %collective-permute-start.11 = (bf16[656,128]{1,0:T(8,128)(2,1)S(1)}, bf16[656,128]{1,0:T(8,128)(2,1)S(1)}, u32[]{:S(2)}, u32[]{:S(2)}) collective-permute-start(bf16[656,128]{1,0:T(8,128)(2,1)S(1)} %broadcast_select_fusion), channel_id=1, source_target_pairs={{0,64},{8,200},{32,96},{40,232},{64,128},{72,8},{96,160},{104,40},... | collective-permute-start | bytes 503816 | tf_op jit(solution)/shard_map/ppermute | solution.py:406
  29.6 9.7 %collective-permute-start.10 = (bf16[656,128]{1,0:T(8,128)(2,1)S(1)}, bf16[656,128]{1,0:T(8,128)(2,1)S(1)}, u32[]{:S(2)}, u32[]{:S(2)}) collective-permute-start(bf16[656,128]{1,0:T(8,128)(2,1)S(1)} %collective-permute-done.7.refs_4_), channel_id=1, source_target_pairs={{0,224},{32,0},{64,32},{96,64},{128,96},{160,128},{192,160},{224,1... | collective-permute-start | bytes 503816 | tf_op jit(solution)/shard_map/ppermute | solution.py:398
  30.9 8.5 %collective-permute-start.9 = (bf16[656,128]{1,0:T(8,128)(2,1)S(1)}, bf16[656,128]{1,0:T(8,128)(2,1)S(1)}, u32[]{:S(2)}, u32[]{:S(2)}) collective-permute-start(bf16[656,128]{1,0:T(8,128)(2,1)S(1)} %collective-permute-done.6.refs_3_), channel_id=1, source_target_pairs={{0,32},{32,64},{64,96},{96,128},{128,160},{160,192},{192,224},{224... | collective-permute-start | bytes 503816 | tf_op jit(solution)/shard_map/ppermute | solution.py:398
  39.4 11.6 %collective-permute-start.12 = (bf16[576,1024]{1,0:T(8,128)(2,1)}, bf16[576,1024]{1,0:T(8,128)(2,1)S(1)}, u32[]{:S(2)}, u32[]{:S(2)}) collective-permute-start(bf16[576,1024]{1,0:T(8,128)(2,1)} %collective-permute-done.8.refs_7_), channel_id=1, source_target_pairs={{0,8},{8,0},{16,24},{24,16},{1,9},{9,1},{17,25},{25,17},{2,10},{10... | collective-permute-start | bytes 3538952 | tf_op jit(solution)/shard_map/ppermute | solution.py:394
  70.9 3.2 %collective-permute-start.13 = (bf16[32,128]{1,0:T(8,128)(2,1)S(1)}, bf16[32,128]{1,0:T(8,128)(2,1)S(1)}, u32[]{:S(2)}, u32[]{:S(2)}) collective-permute-start(bf16[32,128]{1,0:T(8,128)(2,1)S(1)} %get-tuple-element.53), channel_id=1, source_target_pairs={{0,24},{8,16},{16,8},{24,0},{1,25},{9,17},{17,9},{25,1},{2,26},{10... | collective-permute-start | bytes 24584 | tf_op jit(solution)/shard_map/ppermute | solution.py:394
  72.3 2.5 %collective-permute-start.14 = (bf16[32,128]{1,0:T(8,128)(2,1)S(1)}, bf16[32,128]{1,0:T(8,128)(2,1)S(1)}, u32[]{:S(2)}, u32[]{:S(2)}) collective-permute-start(bf16[32,128]{1,0:T(8,128)(2,1)S(1)} %get-tuple-element.54), channel_id=1, source_target_pairs={{0,16},{8,24},{16,0},{24,8},{1,17},{9,25},{17,1},{25,9},{2,18},{10... | collective-permute-start | bytes 24584 | tf_op jit(solution)/shard_map/ppermute | solution.py:394
  72.8 2.0 %collective-permute-start.15 = (bf16[32,128]{1,0:T(8,128)(2,1)S(1)}, bf16[32,128]{1,0:T(8,128)(2,1)S(1)}, u32[]{:S(2)}, u32[]{:S(2)}) collective-permute-start(bf16[32,128]{1,0:T(8,128)(2,1)S(1)} %get-tuple-element.55), channel_id=1, source_target_pairs={{0,8},{8,0},{16,24},{24,16},{1,9},{9,1},{17,25},{25,17},{2,10},{10... | collective-permute-start | bytes 24584 | tf_op jit(solution)/shard_map/ppermute | solution.py:394

commit v5 on v4

--- a/solution.py
+++ b/solution.py
@@ -203,7 +203,7 @@
             pltpu.VMEM((16, 16, DV), jnp.bfloat16),
             pltpu.SemaphoreType.DMA((3,)),
         ],
-        compiler_params=params(8),
+        compiler_params=params(60),
         name="prepare",
     )(queries.reshape(STEPS * 2, 16, DN + R), w_uk, w_uv)
 
@@ -437,7 +437,7 @@
         axis=0,
     )
     lim = visible_limits(selected, lengths)
-    piece, lim, cache = lax.optimization_barrier((piece, lim, cache.T))
+    piece, cache = lax.optimization_barrier((piece, cache.T))
     low, mate = quad_swap(cache, 2), quad_swap(cache, 1)
     up1, down1 = z_shift(piece, 1), z_shift(piece, -1)
     up2, down2 = z_shift(piece, 2), z_shift(piece, -2)

time: 75.7 us -> 81.1 us (1.071)
  Pallas kernels: 15.9 us -> 18.4 us
  waiting for transfers between devices: 19.7 us -> 22 us
  local copies, waits for them, and re-layouts: 3.19 us -> 2.28 us
  starting transfers between devices: 20.1 us -> 21 us
    ppermute x9, waiting for transfers between devices: 9.14 us -> 11.4 us  [quad_swap(): return lax.ppermute(x, ('x', 'core'), [(i, i ^ k) for i in range(NQ)])]
    pallas_call x1, Pallas kernels: 0.67 us -> 1.98 us  [prepare(): pl.pallas_call(prepare_kernel, out_shape=(jax.ShapeDtypeStruct((176, 128)...]
    pallas_call x1, Pallas kernels: 3.33 us -> 4.59 us  [far_positions(): pl.pallas_call(far_kernel, out_shape=jax.ShapeDtypeStruct((NZ, OUT_ROWS,...]
    unnamed x10 -> x8, local copies, waits for them, and re-layouts: 2.48 us -> 1.57 us
  transfers between devices with their start and end apart: 16 -> 16, of which waited for: 6 -> 7; matrix products, arithmetic and copies ran while one was open for 0% -> 0% of each run, Pallas kernels for 15% -> 14%
where the time goes in v5:
time: 81.1 us; the launch traced here: 80.8 us
  waiting for transfers between devices  22 us (27%)
  starting transfers between devices  21 us (26%)
  Pallas kernels  18.4 us (23%)
  blocking collectives  16 us (20%)
  local copies, waits for them, and re-layouts  2.28 us (3%)
  other arithmetic  0.89 us (1%)
    all_to_all x1, blocking collectives, body(): parts = lax.all_to_all(parts, 'z', 0, 0, tiled=True)  16 us
    ppermute x9, waiting for transfers between devices, quad_swap(): return lax.ppermute(x, ('x', 'core'), [(i, i ^ k) for i in range(NQ)])  11.4 us
    ppermute x9, starting transfers between devices, quad_swap(): return lax.ppermute(x, ('x', 'core'), [(i, i ^ k) for i in range(NQ)])  10.9 us
    ppermute x6, waiting for transfers between devices, z_shift(): return lax.ppermute(x, 'z', [(i, (i + k) % NZ) for i in range(NZ)])  10.6 us
    ppermute x6, starting transfers between devices, z_shift(): return lax.ppermute(x, 'z', [(i, (i + k) % NZ) for i in range(NZ)])  9.55 us
    pallas_call x1, Pallas kernels, near_positions(): pl.pallas_call(near_kernel, out_shape=(jax.ShapeDtypeStruct((RH, C + R),...  8.49 us
    pallas_call x1, Pallas kernels, far_positions(): pl.pallas_call(far_kernel, out_shape=jax.ShapeDtypeStruct((NZ, OUT_ROWS,...  4.59 us
    pallas_call x1, Pallas kernels, visible_limits(): pl.pallas_call(limits_kernel, out_shape=jax.ShapeDtypeStruct((NQ, RT, 128...  2.92 us
  transfers between devices with their start and end apart: 16, of which 7 were waited for; matrix products, arithmetic and copies ran while one was open for 0% of the time, Pallas kernels for 14%

profile of v5, /device:TPU:1, one launch (start us, length us, event | category | flops | bytes accessed | tf_op | source)
XLA Modules:
  0.0 80.8 jit_solution(2682075540148780248)
XLA Ops:
  0.0 2.0 %prepare.1 = (bf16[176,128]{1,0:T(8,128)(2,1)}, bf16[176,128]{1,0:T(8,128)(2,1)}, bf16[176,128]{1,0:T(8,128)(2,1)}, bf16[176,128]{1,0:T(8,128)(2,1)}) custom-call(bf16[6,16,192]{2,1,0:T(8,128)(2,1)} %bitcast.48, bf16[16,4,512]{2,1,0:T(4,128)(2,1)} %keys.1, bf16[16,16,128]{2,1,0:T(8,128)(2,1)} %values.1), custom_call_target="tpu_custom_call" | custom-call | tf_op jit(solution)/shard_map/prepare/pallas_call | solution.py:195
  2.0 2.7 %collective-permute-start = (bf16[176,128]{1,0:T(8,128)(2,1)}, bf16[176,128]{1,0:T(8,128)(2,1)S(1)}, u32[]{:S(2)}, u32[]{:S(2)}) collective-permute-start(bf16[176,128]{1,0:T(8,128)(2,1)} %get-tuple-element.30), channel_id=1, source_target_pairs={{0,24},{8,16},{16,8},{24,0},{1,25},{9,17},{17,9},{25,1},{2,26},{10... | collective-permute-start | bytes 135176 | tf_op jit(solution)/shard_map/ppermute | solution.py:394
  4.7 2.0 %collective-permute-start.1 = (bf16[176,128]{1,0:T(8,128)(2,1)}, bf16[176,128]{1,0:T(8,128)(2,1)S(1)}, u32[]{:S(2)}, u32[]{:S(2)}) collective-permute-start(bf16[176,128]{1,0:T(8,128)(2,1)} %get-tuple-element.31), channel_id=1, source_target_pairs={{0,16},{8,24},{16,0},{24,8},{1,17},{9,25},{17,1},{25,9},{2,18},{10... | collective-permute-start | bytes 135176 | tf_op jit(solution)/shard_map/ppermute | solution.py:394
  6.7 2.8 %collective-permute-done.1 = bf16[176,128]{1,0:T(8,128)(2,1)S(1)} collective-permute-done((bf16[176,128]{1,0:T(8,128)(2,1)}, bf16[176,128]{1,0:T(8,128)(2,1)S(1)}, u32[]{:S(2)}, u32[]{:S(2)}) %collective-permute-start.1) | collective-permute-done | bytes 45088 | tf_op jit(solution)/shard_map/ppermute | solution.py:394
  9.4 0.8 %select_bitcast_fusion.3 = (bf16[1,176,128]{2,1,0:T(8,128)(2,1)S(1)}, bf16[1,176,128]{2,1,0:T(8,128)(2,1)S(1)}, bf16[1,176,128]{2,1,0:T(8,128)(2,1)S(1)}, bf16[1,176,128]{2,1,0:T(8,128)(2,1)S(1)}) fusion(pred[]{:T(512)S(6)} %ge.4, bf16[176,128]{1,0:T(8,128)(2,1)S(1)} %collective-permute-done, bf16[176,128]{1,0:T(8,128)(2,1)S(1)} %collective-permute-done.1, ...), kind=kLoop, calls=%fused_computation.9 | loop fusion | flops 180224 | bytes 360450 | tf_op jit(solution)/shard_map/stack | solution.py:429
  10.5 0.6 collective-permute-start.3
  11.1 1.6 %collective-permute-start.4 = (bf16[656,128]{1,0:T(8,128)(2,1)S(1)}, bf16[656,128]{1,0:T(8,128)(2,1)S(1)}, u32[]{:S(2)}, u32[]{:S(2)}) collective-permute-start(bf16[656,128]{1,0:T(8,128)(2,1)S(1)} %pad_maximum_fusion.refs_0_), channel_id=1, source_target_pairs={{0,32},{32,64},{64,96},{96,128},{128,160},{160,192},{192,224},{224... | collective-permute-start | bytes 503816 | tf_op jit(solution)/shard_map/ppermute | solution.py:398
  12.7 3.9 %collective-permute-start.5 = (bf16[656,128]{1,0:T(8,128)(2,1)S(1)}, bf16[656,128]{1,0:T(8,128)(2,1)S(1)}, u32[]{:S(2)}, u32[]{:S(2)}) collective-permute-start(bf16[656,128]{1,0:T(8,128)(2,1)S(1)} %pad_maximum_fusion.refs_0_), channel_id=1, source_target_pairs={{0,224},{32,0},{64,32},{96,64},{128,96},{160,128},{192,160},{224,1... | collective-permute-start | bytes 503816 | tf_op jit(solution)/shard_map/ppermute | solution.py:398
  16.7 4.4 %collective-permute-done.4.refs_1_ = bf16[656,128]{1,0:T(8,128)(2,1)S(1)} collective-permute-done((bf16[656,128]{1,0:T(8,128)(2,1)S(1)}, bf16[656,128]{1,0:T(8,128)(2,1)S(1)}, u32[]{:S(2)}, u32[]{:S(2)}) %collective-permute-start.4) | collective-permute-done | bytes 167968 | tf_op jit(solution)/shard_map/ppermute | solution.py:398
  21.0 1.7 %collective-permute-start.7 = (bf16[656,128]{1,0:T(8,128)(2,1)S(1)}, bf16[656,128]{1,0:T(8,128)(2,1)S(1)}, u32[]{:S(2)}, u32[]{:S(2)}) collective-permute-start(bf16[656,128]{1,0:T(8,128)(2,1)S(1)} %pad_maximum_fusion.refs_0_), channel_id=1, source_target_pairs={{0,192},{32,224},{64,0},{96,32},{128,64},{160,96},{192,128},{224,1... | collective-permute-start | bytes 503816 | tf_op jit(solution)/shard_map/ppermute | solution.py:398
  22.7 3.7 %collective-permute-done.6.refs_3_ = bf16[656,128]{1,0:T(8,128)(2,1)S(1)} collective-permute-done((bf16[656,128]{1,0:T(8,128)(2,1)S(1)}, bf16[656,128]{1,0:T(8,128)(2,1)S(1)}, u32[]{:S(2)}, u32[]{:S(2)}) %collective-permute-start.6) | collective-permute-done | bytes 167968 | tf_op jit(solution)/shard_map/ppermute | solution.py:398
  26.4 2.5 %collective-permute-done.7.refs_4_ = bf16[656,128]{1,0:T(8,128)(2,1)S(1)} collective-permute-done((bf16[656,128]{1,0:T(8,128)(2,1)S(1)}, bf16[656,128]{1,0:T(8,128)(2,1)S(1)}, u32[]{:S(2)}, u32[]{:S(2)}) %collective-permute-start.7) | collective-permute-done | bytes 167968 | tf_op jit(solution)/shard_map/ppermute | solution.py:398
  29.0 0.5 collective-permute-start.11
  29.5 1.2 %collective-permute-start.10 = (bf16[656,128]{1,0:T(8,128)(2,1)S(1)}, bf16[656,128]{1,0:T(8,128)(2,1)S(1)}, u32[]{:S(2)}, u32[]{:S(2)}) collective-permute-start(bf16[656,128]{1,0:T(8,128)(2,1)S(1)} %collective-permute-done.7.refs_4_), channel_id=1, source_target_pairs={{0,224},{32,0},{64,32},{96,64},{128,96},{160,128},{192,160},{224,1... | collective-permute-start | bytes 503816 | tf_op jit(solution)/shard_map/ppermute | solution.py:398
  30.7 1.1 %collective-permute-start.9 = (bf16[656,128]{1,0:T(8,128)(2,1)S(1)}, bf16[656,128]{1,0:T(8,128)(2,1)S(1)}, u32[]{:S(2)}, u32[]{:S(2)}) collective-permute-start(bf16[656,128]{1,0:T(8,128)(2,1)S(1)} %collective-permute-done.6.refs_3_), channel_id=1, source_target_pairs={{0,32},{32,64},{64,96},{96,128},{128,160},{160,192},{192,224},{224... | collective-permute-start | bytes 503816 | tf_op jit(solution)/shard_map/ppermute | solution.py:398
  31.8 7.0 %collective-permute-done.8.refs_7_ = bf16[576,1024]{1,0:T(8,128)(2,1)} collective-permute-done((bf16[576,1024]{1,0:T(8,128)(2,1)S(1)}, bf16[576,1024]{1,0:T(8,128)(2,1)}, u32[]{:S(2)}, u32[]{:S(2)}) %collective-permute-start.8) | collective-permute-done | bytes 1179680 | tf_op jit(solution)/shard_map/ppermute | solution.py:394
  38.8 0.7 copy-done.2
  39.4 3.5 %collective-permute-start.12 = (bf16[576,1024]{1,0:T(8,128)(2,1)}, bf16[576,1024]{1,0:T(8,128)(2,1)}, u32[]{:S(2)}, u32[]{:S(2)}) collective-permute-start(bf16[576,1024]{1,0:T(8,128)(2,1)} %collective-permute-done.8.refs_7_), channel_id=1, source_target_pairs={{0,8},{8,0},{16,24},{24,16},{1,9},{9,1},{17,25},{25,17},{2,10},{10... | collective-permute-start | bytes 3538952 | tf_op jit(solution)/shard_map/ppermute | solution.py:394
  42.9 2.9 %limits.1.refs_4_ = s32[4,192,128]{2,1,0:T(8,128)} custom-call(s32[3,16,64]{2,1,0:T(8,128)} %bitcast.49, s32[1,64]{1,0:T(1,128)} %bitcast.50), custom_call_target="tpu_custom_call" | custom-call | tf_op jit(solution)/shard_map/limits/pallas_call | solution.py:94
  45.8 0.1 settle.1
  45.9 0.9 %copy-done = s32[4,192,128]{2,1,0:T(8,128)S(1)} copy-done((s32[4,192,128]{2,1,0:T(8,128)S(1)}, s32[4,192,128]{2,1,0:T(8,128)}, u32[]{:S(2)}) %copy-start) | copy-done | bytes 393240
  46.8 0.0 copy-done.3
  46.8 8.5 %near_positions.1 = (bf16[768,576]{1,0:T(8,128)(2,1)S(1)}, f32[768,128]{1,0:T(8,128)S(1)}, f32[768,128]{1,0:T(8,128)S(1)}, f32[768,512]{1,0:T(8,128)S(1)}) custom-call(bf16[5,656,128]{2,1,0:T(8,128)(2,1)S(1)} %get-tuple-element.41.refs_0_, bf16[656,128]{1,0:T(8,128)(2,1)S(1)} %copy-done.3, bf16[656,128]{1,0:T(8,128)(2,1)S(1)} %collective-permute-done.10.refs_2_, ...), custom_call_target="tpu_custom_call" | custom-call | flops 5234491392 | bytes 8388608 | tf_op jit(solution)/shard_map/near_positions/pallas_call | solution.py:265
  55.4 4.6 %far_positions.1 = bf16[8,112,128]{2,1,0:T(8,128)(2,1)S(1)} custom-call(bf16[5,656,128]{2,1,0:T(8,128)(2,1)S(1)} %get-tuple-element.41.refs_0_, bf16[656,128]{1,0:T(8,128)(2,1)S(1)} %copy-done.3, bf16[656,128]{1,0:T(8,128)(2,1)S(1)} %collective-permute-done.10.refs_2_, bf16[656,128]{1,0:T(8,128)(2,1)S(1)} %collective-permute-done.11.refs_3_, ...), custom_call_target="tpu_custom_call" | custom-call | flops 1811939328 | bytes 8388608 | tf_op jit(solution)/shard_map/far_positions/pallas_call | solution.py:336
  59.9 16.0 %all_to_all.5.parts = bf16[8,112,128]{2,1,0:T(8,128)(2,1)S(1)} all-to-all(bf16[8,112,128]{2,1,0:T(8,128)(2,1)S(1)} %far_positions.1), channel_id=1, replica_groups=mesh['z'=8,'x'=2,'core'=2,'head'=8] {'z'}, dimensions={0} | all-to-all | bytes 458752 | tf_op jit(solution)/shard_map/all_to_all | solution.py:453
  76.0 0.3 combine.1
  76.3 1.4 %collective-permute-start.13 = (bf16[32,128]{1,0:T(8,128)(2,1)S(1)}, bf16[32,128]{1,0:T(8,128)(2,1)S(1)}, u32[]{:S(2)}, u32[]{:S(2)}) collective-permute-start(bf16[32,128]{1,0:T(8,128)(2,1)S(1)} %get-tuple-element.51), channel_id=1, source_target_pairs={{0,24},{8,16},{16,8},{24,0},{1,25},{9,17},{17,9},{25,1},{2,26},{10... | collective-permute-start | bytes 24584 | tf_op jit(solution)/shard_map/ppermute | solution.py:394
  77.7 0.5 collective-permute-start.14
  78.2 0.3 collective-permute-start.15
  78.4 1.0 %collective-permute-done.13 = bf16[32,128]{1,0:T(8,128)(2,1)S(1)} collective-permute-done((bf16[32,128]{1,0:T(8,128)(2,1)S(1)}, bf16[32,128]{1,0:T(8,128)(2,1)S(1)}, u32[]{:S(2)}, u32[]{:S(2)}) %collective-permute-start.13) | collective-permute-done | bytes 8224 | tf_op jit(solution)/shard_map/ppermute | solution.py:394
  79.5 0.7 collective-permute-done.14
  80.2 0.6 copy.18
  (32 shorter events, 0.2 us)
Async XLA Ops:
  0.0 10.5 %copy-start.1 = (bf16[1024,576]{0,1:T(8,128)(2,1)S(1)}, bf16[1024,576]{0,1:T(8,128)(2,1)}, u32[]{:S(2)}) copy-start(bf16[1024,576]{0,1:T(8,128)(2,1)} %param.7) | copy-start | bytes 3538948
  2.0 4.7 %collective-permute-start = (bf16[176,128]{1,0:T(8,128)(2,1)}, bf16[176,128]{1,0:T(8,128)(2,1)S(1)}, u32[]{:S(2)}, u32[]{:S(2)}) collective-permute-start(bf16[176,128]{1,0:T(8,128)(2,1)} %get-tuple-element.30), channel_id=1, source_target_pairs={{0,24},{8,16},{16,8},{24,0},{1,25},{9,17},{17,9},{25,1},{2,26},{10... | collective-permute-start | bytes 135176 | tf_op jit(solution)/shard_map/ppermute | solution.py:394
  4.7 4.7 %collective-permute-start.1 = (bf16[176,128]{1,0:T(8,128)(2,1)}, bf16[176,128]{1,0:T(8,128)(2,1)S(1)}, u32[]{:S(2)}, u32[]{:S(2)}) collective-permute-start(bf16[176,128]{1,0:T(8,128)(2,1)} %get-tuple-element.31), channel_id=1, source_target_pairs={{0,16},{8,24},{16,0},{24,8},{1,17},{9,25},{17,1},{25,9},{2,18},{10... | collective-permute-start | bytes 135176 | tf_op jit(solution)/shard_map/ppermute | solution.py:394
  6.7 2.8 %collective-permute-start.2 = (bf16[176,128]{1,0:T(8,128)(2,1)}, bf16[176,128]{1,0:T(8,128)(2,1)S(1)}, u32[]{:S(2)}, u32[]{:S(2)}) collective-permute-start(bf16[176,128]{1,0:T(8,128)(2,1)} %get-tuple-element.32), channel_id=1, source_target_pairs={{0,8},{8,0},{16,24},{24,16},{1,9},{9,1},{17,25},{25,17},{2,10},{10... | collective-permute-start | bytes 135176 | tf_op jit(solution)/shard_map/ppermute | solution.py:394
  10.5 18.5 %collective-permute-start.3 = (bf16[576,1024]{1,0:T(8,128)(2,1)S(1)}, bf16[576,1024]{1,0:T(8,128)(2,1)S(1)}, u32[]{:S(2)}, u32[]{:S(2)}) collective-permute-start(bf16[576,1024]{1,0:T(8,128)(2,1)S(1)} %bitcast.38), channel_id=1, source_target_pairs={{0,8},{8,0},{16,24},{24,16},{1,9},{9,1},{17,25},{25,17},{2,10},{10... | collective-permute-start | bytes 3538952 | tf_op jit(solution)/shard_map/ppermute | solution.py:394
  11.1 27.6 %collective-permute-start.8 = (bf16[576,1024]{1,0:T(8,128)(2,1)S(1)}, bf16[576,1024]{1,0:T(8,128)(2,1)}, u32[]{:S(2)}, u32[]{:S(2)}) collective-permute-start(bf16[576,1024]{1,0:T(8,128)(2,1)S(1)} %bitcast.39), channel_id=1, source_target_pairs={{0,16},{8,24},{16,0},{24,8},{1,17},{9,25},{17,1},{25,9},{2,18},{10... | collective-permute-start | bytes 3538952 | tf_op jit(solution)/shard_map/ppermute | solution.py:394
  11.1 9.9 %collective-permute-start.4 = (bf16[656,128]{1,0:T(8,128)(2,1)S(1)}, bf16[656,128]{1,0:T(8,128)(2,1)S(1)}, u32[]{:S(2)}, u32[]{:S(2)}) collective-permute-start(bf16[656,128]{1,0:T(8,128)(2,1)S(1)} %pad_maximum_fusion.refs_0_), channel_id=1, source_target_pairs={{0,32},{32,64},{64,96},{96,128},{128,160},{160,192},{192,224},{224... | collective-permute-start | bytes 503816 | tf_op jit(solution)/shard_map/ppermute | solution.py:398
  12.7 10.0 %collective-permute-start.5 = (bf16[656,128]{1,0:T(8,128)(2,1)S(1)}, bf16[656,128]{1,0:T(8,128)(2,1)S(1)}, u32[]{:S(2)}, u32[]{:S(2)}) collective-permute-start(bf16[656,128]{1,0:T(8,128)(2,1)S(1)} %pad_maximum_fusion.refs_0_), channel_id=1, source_target_pairs={{0,224},{32,0},{64,32},{96,64},{128,96},{160,128},{192,160},{224,1... | collective-permute-start | bytes 503816 | tf_op jit(solution)/shard_map/ppermute | solution.py:398
  16.7 9.8 %collective-permute-start.6 = (bf16[656,128]{1,0:T(8,128)(2,1)S(1)}, bf16[656,128]{1,0:T(8,128)(2,1)S(1)}, u32[]{:S(2)}, u32[]{:S(2)}) collective-permute-start(bf16[656,128]{1,0:T(8,128)(2,1)S(1)} %pad_maximum_fusion.refs_0_), channel_id=1, source_target_pairs={{0,64},{32,96},{64,128},{96,160},{128,192},{160,224},{192,0},{224,... | collective-permute-start | bytes 503816 | tf_op jit(solution)/shard_map/ppermute | solution.py:398
  21.0 7.9 %collective-permute-start.7 = (bf16[656,128]{1,0:T(8,128)(2,1)S(1)}, bf16[656,128]{1,0:T(8,128)(2,1)S(1)}, u32[]{:S(2)}, u32[]{:S(2)}) collective-permute-start(bf16[656,128]{1,0:T(8,128)(2,1)S(1)} %pad_maximum_fusion.refs_0_), channel_id=1, source_target_pairs={{0,192},{32,224},{64,0},{96,32},{128,64},{160,96},{192,128},{224,1... | collective-permute-start | bytes 503816 | tf_op jit(solution)/shard_map/ppermute | solution.py:398
  29.0 9.8 %collective-permute-start.11 = (bf16[656,128]{1,0:T(8,128)(2,1)S(1)}, bf16[656,128]{1,0:T(8,128)(2,1)S(1)}, u32[]{:S(2)}, u32[]{:S(2)}) collective-permute-start(bf16[656,128]{1,0:T(8,128)(2,1)S(1)} %broadcast_select_fusion), channel_id=1, source_target_pairs={{0,64},{8,200},{32,96},{40,232},{64,128},{72,8},{96,160},{104,40},... | collective-permute-start | bytes 503816 | tf_op jit(solution)/shard_map/ppermute | solution.py:406
  29.5 9.3 %collective-permute-start.10 = (bf16[656,128]{1,0:T(8,128)(2,1)S(1)}, bf16[656,128]{1,0:T(8,128)(2,1)S(1)}, u32[]{:S(2)}, u32[]{:S(2)}) collective-permute-start(bf16[656,128]{1,0:T(8,128)(2,1)S(1)} %collective-permute-done.7.refs_4_), channel_id=1, source_target_pairs={{0,224},{32,0},{64,32},{96,64},{128,96},{160,128},{192,160},{224,1... | collective-permute-start | bytes 503816 | tf_op jit(solution)/shard_map/ppermute | solution.py:398
  30.7 8.1 %collective-permute-start.9 = (bf16[656,128]{1,0:T(8,128)(2,1)S(1)}, bf16[656,128]{1,0:T(8,128)(2,1)S(1)}, u32[]{:S(2)}, u32[]{:S(2)}) collective-permute-start(bf16[656,128]{1,0:T(8,128)(2,1)S(1)} %collective-permute-done.6.refs_3_), channel_id=1, source_target_pairs={{0,32},{32,64},{64,96},{96,128},{128,160},{160,192},{192,224},{224... | collective-permute-start | bytes 503816 | tf_op jit(solution)/shard_map/ppermute | solution.py:398
  38.8 0.7 copy-start.2
  39.4 15.9 %collective-permute-start.12 = (bf16[576,1024]{1,0:T(8,128)(2,1)}, bf16[576,1024]{1,0:T(8,128)(2,1)}, u32[]{:S(2)}, u32[]{:S(2)}) collective-permute-start(bf16[576,1024]{1,0:T(8,128)(2,1)} %collective-permute-done.8.refs_7_), channel_id=1, source_target_pairs={{0,8},{8,0},{16,24},{24,16},{1,9},{9,1},{17,25},{25,17},{2,10},{10... | collective-permute-start | bytes 3538952 | tf_op jit(solution)/shard_map/ppermute | solution.py:394
  45.8 1.0 %copy-start = (s32[4,192,128]{2,1,0:T(8,128)S(1)}, s32[4,192,128]{2,1,0:T(8,128)}, u32[]{:S(2)}) copy-start(s32[4,192,128]{2,1,0:T(8,128)} %limits.1.refs_4_) | copy-start | bytes 1179652
  45.8 1.0 %copy-start.3 = (bf16[656,128]{1,0:T(8,128)(2,1)S(1)}, bf16[656,128]{1,0:T(8,128)(2,1)}, u32[]{:S(2)}) copy-start(bf16[656,128]{1,0:T(8,128)(2,1)} %copy-done.2) | copy-start | bytes 503812
  76.3 3.2 %collective-permute-start.13 = (bf16[32,128]{1,0:T(8,128)(2,1)S(1)}, bf16[32,128]{1,0:T(8,128)(2,1)S(1)}, u32[]{:S(2)}, u32[]{:S(2)}) collective-permute-start(bf16[32,128]{1,0:T(8,128)(2,1)S(1)} %get-tuple-element.51), channel_id=1, source_target_pairs={{0,24},{8,16},{16,8},{24,0},{1,25},{9,17},{17,9},{25,1},{2,26},{10... | collective-permute-start | bytes 24584 | tf_op jit(solution)/shard_map/ppermute | solution.py:394
  77.7 2.5 %collective-permute-start.14 = (bf16[32,128]{1,0:T(8,128)(2,1)S(1)}, bf16[32,128]{1,0:T(8,128)(2,1)S(1)}, u32[]{:S(2)}, u32[]{:S(2)}) collective-permute-start(bf16[32,128]{1,0:T(8,128)(2,1)S(1)} %get-tuple-element.52), channel_id=1, source_target_pairs={{0,16},{8,24},{16,0},{24,8},{1,17},{9,25},{17,1},{25,9},{2,18},{10... | collective-permute-start | bytes 24584 | tf_op jit(solution)/shard_map/ppermute | solution.py:394
  78.2 2.0 %collective-permute-start.15 = (bf16[32,128]{1,0:T(8,128)(2,1)S(1)}, bf16[32,128]{1,0:T(8,128)(2,1)S(1)}, u32[]{:S(2)}, u32[]{:S(2)}) collective-permute-start(bf16[32,128]{1,0:T(8,128)(2,1)S(1)} %get-tuple-element.53), channel_id=1, source_target_pairs={{0,8},{8,0},{16,24},{24,16},{1,9},{9,1},{17,25},{25,17},{2,10},{10... | collective-permute-start | bytes 24584 | tf_op jit(solution)/shard_map/ppermute | solution.py:394
